TPU v7x, 256 devices: a whole 4x4x8 slice. The times are simulated.
256 devices in a mesh: video: 8 (over y, core), audio: 16 (over z, x_hi), tp: 2 (over x_lo).
Axes of the slice: x: 4 (x_hi: 2, x_lo: 2; x = x_hi * 2 + x_lo), y: 4, z: 8, core: 2. Of those that a mesh axis runs over, the one named last changes fastest.
Arguments:
- query_video: bfloat16 [32768, 3072], P(('video', 'audio'), 'tp'), may hold values from -400 to 400
- key_video: bfloat16 [32768, 3072], P(('video', 'audio'), 'tp'), may hold values from -6 to 6
- value_video: bfloat16 [32768, 3072], P(('video', 'audio'), 'tp'), may hold values from -6 to 6
- query_audio: bfloat16 [4096, 3072], P(('video', 'audio'), 'tp'), may hold values from -400 to 400
- key_audio: bfloat16 [4096, 3072], P(('video', 'audio'), 'tp'), may hold values from -6 to 6
- value_audio: bfloat16 [4096, 3072], P(('video', 'audio'), 'tp'), may hold values from -6 to 6
- conv_video: float32 [3, 3072], P(None, 'tp'), may hold values from -3 to 3
- conv_audio: float32 [3, 3072], P(None, 'tp'), may hold values from -3 to 3
- gain_video: float32 [3072], P('tp'), may hold values from 0.1 to 1.9
- gain_audio: float32 [3072], P('tp'), may hold values from 0.1 to 1.9
- video_window: int32 [128, 2], replicated, may hold values from 0 to 4096, as said below
- audio_window: int32 [128, 2], replicated, may hold values from 0 to 32768, as said below
- video_valid: int32 [128], replicated, may hold values from 65 to 256
- audio_valid: int32 [128], replicated, may hold values from 9 to 32
- cotangent_video: bfloat16 [32768, 3072], P(('video', 'audio'), 'tp'), may hold values from -6 to 6
- cotangent_audio: bfloat16 [4096, 3072], P(('video', 'audio'), 'tp'), may hold values from -6 to 6
Outputs:
- output_video: bfloat16 [32768, 3072], P(('video', 'audio'), 'tp')
- output_audio: bfloat16 [4096, 3072], P(('video', 'audio'), 'tp')
- query_grad_video: bfloat16 [32768, 3072], P(('video', 'audio'), 'tp')
- key_grad_video: bfloat16 [32768, 3072], P(('video', 'audio'), 'tp')
- value_grad_video: bfloat16 [32768, 3072], P(('video', 'audio'), 'tp')
- query_grad_audio: bfloat16 [4096, 3072], P(('video', 'audio'), 'tp')
- key_grad_audio: bfloat16 [4096, 3072], P(('video', 'audio'), 'tp')
- value_grad_audio: bfloat16 [4096, 3072], P(('video', 'audio'), 'tp')
- taps_grad_video: float32 [3, 3072], P(None, 'tp')
- taps_grad_audio: float32 [3, 3072], P(None, 'tp')
- gain_grad_video: float32 [3072], P('tp')
- gain_grad_audio: float32 [3072], P('tp')
Inputs may be any that keep to these rules, and one draw needn't show every extreme that they name: video_window[b] = [lower, upper) contains all audio tokens of block b; lower lies in block b - 1 (0 for b = 0) and upper - 1 in block b + 1 (upper = 4096 for the last block). audio_window[c] = [lower, upper) contains all video tokens of block c; lower lies in block c - 1 (0 for c = 0) and upper - 1 in block c + 1 (upper = 32768 for the last block).
All inputs are finite; a program needn't handle non-finite values.
Results may differ from a plain program's by a relative error of at most 0.022.
Values may be sent and summed in bfloat16 or wider, within the bound.
No kernel may reach another device: no remote copies, remote signals or barrier semaphores. Data moves between devices by JAX's collectives and lax.ppermute only.
A program may use at most 128 MiB of HBM per device.

v0:
```python
import jax
import jax.numpy as jnp
from jax import lax
from jax.sharding import PartitionSpec as P

HEAD_DIM = 128
D = 3072
STRIDE = 32


NEGATIVE = -1e30
EPSILON = 1e-06


def from_behind(block, axis, distance):
    devices = range(lax.axis_size(axis))
    route = [(i - distance, i) for i in devices if i - distance in devices]
    return lax.ppermute(block, axis, route)


def with_halo(block, sides, width):
    for axis, dim in sides:
        count = lax.axis_size(axis)
        forward = [(i, i + 1) for i in range(count - 1)]
        backward = [(target, source) for source, target in forward]
        low = lax.ppermute(
            lax.slice_in_dim(block, block.shape[dim] - width, None, axis=dim), axis, forward
        )
        high = lax.ppermute(lax.slice_in_dim(block, 0, width, axis=dim), axis, backward)
        block = jnp.concatenate([low, block, high], axis=dim)
    return block


def split_heads(rows):
    return rows.reshape(rows.shape[0], -1, HEAD_DIM)


def join_heads(heads):
    return heads.reshape(heads.shape[0], -1)


def key_visible(window, valid, block, key_rows):
    zero_index = jnp.zeros((), jnp.int32)
    bounds = lax.dynamic_slice(window, (block, zero_index), (1, 2))
    valid_pad = jnp.concatenate([jnp.zeros((1,), jnp.int32), valid, jnp.zeros((1,), jnp.int32)])
    valid_three = jnp.repeat(lax.dynamic_slice(valid_pad, (block,), (3,)), key_rows)
    offsets = jnp.arange(3 * key_rows, dtype=jnp.int32)
    position = (block - 1) * key_rows + offsets
    return (
        (position >= bounds[0, 0]) & (position < bounds[0, 1]) & (offsets % key_rows < valid_three)
    )


def neighbour_keys(keys, values):
    preceding = from_behind((keys, values), ("video", "audio"), 1)
    following = from_behind((keys, values), ("video", "audio"), -1)
    near_keys = jnp.concatenate([preceding[0], keys, following[0]], 0)
    near_values = jnp.concatenate([preceding[1], values, following[1]], 0)
    return (near_keys, near_values)


def attend(queries, near_keys, near_values, visible):
    factor = HEAD_DIM ** (-0.5)
    scores = (
        jnp.einsum(
            "qhd,khd->hqk",
            split_heads(queries),
            split_heads(near_keys),
            preferred_element_type=jnp.float32,
        )
        * factor
    )
    scores = jnp.where(visible[None, None, :], scores, NEGATIVE)
    peak = jnp.max(scores, axis=-1, keepdims=True)
    log_total = peak[..., 0] + jnp.log(jnp.sum(jnp.exp(scores - peak), axis=-1))
    probability = jnp.exp(scores - log_total[..., None])
    prob_round = probability.astype(jnp.bfloat16)
    attended = jnp.einsum(
        "hqk,khd->qhd", prob_round, split_heads(near_values), preferred_element_type=jnp.float32
    )
    return (join_heads(attended).astype(jnp.bfloat16), log_total, probability, prob_round)


def temporal_mix(attended, taps, stride):
    extended = with_halo(attended, ((("video", "audio"), 0),), stride).astype(jnp.float32)
    rows = attended.shape[0]
    earlier = extended[:rows]
    signal = extended[stride : stride + rows]
    later = extended[2 * stride :]
    mixed = taps[0] * earlier + taps[1] * signal + taps[2] * later
    return (mixed, earlier, signal, later)


def mix_backward(mixed_grad, taps, stride, earlier, signal, later):
    extended = with_halo(mixed_grad, ((("video", "audio"), 0),), stride)
    rows = mixed_grad.shape[0]
    upstream = (
        taps[0] * extended[2 * stride :] + taps[1] * mixed_grad + taps[2] * extended[:rows]
    ).astype(jnp.bfloat16)
    taps_part = jnp.stack(
        [
            jnp.sum(mixed_grad * earlier, 0),
            jnp.sum(mixed_grad * signal, 0),
            jnp.sum(mixed_grad * later, 0),
        ]
    )
    return (upstream, taps_part)


def query_side(attended, upstream, near_keys, near_values, probability):
    factor = HEAD_DIM ** (-0.5)
    grad_heads = split_heads(upstream)
    prob_grad = jnp.einsum(
        "qhd,khd->hqk", grad_heads, split_heads(near_values), preferred_element_type=jnp.float32
    )
    row_dots = jnp.einsum(
        "qhd,qhd->hq", grad_heads, split_heads(attended), preferred_element_type=jnp.float32
    )
    score_grad = (probability * (prob_grad - row_dots[..., None])).astype(jnp.bfloat16)
    query_grad = (
        jnp.einsum(
            "hqk,khd->qhd", score_grad, split_heads(near_keys), preferred_element_type=jnp.float32
        )
        * factor
    )
    return (join_heads(query_grad).astype(jnp.bfloat16), row_dots, score_grad)


def returned_parts(score_grad, prob_round, queries, upstream):
    factor = HEAD_DIM ** (-0.5)
    key_part = join_heads(
        jnp.einsum(
            "hqk,qhd->khd", score_grad, split_heads(queries), preferred_element_type=jnp.float32
        )
        * factor
    )
    value_part = join_heads(
        jnp.einsum(
            "hqk,qhd->khd", prob_round, split_heads(upstream), preferred_element_type=jnp.float32
        )
    )
    return (key_part, value_part)


def settle_parts(key_part, value_part, from_following, from_preceding, key_rows):
    key_grad = key_part[key_rows : 2 * key_rows] + from_following[0] + from_preceding[0]
    value_grad = value_part[key_rows : 2 * key_rows] + from_following[1] + from_preceding[1]
    return (key_grad.astype(jnp.bfloat16), value_grad.astype(jnp.bfloat16))


def norm_backward(cotangent, gains, mixed, inverse, inner):
    incoming = cotangent.astype(jnp.float32)
    scaled = incoming * gains
    gain_part = jnp.sum(incoming * mixed * inverse, axis=0)
    mixed_grad = inverse * scaled - mixed * inverse * inverse * inverse * inner[:, None] / D
    return (mixed_grad, gain_part)


def per_device(
    query_video,
    key_video,
    value_video,
    query_audio,
    key_audio,
    value_audio,
    conv_video,
    conv_audio,
    gain_video,
    gain_audio,
    video_window,
    audio_window,
    video_valid,
    audio_valid,
    cotangent_video,
    cotangent_audio,
):
    block = lax.axis_index(("video", "audio"))
    video_rows = query_video.shape[0]
    audio_rows = query_audio.shape[0]
    near_key_audio, near_value_audio = neighbour_keys(key_audio, value_audio)
    near_key_video, near_value_video = neighbour_keys(key_video, value_video)
    seen_video = key_visible(video_window, audio_valid, block, audio_rows)
    seen_audio = key_visible(audio_window, video_valid, block, video_rows)
    attended_video, total_video, prob_video, round_video = attend(
        query_video, near_key_audio, near_value_audio, seen_video
    )
    attended_audio, total_audio, prob_audio, round_audio = attend(
        query_audio, near_key_video, near_value_video, seen_audio
    )
    mixed_video, early_video, signal_video, late_video = temporal_mix(
        attended_video, conv_video, STRIDE
    )
    mixed_audio, early_audio, signal_audio, late_audio = temporal_mix(attended_audio, conv_audio, 1)
    square_video, square_audio = lax.psum(
        (jnp.sum(mixed_video * mixed_video, -1), jnp.sum(mixed_audio * mixed_audio, -1)), "tp"
    )
    inverse_video = lax.rsqrt(square_video / D + EPSILON)[:, None]
    inverse_audio = lax.rsqrt(square_audio / D + EPSILON)[:, None]
    output_video = (mixed_video * inverse_video * gain_video).astype(jnp.bfloat16)
    output_audio = (mixed_audio * inverse_audio * gain_audio).astype(jnp.bfloat16)
    scaled_video = cotangent_video.astype(jnp.float32) * gain_video
    scaled_audio = cotangent_audio.astype(jnp.float32) * gain_audio
    inner_video, inner_audio = lax.psum(
        (jnp.sum(scaled_video * mixed_video, -1), jnp.sum(scaled_audio * mixed_audio, -1)), "tp"
    )
    mixed_grad_video, gain_part_video = norm_backward(
        cotangent_video, gain_video, mixed_video, inverse_video, inner_video
    )
    mixed_grad_audio, gain_part_audio = norm_backward(
        cotangent_audio, gain_audio, mixed_audio, inverse_audio, inner_audio
    )
    upstream_video, taps_part_video = mix_backward(
        mixed_grad_video, conv_video, STRIDE, early_video, signal_video, late_video
    )
    upstream_audio, taps_part_audio = mix_backward(
        mixed_grad_audio, conv_audio, 1, early_audio, signal_audio, late_audio
    )
    taps_grad_video, taps_grad_audio, gain_grad_video, gain_grad_audio = lax.psum(
        (taps_part_video, taps_part_audio, gain_part_video, gain_part_audio), ("video", "audio")
    )
    query_grad_video, dots_video, score_video = query_side(
        attended_video, upstream_video, near_key_audio, near_value_audio, prob_video
    )
    query_grad_audio, dots_audio, score_audio = query_side(
        attended_audio, upstream_audio, near_key_video, near_value_video, prob_audio
    )
    key_part, value_part = returned_parts(score_video, round_video, query_video, upstream_video)
    from_following = (
        from_behind(key_part[:audio_rows].astype(jnp.bfloat16), ("video", "audio"), -1).astype(
            jnp.float32
        ),
        from_behind(value_part[:audio_rows].astype(jnp.bfloat16), ("video", "audio"), -1).astype(
            jnp.float32
        ),
    )
    from_preceding = (
        from_behind(key_part[2 * audio_rows :].astype(jnp.bfloat16), ("video", "audio"), 1).astype(
            jnp.float32
        ),
        from_behind(
            value_part[2 * audio_rows :].astype(jnp.bfloat16), ("video", "audio"), 1
        ).astype(jnp.float32),
    )
    key_grad_audio, value_grad_audio = settle_parts(
        key_part, value_part, from_following, from_preceding, audio_rows
    )
    video_key_part, video_value_part = returned_parts(
        score_audio, round_audio, query_audio, upstream_audio
    )
    video_from_following = (
        from_behind(
            video_key_part[:video_rows].astype(jnp.bfloat16), ("video", "audio"), -1
        ).astype(jnp.float32),
        from_behind(
            video_value_part[:video_rows].astype(jnp.bfloat16), ("video", "audio"), -1
        ).astype(jnp.float32),
    )
    video_from_preceding = (
        from_behind(
            video_key_part[2 * video_rows :].astype(jnp.bfloat16), ("video", "audio"), 1
        ).astype(jnp.float32),
        from_behind(
            video_value_part[2 * video_rows :].astype(jnp.bfloat16), ("video", "audio"), 1
        ).astype(jnp.float32),
    )
    key_grad_video, value_grad_video = settle_parts(
        video_key_part, video_value_part, video_from_following, video_from_preceding, video_rows
    )
    return (
        output_video,
        output_audio,
        query_grad_video,
        key_grad_video,
        value_grad_video,
        query_grad_audio,
        key_grad_audio,
        value_grad_audio,
        taps_grad_video,
        taps_grad_audio,
        gain_grad_video,
        gain_grad_audio,
    )


def solution(mesh):
    in_specs = (
        P(("video", "audio"), "tp"),
        P(("video", "audio"), "tp"),
        P(("video", "audio"), "tp"),
        P(("video", "audio"), "tp"),
        P(("video", "audio"), "tp"),
        P(("video", "audio"), "tp"),
        P(None, "tp"),
        P(None, "tp"),
        P("tp"),
        P("tp"),
        P(),
        P(),
        P(),
        P(),
        P(("video", "audio"), "tp"),
        P(("video", "audio"), "tp"),
    )
    out_specs = (
        P(("video", "audio"), "tp"),
        P(("video", "audio"), "tp"),
        P(("video", "audio"), "tp"),
        P(("video", "audio"), "tp"),
        P(("video", "audio"), "tp"),
        P(("video", "audio"), "tp"),
        P(("video", "audio"), "tp"),
        P(("video", "audio"), "tp"),
        P(None, "tp"),
        P(None, "tp"),
        P("tp"),
        P("tp"),
    )
    return jax.shard_map(
        per_device, mesh=mesh, in_specs=in_specs, out_specs=out_specs, check_vma=False
    )
```

profile of v0, /device:TPU:2, one launch (start us, length us, event | category | flops | bytes accessed | tf_op | source)
XLA Modules:
  0.0 911.8 jit_solution(2965483205751169421)
XLA Ops:
  0.7 4.8 collective-permute-start.2
  6.8 6.1 collective-permute-start
  23.8 6.7 collective-permute-start.8
  35.8 7.6 collective-permute-start.4
  43.5 45.8 %collective-permute-done.5 = bf16[32,1536]{0,1:T(8,128)(2,1)S(1)} collective-permute-done((bf16[32,1536]{0,1:T(8,128)(2,1)S(1)}, bf16[32,1536]{0,1:T(8,128)(2,1)S(1)}, u32[]{:S(2)}, u32[]{:S(2)}) %collective-permute-start.5) | collective-permute-done | bytes 98336 | tf_op jit(solution)/shard_map/ppermute | solution.py:29
  92.7 3.1 multiply_reduce_fusion.3
  99.1 8.0 collective-permute-done.6
  109.8 8.6 collective-permute-start.10
  119.8 7.0 collective-permute-done.11
  128.2 5.6 all-reduce.2
  137.4 2.7 fusion.5
  140.0 5.6 all-reduce.1
  147.4 4.1 multiply_reduce_fusion.2
  153.1 6.9 collective-permute-start.15
  167.9 7.0 collective-permute-start.13
  176.3 650.2 %all-reduce = (f32[3,1536]{1,0:T(4,128)}, f32[3,1536]{1,0:T(4,128)}, f32[1536]{0:T(1024)}, f32[1536]{0:T(1024)}) all-reduce(f32[3,1536]{1,0:T(4,128)S(1)} %pad_maximum_fusion.6, f32[3,1536]{1,0:T(4,128)S(1)} %pad_maximum_fusion.7, f32[1536]{0:T(1024)S(1)} %copy-done.31, ...), channel_id=1, replica_groups=mesh['video'=8,'audio'=16,'tp'=2] {'video','audio'}, use_global_device_ids=true, to_apply=%region_15.16 | all-reduce | flops 12288 | bytes 98304 | tf_op jit(solution)/shard_map/psum | solution.py:218
  830.1 3.7 fusion.79
  834.4 3.0 fusion.80
  850.5 7.0 collective-permute-start.17
  868.4 2.8 collective-permute-start.21
  877.2 8.2 collective-permute-done.21
  885.4 5.9 collective-permute-start.23
  894.8 4.5 collective-permute-done.22
  902.7 6.8 collective-permute-done.16
  (205 shorter events, 88.5 us)
Async XLA Ops:
  0.7 23.1 %collective-permute-start.2 = (bf16[32,1536]{1,0:T(8,128)(2,1)}, bf16[32,1536]{1,0:T(8,128)(2,1)}, u32[]{:S(2)}, u32[]{:S(2)}) collective-permute-start(bf16[32,1536]{1,0:T(8,128)(2,1)} %param.20), channel_id=1, source_target_pairs={{0,2},{2,4},{4,6},{6,8},{8,10},{10,12},{12,14},{14,16},{16,18},{18... | collective-permute-start | bytes 294920 | tf_op jit(solution)/shard_map/ppermute | solution.py:18
  5.5 25.1 %collective-permute-start.3 = (bf16[32,1536]{1,0:T(8,128)(2,1)}, bf16[32,1536]{1,0:T(8,128)(2,1)}, u32[]{:S(2)}, u32[]{:S(2)}) collective-permute-start(bf16[32,1536]{1,0:T(8,128)(2,1)} %param.20), channel_id=1, source_target_pairs={{2,0},{4,2},{6,4},{8,6},{10,8},{12,10},{14,12},{16,14},{18,16},{20... | collective-permute-start | bytes 294920 | tf_op jit(solution)/shard_map/ppermute | solution.py:18
  6.8 26.7 %collective-permute-start = (bf16[32,1536]{1,0:T(8,128)(2,1)}, bf16[32,1536]{1,0:T(8,128)(2,1)S(1)}, u32[]{:S(2)}, u32[]{:S(2)}) collective-permute-start(bf16[32,1536]{1,0:T(8,128)(2,1)} %param.21), channel_id=1, source_target_pairs={{0,2},{2,4},{4,6},{6,8},{8,10},{10,12},{12,14},{14,16},{16,18},{18... | collective-permute-start | bytes 294920 | tf_op jit(solution)/shard_map/ppermute | solution.py:18
  12.9 20.6 %collective-permute-start.1 = (bf16[32,1536]{1,0:T(8,128)(2,1)}, bf16[32,1536]{1,0:T(8,128)(2,1)S(1)}, u32[]{:S(2)}, u32[]{:S(2)}) collective-permute-start(bf16[32,1536]{1,0:T(8,128)(2,1)} %param.21), channel_id=1, source_target_pairs={{2,0},{4,2},{6,4},{8,6},{10,8},{12,10},{14,12},{16,14},{18,16},{20... | collective-permute-start | bytes 294920 | tf_op jit(solution)/shard_map/ppermute | solution.py:18
  16.5 79.3 %collective-permute-start.9 = (bf16[256,1536]{0,1:T(8,128)(2,1)}, bf16[256,1536]{0,1:T(8,128)(2,1)}, u32[]{:S(2)}, u32[]{:S(2)}) collective-permute-start(bf16[256,1536]{0,1:T(8,128)(2,1)} %copy.93), channel_id=1, source_target_pairs={{2,0},{4,2},{6,4},{8,6},{10,8},{12,10},{14,12},{16,14},{18,16},{20... | collective-permute-start | bytes 2359304 | tf_op jit(solution)/shard_map/ppermute | solution.py:18
  23.8 71.9 %collective-permute-start.8 = (bf16[256,1536]{0,1:T(8,128)(2,1)}, bf16[256,1536]{0,1:T(8,128)(2,1)S(1)}, u32[]{:S(2)}, u32[]{:S(2)}) collective-permute-start(bf16[256,1536]{0,1:T(8,128)(2,1)} %copy.93), channel_id=1, source_target_pairs={{0,2},{2,4},{4,6},{6,8},{8,10},{10,12},{12,14},{14,16},{16,18},{18... | collective-permute-start | bytes 2359304 | tf_op jit(solution)/shard_map/ppermute | solution.py:18
  30.6 68.5 %collective-permute-start.7 = (bf16[256,1536]{0,1:T(8,128)(2,1)}, bf16[256,1536]{0,1:T(8,128)(2,1)S(1)}, u32[]{:S(2)}, u32[]{:S(2)}) collective-permute-start(bf16[256,1536]{0,1:T(8,128)(2,1)} %copy.90), channel_id=1, source_target_pairs={{2,0},{4,2},{6,4},{8,6},{10,8},{12,10},{14,12},{16,14},{18,16},{20... | collective-permute-start | bytes 2359304 | tf_op jit(solution)/shard_map/ppermute | solution.py:18
  34.5 54.7 %collective-permute-start.5 = (bf16[32,1536]{0,1:T(8,128)(2,1)S(1)}, bf16[32,1536]{0,1:T(8,128)(2,1)S(1)}, u32[]{:S(2)}, u32[]{:S(2)}) collective-permute-start(bf16[32,1536]{0,1:T(8,128)(2,1)S(1)} %bitcast.183), channel_id=1, source_target_pairs={{2,0},{4,2},{6,4},{8,6},{10,8},{12,10},{14,12},{16,14},{18,16},{20... | collective-permute-start | bytes 294920 | tf_op jit(solution)/shard_map/ppermute | solution.py:29
  35.8 56.2 %collective-permute-start.4 = (bf16[32,1536]{0,1:T(8,128)(2,1)S(1)}, bf16[32,1536]{0,1:T(8,128)(2,1)S(1)}, u32[]{:S(2)}, u32[]{:S(2)}) collective-permute-start(bf16[32,1536]{0,1:T(8,128)(2,1)S(1)} %bitcast.182), channel_id=1, source_target_pairs={{0,2},{2,4},{4,6},{6,8},{8,10},{10,12},{12,14},{14,16},{16,18},{18... | collective-permute-start | bytes 294920 | tf_op jit(solution)/shard_map/ppermute | solution.py:26
  89.2 17.9 %collective-permute-start.6 = (bf16[256,1536]{0,1:T(8,128)(2,1)}, bf16[256,1536]{0,1:T(8,128)(2,1)S(1)}, u32[]{:S(2)}, u32[]{:S(2)}) collective-permute-start(bf16[256,1536]{0,1:T(8,128)(2,1)} %copy.90), channel_id=1, source_target_pairs={{0,2},{2,4},{4,6},{6,8},{8,10},{10,12},{12,14},{14,16},{16,18},{18... | collective-permute-start | bytes 2359304 | tf_op jit(solution)/shard_map/ppermute | solution.py:18
  109.8 10.0 %collective-permute-start.10 = (bf16[1,1536]{1,0:T(2,128)(2,1)S(1)}, bf16[1,1536]{1,0:T(2,128)(2,1)S(1)}, u32[]{:S(2)}, u32[]{:S(2)}) collective-permute-start(bf16[1,1536]{1,0:T(2,128)(2,1)S(1)} %get-tuple-element.94), channel_id=1, source_target_pairs={{0,2},{2,4},{4,6},{6,8},{8,10},{10,12},{12,14},{14,16},{16,18},{18... | collective-permute-start | bytes 9224 | tf_op jit(solution)/shard_map/ppermute | solution.py:26
  118.5 8.3 collective-permute-start.11
  151.7 674.8 %collective-permute-start.14 = (f32[1,1536]{1,0:T(1,128)S(1)}, f32[1,1536]{1,0:T(1,128)S(1)}, u32[]{:S(2)}, u32[]{:S(2)}) collective-permute-start(f32[1,1536]{1,0:T(1,128)S(1)} %get-tuple-element.92), channel_id=1, source_target_pairs={{2,0},{4,2},{6,4},{8,6},{10,8},{12,10},{14,12},{16,14},{18,16},{20... | collective-permute-start | bytes 18440 | tf_op jit(solution)/shard_map/ppermute | solution.py:29
  153.1 673.4 %collective-permute-start.15 = (f32[1,1536]{1,0:T(1,128)S(1)}, f32[1,1536]{1,0:T(1,128)S(1)}, u32[]{:S(2)}, u32[]{:S(2)}) collective-permute-start(f32[1,1536]{1,0:T(1,128)S(1)} %get-tuple-element.93), channel_id=1, source_target_pairs={{0,2},{2,4},{4,6},{6,8},{8,10},{10,12},{12,14},{14,16},{16,18},{18... | collective-permute-start | bytes 18440 | tf_op jit(solution)/shard_map/ppermute | solution.py:26
  167.9 693.9 %collective-permute-start.13 = (f32[32,1536]{1,0:T(8,128)}, f32[32,1536]{1,0:T(8,128)}, u32[]{:S(2)}, u32[]{:S(2)}) collective-permute-start(f32[32,1536]{1,0:T(8,128)} %copy.103), channel_id=1, source_target_pairs={{0,2},{2,4},{4,6},{6,8},{8,10},{10,12},{12,14},{14,16},{16,18},{18... | collective-permute-start | bytes 589832 | tf_op jit(solution)/shard_map/ppermute | solution.py:26
  174.9 685.7 %collective-permute-start.12 = (f32[32,1536]{1,0:T(8,128)}, f32[32,1536]{1,0:T(8,128)}, u32[]{:S(2)}, u32[]{:S(2)}) collective-permute-start(f32[32,1536]{1,0:T(8,128)} %copy.101), channel_id=1, source_target_pairs={{2,0},{4,2},{6,4},{8,6},{10,8},{12,10},{14,12},{16,14},{18,16},{20... | collective-permute-start | bytes 589832 | tf_op jit(solution)/shard_map/ppermute | solution.py:29
  840.0 60.0 %collective-permute-start.19 = (bf16[256,1536]{1,0:T(8,128)(2,1)}, bf16[256,1536]{1,0:T(8,128)(2,1)}, u32[]{:S(2)}, u32[]{:S(2)}) collective-permute-start(bf16[256,1536]{1,0:T(8,128)(2,1)} %copy.117), channel_id=1, source_target_pairs={{0,2},{2,4},{4,6},{6,8},{8,10},{10,12},{12,14},{14,16},{16,18},{18... | collective-permute-start | bytes 2359304 | tf_op jit(solution)/shard_map/ppermute | solution.py:18
  842.2 57.8 %collective-permute-start.18 = (bf16[256,1536]{1,0:T(8,128)(2,1)}, bf16[256,1536]{1,0:T(8,128)(2,1)}, u32[]{:S(2)}, u32[]{:S(2)}) collective-permute-start(bf16[256,1536]{1,0:T(8,128)(2,1)} %copy.115), channel_id=1, source_target_pairs={{2,0},{4,2},{6,4},{8,6},{10,8},{12,10},{14,12},{16,14},{18,16},{20... | collective-permute-start | bytes 2359304 | tf_op jit(solution)/shard_map/ppermute | solution.py:18
  850.5 52.2 %collective-permute-start.17 = (bf16[256,1536]{1,0:T(8,128)(2,1)}, bf16[256,1536]{1,0:T(8,128)(2,1)}, u32[]{:S(2)}, u32[]{:S(2)}) collective-permute-start(bf16[256,1536]{1,0:T(8,128)(2,1)} %copy.113), channel_id=1, source_target_pairs={{0,2},{2,4},{4,6},{6,8},{8,10},{10,12},{12,14},{14,16},{16,18},{18... | collective-permute-start | bytes 2359304 | tf_op jit(solution)/shard_map/ppermute | solution.py:18
  868.4 17.0 %collective-permute-start.21 = (bf16[32,1536]{1,0:T(8,128)(2,1)S(1)}, bf16[32,1536]{1,0:T(8,128)(2,1)S(1)}, u32[]{:S(2)}, u32[]{:S(2)}) collective-permute-start(bf16[32,1536]{1,0:T(8,128)(2,1)S(1)} %bitcast.187), channel_id=1, source_target_pairs={{0,2},{2,4},{4,6},{6,8},{8,10},{10,12},{12,14},{14,16},{16,18},{18... | collective-permute-start | bytes 294920 | tf_op jit(solution)/shard_map/ppermute | solution.py:18
  871.1 20.1 %collective-permute-start.20 = (bf16[32,1536]{1,0:T(8,128)(2,1)S(1)}, bf16[32,1536]{1,0:T(8,128)(2,1)S(1)}, u32[]{:S(2)}, u32[]{:S(2)}) collective-permute-start(bf16[32,1536]{1,0:T(8,128)(2,1)S(1)} %bitcast.185), channel_id=1, source_target_pairs={{2,0},{4,2},{6,4},{8,6},{10,8},{12,10},{14,12},{16,14},{18,16},{20... | collective-permute-start | bytes 294920 | tf_op jit(solution)/shard_map/ppermute | solution.py:18
  885.4 8.1 collective-permute-start.23
  891.3 8.0 collective-permute-start.22
  893.5 16.0 %collective-permute-start.16 = (bf16[256,1536]{1,0:T(8,128)(2,1)}, bf16[256,1536]{1,0:T(8,128)(2,1)S(1)}, u32[]{:S(2)}, u32[]{:S(2)}) collective-permute-start(bf16[256,1536]{1,0:T(8,128)(2,1)} %copy.111), channel_id=1, source_target_pairs={{2,0},{4,2},{6,4},{8,6},{10,8},{12,10},{14,12},{16,14},{18,16},{20... | collective-permute-start | bytes 2359304 | tf_op jit(solution)/shard_map/ppermute | solution.py:18
  (43 other events, 2495.2 us)
where the time goes:
time: 916 us; the launch traced here: 912 us
  blocking collectives  661 us (72%)
  starting transfers between devices  82.6 us (9%)
  waiting for transfers between devices  81.9 us (9%)
  local copies, waits for them, and re-layouts  36.2 us (4%)
  other arithmetic  31.6 us (3%)
  matrix products  16.6 us (2%)
    psum x1, blocking collectives, per_device(): lax.psum((taps_part_video, taps_part_audio, gain_part_video, gain_part_au...  650 us
    ppermute x4, waiting for transfers between devices, with_halo(): lax.ppermute(lax.slice_in_dim(block, 0, width, axis=dim), axis, backward)  52.7 us
    ppermute x16, starting transfers between devices, from_behind(): return lax.ppermute(block, axis, route)  47.2 us
    ppermute x4, starting transfers between devices, with_halo(): lax.ppermute(lax.slice_in_dim(block, block.shape[dim] - width, None, axis...  30.1 us
    ppermute x16, waiting for transfers between devices, from_behind(): return lax.ppermute(block, axis, route)  27.8 us
  transfers between devices with their start and end apart: 24, of which 8 were waited for; matrix products, arithmetic and copies ran while one was open for 7% of the time, Pallas kernels for 0%

commit v1 on v0

v1 whole, which is shorter than its diff:
```python
import jax
import jax.numpy as jnp
from jax import lax
from jax.experimental import pallas as pl
from jax.experimental.pallas import tpu as pltpu
from jax.sharding import PartitionSpec as P

HEAD_DIM = 128
STRIDE = 32
NEGATIVE = -1e30
EPSILON = 1e-06
FACTOR = HEAD_DIM ** (-0.5)
BLOCKS = ("video", "audio")
BF = jnp.bfloat16
F32 = jnp.float32
PAD = 128


def dot(a, b, over_a, over_b):
    return lax.dot_general(
        a, b, (((over_a,), (over_b,)), ((), ())), preferred_element_type=F32
    )


def call(kernel, outs, args, scalars, flops, scratch=()):
    vmem = pl.BlockSpec(memory_space=pltpu.VMEM)
    smem = pl.BlockSpec(memory_space=pltpu.SMEM)
    size = sum(a.size * a.dtype.itemsize for a in args)
    return pl.pallas_call(
        kernel,
        out_shape=[jax.ShapeDtypeStruct(s, d) for s, d in outs],
        in_specs=[smem] * len(scalars) + [vmem] * len(args),
        out_specs=[vmem] * len(outs),
        scratch_shapes=list(scratch),
        compiler_params=pltpu.CompilerParams(vmem_limit_bytes=48 * 1024 * 1024),
        cost_estimate=pl.CostEstimate(flops=flops, bytes_accessed=size, transcendentals=0),
    )(*scalars, *args)


def other(i, count):
    return (i + 2 * (i & 1) - 1 + count) & (count - 1)


def columns(h):
    return slice(h * HEAD_DIM, (h + 1) * HEAD_DIM)


def pack_stats(tile):
    high = tile.astype(BF).astype(F32)
    rest = tile - high
    middle = rest.astype(BF).astype(F32)
    low = rest - middle
    return (high + pltpu.roll(middle, 16, 1) + pltpu.roll(low, 32, 1)).astype(BF)


def unpack_stats(packed):
    wide = packed.astype(F32)
    return wide + (pltpu.roll(wide, PAD - 16, 1) + pltpu.roll(wide, PAD - 32, 1))


def audio_bias(i, count, window, valid, rows_q, rows_k):
    lane = lax.broadcasted_iota(jnp.int32, (rows_q, rows_k), 1)
    position = i * rows_k + lane
    parts = []
    for c in (i, i ^ 1, other(i, count)):
        seen = (position >= window[c, 0]) & (position < window[c, 1]) & (lane < valid[i])
        parts.append(jnp.where(seen, 0.0, NEGATIVE))
    return jnp.concatenate(parts, 0)


def video_bias(i, count, window, valid, rows_q, rows_k):
    row = lax.broadcasted_iota(jnp.int32, (rows_k, rows_q), 0)
    parts = []
    for c in (i, i ^ 1, other(i, count)):
        position = c * rows_k + row
        seen = (position >= window[i, 0]) & (position < window[i, 1]) & (row < valid[c])
        parts.append(jnp.where(seen, 0.0, NEGATIVE))
    return jnp.concatenate(parts, 0)


def audio_forward(count, idx, window, valid, q, qe, qo, k, v, send_e, send_o, own, own_lse):
    rows = q.shape[0]
    heads = q.shape[1] // HEAD_DIM
    bias = audio_bias(idx[0], count, window, valid, rows, k.shape[0])
    lane = lax.broadcasted_iota(jnp.int32, (3 * rows, PAD), 1)
    tile = jnp.zeros((3 * rows, PAD), F32)
    for h in range(heads):
        c = columns(h)
        near = jnp.concatenate([q[:, c], qe[:, c], qo[:, c]], 0)
        scores = dot(near, k[:, c], 1, 1) * FACTOR + bias
        peak = jnp.max(scores, 1, keepdims=True)
        weight = jnp.exp(scores - peak)
        total = jnp.sum(weight, 1, keepdims=True)
        part = dot(weight.astype(BF), v[:, c], 1, 0) / total
        tile = jnp.where(lane == h, peak + jnp.log(total), tile)
        own[:, c] = part[:rows]
        send_e[:, c] = part[rows : 2 * rows].astype(BF)
        send_o[:, c] = part[2 * rows :].astype(BF)
    own_lse[...] = tile[:rows]
    tail = slice(heads * HEAD_DIM, heads * HEAD_DIM + PAD)
    send_e[:, tail] = pack_stats(tile[rows : 2 * rows])
    send_o[:, tail] = pack_stats(tile[2 * rows :])


def video_forward(
    count, idx, window, valid, q, k, ke, ko, v, ve, vo, att, lse, send_e, send_o
):
    rows = q.shape[0]
    heads = q.shape[1] // HEAD_DIM
    i = idx[0]
    bias = video_bias(i, count, window, valid, rows, k.shape[0])
    lse[...] = jnp.zeros(lse.shape, F32)
    for h in range(heads):
        c = columns(h)
        keys = jnp.concatenate([k[:, c], ke[:, c], ko[:, c]], 0)
        values = jnp.concatenate([v[:, c], ve[:, c], vo[:, c]], 0)
        scores = dot(keys, q[:, c], 1, 1) * FACTOR + bias
        peak = jnp.max(scores, 0, keepdims=True)
        weight = jnp.exp(scores - peak)
        total = jnp.sum(weight, 0, keepdims=True)
        prob = (weight * (1.0 / total)).astype(BF)
        att[:, c] = dot(prob, values, 0, 0).astype(BF)
        lse[h : h + 1, :] = peak + jnp.log(total)
    half = send_e.shape[0]
    odd = i & 1
    last = rows - half
    send_e[...] = att[pl.ds(pl.multiple_of((1 - odd) * last, 64), half), :]
    send_o[...] = att[pl.ds(pl.multiple_of(odd * last, 64), half), :]


def audio_combine(idx, own, own_lse, re, ro, att, total, send_e, send_o):
    rows = own.shape[0]
    heads = own.shape[1] // HEAD_DIM
    tail = slice(heads * HEAD_DIM, heads * HEAD_DIM + PAD)
    mine = own_lse[...]
    first = unpack_stats(re[:, tail])
    second = unpack_stats(ro[:, tail])
    peak = jnp.maximum(mine, jnp.maximum(first, second))
    whole = peak + jnp.log(
        jnp.exp(mine - peak) + jnp.exp(first - peak) + jnp.exp(second - peak)
    )
    total[...] = whole
    wm, we, wo = jnp.exp(mine - whole), jnp.exp(first - whole), jnp.exp(second - whole)
    for h in range(heads):
        c = columns(h)
        att[:, c] = (
            own[:, c] * wm[:, h : h + 1]
            + re[:, c].astype(F32) * we[:, h : h + 1]
            + ro[:, c].astype(F32) * wo[:, h : h + 1]
        ).astype(BF)
    odd = idx[0] & 1
    send_e[...] = att[pl.ds(pl.multiple_of((1 - odd) * (rows - 16), 16), 16), :]
    send_o[...] = att[pl.ds(pl.multiple_of(odd * (rows - 16), 16), 16), :]


class Mix:
    def __init__(self, count, idx, refs):
        self.i = idx[0]
        self.even = (self.i & 1) == 0
        self.has_prev = (self.i > 0).astype(F32)
        self.has_next = (self.i < count - 1).astype(F32)
        (self.att_v, self.hve, self.hvo, self.cot_v, self.cve, self.cvo,
         self.att_a, self.hae, self.hao, self.cot_a, self.cae, self.cao,
         self.conv_v, self.conv_a, self.gain_v, self.gain_a) = refs
        self.chunks = self.att_v.shape[0] // STRIDE

    def before(self, e, o):
        return jnp.where(self.even, o.astype(F32), e.astype(F32)) * self.has_prev

    def after(self, e, o):
        return jnp.where(self.even, e.astype(F32), o.astype(F32)) * self.has_next

    def video_att(self, g, c):
        if 0 <= g < self.chunks:
            return self.att_v[g * STRIDE : (g + 1) * STRIDE, c].astype(F32)
        if g < 0:
            s = slice((g + 2) * STRIDE, (g + 3) * STRIDE)
            return self.before(self.hve[s, c], self.hvo[s, c])
        s = slice((g - self.chunks) * STRIDE, (g - self.chunks + 1) * STRIDE)
        return self.after(self.hve[s, c], self.hvo[s, c])

    def video_cot(self, g, c):
        if 0 <= g < self.chunks:
            return self.cot_v[g * STRIDE : (g + 1) * STRIDE, c].astype(F32)
        if g < 0:
            return self.before(self.cve[:, c], self.cvo[:, c])
        return self.after(self.cve[:, c], self.cvo[:, c])

    def extended(self, own, e, o, c):
        low = self.before(e[:, c], o[:, c])[8:16]
        high = self.after(e[:, c], o[:, c])[0:8]
        return jnp.concatenate([low, own[:, c].astype(F32), high], 0)

    def audio(self, c):
        att = self.extended(self.att_a, self.hae, self.hao, c)
        rows = att.shape[0]
        early = pltpu.roll(att, 1, 0)
        late = pltpu.roll(att, rows - 1, 0)
        taps = self.conv_a
        mixed = taps[0:1, c] * early + taps[1:2, c] * att + taps[2:3, c] * late
        cot = self.extended(self.cot_a, self.cae, self.cao, c)
        return mixed, cot, early, att, late


def row_sums(count, idx, *refs):
    mix = Mix(count, idx, refs[:-1])
    stats = refs[-1]
    heads = mix.att_v.shape[1] // HEAD_DIM
    rows_a = mix.att_a.shape[0] + 16
    lane = lax.broadcasted_iota(jnp.int32, (STRIDE, PAD), 1)
    tile = jnp.zeros((STRIDE, PAD), F32)
    taps = mix.conv_v
    for g in range(-1, mix.chunks + 1):
        square = jnp.zeros((STRIDE, HEAD_DIM), F32)
        inner = jnp.zeros((STRIDE, HEAD_DIM), F32)
        for h in range(heads):
            c = columns(h)
            mixed = (
                taps[0:1, c] * mix.video_att(g - 1, c)
                + taps[1:2, c] * mix.video_att(g, c)
                + taps[2:3, c] * mix.video_att(g + 1, c)
            )
            square += mixed * mixed
            inner += mix.video_cot(g, c) * mix.gain_v[0:1, c] * mixed
        tile = jnp.where(lane == g + 1, jnp.sum(square, 1, keepdims=True), tile)
        tile = jnp.where(lane == g + 17, jnp.sum(inner, 1, keepdims=True), tile)
    lane_a = lax.broadcasted_iota(jnp.int32, (rows_a, PAD), 1)
    square = jnp.zeros((rows_a, HEAD_DIM), F32)
    inner = jnp.zeros((rows_a, HEAD_DIM), F32)
    for h in range(heads):
        c = columns(h)
        mixed, cot, _, _, _ = mix.audio(c)
        square += mixed * mixed
        inner += cot * mix.gain_a[0:1, c] * mixed
    tile_a = jnp.where(
        lane_a == 0,
        jnp.sum(square, 1, keepdims=True),
        jnp.where(lane_a == 1, jnp.sum(inner, 1, keepdims=True), 0.0),
    )
    stats[0:STRIDE, :] = tile
    stats[STRIDE:, :] = tile_a


def norm_backward(count, width, idx, *refs):
    mix = Mix(count, idx, refs[2:18])
    mine, theirs = refs[0], refs[1]
    total_a = refs[18]
    out_v, up_v, out_a, up_a, up_send, dots_a, parts = refs[19:26]
    scale_ref, shrink_ref = refs[26:28]
    heads = mix.att_v.shape[1] // HEAD_DIM
    sums = mine[...] + theirs[...]
    rows_a = mix.att_a.shape[0]
    ext = rows_a + 16
    for g in range(mix.chunks + 2):
        inverse = lax.rsqrt(sums[0:STRIDE, g : g + 1] / width + EPSILON)
        inner = sums[0:STRIDE, g + 16 : g + 17]
        if g == 0:
            present = mix.has_prev
        elif g == mix.chunks + 1:
            present = mix.has_next
        else:
            present = 1.0
        s = slice(g * STRIDE, (g + 1) * STRIDE)
        scale_ref[s, :] = jnp.broadcast_to(inverse * present, (STRIDE, HEAD_DIM))
        shrink_ref[s, :] = jnp.broadcast_to(
            inverse * inverse * inverse * inner / width * present, (STRIDE, HEAD_DIM)
        )
    row = lax.broadcasted_iota(jnp.int32, (ext, HEAD_DIM), 0)
    present = jnp.where(row < 8, mix.has_prev, jnp.where(row >= rows_a + 8, mix.has_next, 1.0))
    inverse = lax.rsqrt(sums[STRIDE:, 0:1] / width + EPSILON)
    scale_a = jnp.broadcast_to(inverse, (ext, HEAD_DIM)) * present
    shrink_a = (
        jnp.broadcast_to(
            inverse * inverse * inverse * sums[STRIDE:, 1:2] / width, (ext, HEAD_DIM)
        )
        * present
    )
    lane = lax.broadcasted_iota(jnp.int32, (rows_a, PAD), 1)
    dots = jnp.zeros((rows_a, PAD), F32)
    own = slice(8, 8 + rows_a)
    for h in range(heads):
        c = columns(h)
        taps = [mix.conv_v[k : k + 1, c] for k in range(3)]
        gain = mix.gain_v[0:1, c]
        sum_taps = [jnp.zeros((STRIDE, HEAD_DIM), F32) for _ in range(3)]
        sum_gain = jnp.zeros((STRIDE, HEAD_DIM), F32)
        atts = [mix.video_att(g, c) for g in (-2, -1, 0)]
        grads = []
        for g in range(-1, mix.chunks + 1):
            early, here, late = atts
            mixed = taps[0] * early + taps[1] * here + taps[2] * late
            s = slice((g + 1) * STRIDE, (g + 2) * STRIDE)
            scale = scale_ref[s, :]
            incoming = mix.video_cot(g, c)
            grad = scale * (incoming * gain) - mixed * shrink_ref[s, :]
            if 0 <= g < mix.chunks:
                normed = mixed * scale
                out_v[g * STRIDE : (g + 1) * STRIDE, c] = (normed * gain).astype(BF)
                sum_gain += incoming * normed
                for k in range(3):
                    sum_taps[k] += grad * atts[k]
            grads = (grads + [grad])[-3:]
            if g >= 1:
                up_v[(g - 1) * STRIDE : g * STRIDE, c] = (
                    taps[0] * grads[2] + taps[1] * grads[1] + taps[2] * grads[0]
                ).astype(BF)
            if g < mix.chunks:
                atts = atts[1:] + [mix.video_att(g + 2, c)]
        for k in range(3):
            parts[k : k + 1, c] = jnp.sum(sum_taps[k], 0, keepdims=True)
        parts[3:4, c] = jnp.sum(sum_gain, 0, keepdims=True)

        mixed, cot, early, att, late = mix.audio(c)
        gain = mix.gain_a[0:1, c]
        taps = [mix.conv_a[k : k + 1, c] for k in range(3)]
        normed = mixed * scale_a
        grad = scale_a * (cot * gain) - mixed * shrink_a
        out_a[:, c] = (normed * gain)[own].astype(BF)
        upstream = (
            taps[0] * pltpu.roll(grad, ext - 1, 0)
            + taps[1] * grad
            + taps[2] * pltpu.roll(grad, 1, 0)
        )[own].astype(BF)
        up_a[:, c] = upstream
        up_send[:, c] = upstream
        row_dot = jnp.sum(upstream.astype(F32) * att[own], 1, keepdims=True)
        dots = jnp.where(lane == h, row_dot, dots)
        for k, shifted in enumerate((early, att, late)):
            parts[4 + k : 5 + k, c] = jnp.sum((grad * shifted)[own], 0, keepdims=True)
        parts[7:8, c] = jnp.sum((cot * normed)[own], 0, keepdims=True)
    dots_a[...] = dots
    tail = slice(heads * HEAD_DIM, heads * HEAD_DIM + PAD)
    packed = pack_stats(jnp.where(lane < heads, total_a[...], 0.0)).astype(F32)
    packed_dots = pack_stats(dots).astype(F32)
    up_send[:, tail] = (packed + pltpu.roll(packed_dots, 64, 1)).astype(BF)


def video_backward(
    count, idx, window, valid, q, up, lse, k, ke, ko, v, ve, vo, dq, own, send_e, send_o
):
    rows = q.shape[0]
    heads = q.shape[1] // HEAD_DIM
    near = k.shape[0]
    bias = video_bias(idx[0], count, window, valid, rows, near)
    for h in range(heads):
        c = columns(h)
        keys = jnp.concatenate([k[:, c], ke[:, c], ko[:, c]], 0)
        values = jnp.concatenate([v[:, c], ve[:, c], vo[:, c]], 0)
        queries = q[:, c]
        upstream = up[:, c]
        scores = dot(keys, queries, 1, 1) * FACTOR + bias
        prob = jnp.exp(scores - lse[h : h + 1, :])
        prob_grad = dot(values, upstream, 1, 1)
        row_dot = jnp.sum(prob * prob_grad, 0, keepdims=True)
        score_grad = (prob * (prob_grad - row_dot)).astype(BF)
        dq[:, c] = (dot(score_grad, keys, 0, 0) * FACTOR).astype(BF)
        dk = dot(score_grad, queries, 1, 0) * FACTOR
        dv = dot(prob.astype(BF), upstream, 1, 0)
        own[0:near, c] = dk[0:near]
        own[near:, c] = dv[0:near]
        send_e[0:near, c] = dk[near : 2 * near].astype(BF)
        send_e[near:, c] = dv[near : 2 * near].astype(BF)
        send_o[0:near, c] = dk[2 * near :].astype(BF)
        send_o[near:, c] = dv[2 * near :].astype(BF)


def audio_backward(
    count, idx, window, valid, q, qe, qo, up, upe, upo, total, dots, k, v,
    dk, dv, own, send_e, send_o,
):
    rows = q.shape[0]
    heads = q.shape[1] // HEAD_DIM
    tail = slice(heads * HEAD_DIM, heads * HEAD_DIM + PAD)
    bias = audio_bias(idx[0], count, window, valid, rows, k.shape[0])
    totals, row_dots = [total[...]], [dots[...]]
    for packed in (upe[:, tail], upo[:, tail]):
        wide = unpack_stats(packed)
        totals.append(wide)
        row_dots.append(pltpu.roll(wide, 64, 1))
    totals = jnp.concatenate(totals, 0)
    row_dots = jnp.concatenate(row_dots, 0)
    for h in range(heads):
        c = columns(h)
        queries = jnp.concatenate([q[:, c], qe[:, c], qo[:, c]], 0)
        upstream = jnp.concatenate([up[:, c], upe[:, c], upo[:, c]], 0)
        keys, values = k[:, c], v[:, c]
        scores = dot(queries, keys, 1, 1) * FACTOR + bias
        prob = jnp.exp(scores - totals[:, h : h + 1])
        prob_grad = dot(upstream, values, 1, 1)
        score_grad = (prob * (prob_grad - row_dots[:, h : h + 1])).astype(BF)
        dq = dot(score_grad, keys, 1, 0) * FACTOR
        dk[:, c] = (dot(score_grad, queries, 0, 0) * FACTOR).astype(BF)
        dv[:, c] = dot(prob.astype(BF), upstream, 0, 0).astype(BF)
        own[:, c] = dq[:rows]
        send_e[:, c] = dq[rows : 2 * rows].astype(BF)
        send_o[:, c] = dq[2 * rows :].astype(BF)


def per_device(
    query_video,
    key_video,
    value_video,
    query_audio,
    key_audio,
    value_audio,
    conv_video,
    conv_audio,
    gain_video,
    gain_audio,
    video_window,
    audio_window,
    video_valid,
    audio_valid,
    cotangent_video,
    cotangent_audio,
):
    count = video_window.shape[0]
    block = lax.axis_index(BLOCKS)
    idx = block.astype(jnp.int32).reshape(1)
    odd = block & 1
    rows_v, wide = query_video.shape
    rows_a = query_audio.shape[0]
    heads = wide // HEAD_DIM
    model = wide * lax.axis_size("tp")
    even_route = [(i, i ^ 1) for i in range(count)]
    odd_route = [(i, other(i, count)) for i in range(count)]

    def swap_e(x):
        return lax.ppermute(x, BLOCKS, even_route)

    def swap_o(x):
        return lax.ppermute(x, BLOCKS, odd_route)

    def bind(f, *extra):
        def kernel(*refs):
            return f(*extra, *refs)

        return kernel

    qe, qo = swap_e(query_audio), swap_o(query_audio)
    ke, ko = swap_e(key_audio), swap_o(key_audio)
    ve, vo = swap_e(value_audio), swap_o(value_audio)

    def edge(x, rows, to_even):
        last = x.shape[0] - rows
        start = (1 - odd) * last if to_even else odd * last
        return lax.dynamic_slice_in_dim(x, start, rows, 0)

    cve = swap_e(edge(cotangent_video, STRIDE, True))
    cvo = swap_o(edge(cotangent_video, STRIDE, False))
    cae = swap_e(edge(cotangent_audio, 16, True))
    cao = swap_o(edge(cotangent_audio, 16, False))

    mm = 2 * heads * 3 * rows_a * rows_v * HEAD_DIM
    packed = ((rows_a, wide + PAD), BF)
    audio_info = (idx, audio_window, video_valid)
    video_info = (idx, video_window, audio_valid)
    send_e, send_o, own_part, own_lse = call(
        bind(audio_forward, count),
        [packed, packed, ((rows_a, wide), F32), ((rows_a, PAD), F32)],
        [query_audio, qe, qo, key_video, value_video],
        audio_info,
        2 * mm,
    )
    pe, po = swap_e(send_e), swap_o(send_o)
    keys_values = [key_audio, ke, ko, value_audio, ve, vo]
    halo = ((2 * STRIDE, wide), BF)
    att_v, lse_v, hv_e, hv_o = call(
        bind(video_forward, count),
        [((rows_v, wide), BF), (((heads + 7) // 8 * 8, rows_v), F32), halo, halo],
        [query_video] + keys_values,
        video_info,
        2 * mm,
    )
    hve, hvo = swap_e(hv_e), swap_o(hv_o)
    halo_a = ((16, wide), BF)
    att_a, total_a, ha_e, ha_o = call(
        audio_combine,
        [((rows_a, wide), BF), ((rows_a, PAD), F32), halo_a, halo_a],
        [own_part, own_lse, pe, po],
        (idx,),
        10**6,
    )
    hae, hao = swap_e(ha_e), swap_o(ha_o)

    mix_args = [
        att_v, hve, hvo, cotangent_video, cve, cvo,
        att_a, hae, hao, cotangent_audio, cae, cao,
        conv_video, conv_audio, gain_video.reshape(1, wide), gain_audio.reshape(1, wide),
    ]
    stats_rows = STRIDE + rows_a + 16
    (stats,) = call(
        bind(row_sums, count), [((stats_rows, PAD), F32)], mix_args, (idx,), 10**7
    )
    tp_size = lax.axis_size("tp")
    stats_other = lax.ppermute(stats, "tp", [(i, i ^ 1) for i in range(tp_size)])
    chunks = rows_v // STRIDE
    out_v, up_v, out_a, up_a, up_send, dots_a, parts = call(
        bind(norm_backward, count, model),
        [
            ((rows_v, wide), BF),
            ((rows_v, wide), BF),
            ((rows_a, wide), BF),
            ((rows_a, wide), BF),
            packed,
            ((rows_a, PAD), F32),
            ((8, wide), F32),
        ],
        [stats, stats_other] + mix_args + [total_a],
        (idx,),
        10**7,
        [pltpu.VMEM(((chunks + 2) * STRIDE, HEAD_DIM), F32)] * 2,
    )
    upe, upo = swap_e(up_send), swap_o(up_send)
    total = parts
    for bits in (1, 2, 4, 14, 16, 32, 96):
        total = total + lax.ppermute(total, BLOCKS, [(i, i ^ bits) for i in range(count)])

    two = ((2 * rows_a, wide), BF)
    dq_v, dkv_own, dkv_e, dkv_o = call(
        bind(video_backward, count),
        [((rows_v, wide), BF), ((2 * rows_a, wide), F32), two, two],
        [query_video, up_v, lse_v] + keys_values,
        video_info,
        5 * mm,
    )
    dkve, dkvo = swap_e(dkv_e), swap_o(dkv_o)
    dk_v, dv_v, dq_own, dq_e, dq_o = call(
        bind(audio_backward, count),
        [
            ((rows_v, wide), BF),
            ((rows_v, wide), BF),
            ((rows_a, wide), F32),
            ((rows_a, wide), BF),
            ((rows_a, wide), BF),
        ],
        [query_audio, qe, qo, up_a, upe, upo, total_a, dots_a, key_video, value_video],
        audio_info,
        5 * mm,
    )
    dqe, dqo = swap_e(dq_e), swap_o(dq_o)
    dkv = (dkv_own + dkve.astype(F32) + dkvo.astype(F32)).astype(BF)
    dq_a = (dq_own + dqe.astype(F32) + dqo.astype(F32)).astype(BF)
    return (
        out_v,
        out_a,
        dq_v,
        dk_v,
        dv_v,
        dq_a,
        dkv[:rows_a],
        dkv[rows_a:],
        total[0:3],
        total[4:7],
        total[3],
        total[7],
    )


def solution(mesh):
    rows = P(BLOCKS, "tp")
    in_specs = (rows,) * 6 + (P(None, "tp"),) * 2 + (P("tp"),) * 2 + (P(),) * 4 + (rows,) * 2
    out_specs = (rows,) * 8 + (P(None, "tp"),) * 2 + (P("tp"),) * 2
    return jax.shard_map(
        per_device, mesh=mesh, in_specs=in_specs, out_specs=out_specs, check_vma=False
    )
```

time: 916 us -> 118 us (0.13)
  blocking collectives: 661 us -> 0 us
  waiting for transfers between devices: 81.9 us -> 24.9 us
  local copies, waits for them, and re-layouts: 36.2 us -> 5.38 us
  other arithmetic: 31.6 us -> 0.79 us
  Pallas kernels: 0 us -> 24 us
  starting transfers between devices: 82.6 us -> 61.9 us
  matrix products: 16.6 us -> 0 us
    psum x3 -> x0, blocking collectives: 661 us -> none  [the longest x1 650 us: per_device(): lax.psum((taps_part_video, taps_part_audio, gain_part_video, gain_part_au...]
    ppermute x24 -> x30, waiting for transfers between devices: 81.9 us -> 24.9 us  [the longest x7 12 us: per_device(): lax.ppermute(total, BLOCKS, [(i, i ^ bits) for i in range(count)])]
    pallas_call x0 -> x7, Pallas kernels: none -> 24 us  [call(): pl.pallas_call(kernel, out_shape=[jax.ShapeDtypeStruct(s, d) for s, d in...]
    ppermute x24 -> x30, starting transfers between devices: 82.6 us -> 61.9 us  [the longest x11 45.4 us: swap_o(): return lax.ppermute(x, BLOCKS, odd_route)]
    dot_general x12 -> x0, matrix products: 16.6 us -> none  [the longest x2 4.07 us: returned_parts(): jnp.einsum('hqk,qhd->khd', score_grad, split_heads(queries), preferred_el...]
    reduce_sum x8 -> x0, other arithmetic: 15.2 us -> none  [the longest x2 5.91 us: mix_backward(): jnp.sum(mixed_grad * earlier, 0)]
    slice x16 -> x3, local copies, waits for them, and re-layouts: 15.1 us -> 1.94 us  [the longest x1 0.69 us: per_device(): dkv[rows_a:]]
    unnamed x94 -> x38, local copies, waits for them, and re-layouts: 12.8 us -> 2.56 us
  transfers between devices with their start and end apart: 24 -> 30, of which waited for: 8 -> 11; matrix products, arithmetic and copies ran while one was open for 7% -> 2% of each run, Pallas kernels for 0% -> 16%
where the time goes in v1:
time: 118 us
  starting transfers between devices  61.9 us (52%)
  waiting for transfers between devices  24.9 us (21%)
  Pallas kernels  24 us (20%)
  local copies, waits for them, and re-layouts  5.38 us (5%)
    ppermute x11, starting transfers between devices, swap_o(): return lax.ppermute(x, BLOCKS, odd_route)  45.4 us
    pallas_call x7, Pallas kernels, call(): pl.pallas_call(kernel, out_shape=[jax.ShapeDtypeStruct(s, d) for s, d in...  24 us
    ppermute x7, waiting for transfers between devices, per_device(): lax.ppermute(total, BLOCKS, [(i, i ^ bits) for i in range(count)])  12 us
    ppermute x11, starting transfers between devices, swap_e(): return lax.ppermute(x, BLOCKS, even_route)  11.9 us
    ppermute x11, waiting for transfers between devices, swap_e(): return lax.ppermute(x, BLOCKS, even_route)  5.39 us
    ppermute x11, waiting for transfers between devices, swap_o(): return lax.ppermute(x, BLOCKS, odd_route)  4.59 us
    ppermute x7, starting transfers between devices, per_device(): lax.ppermute(total, BLOCKS, [(i, i ^ bits) for i in range(count)])  3 us
    ppermute x1, waiting for transfers between devices, per_device(): lax.ppermute(stats, 'tp', [(i, i ^ 1) for i in range(tp_size)])  2.91 us
  transfers between devices with their start and end apart: 30, of which 11 were waited for; matrix products, arithmetic and copies ran while one was open for 2% of the time, Pallas kernels for 16%

profile of v1, /device:TPU:2, one launch (start us, length us, event | category | flops | bytes accessed | tf_op | source)
XLA Modules:
  0.0 117.9 jit_solution(6781939129255133080)
XLA Ops:
  0.6 9.4 %collective-permute-start.9 = (bf16[32,1536]{1,0:T(8,128)(2,1)}, bf16[32,1536]{1,0:T(8,128)(2,1)S(1)}, u32[]{:S(2)}, u32[]{:S(2)}) collective-permute-start(bf16[32,1536]{1,0:T(8,128)(2,1)} %refs_3_.7), channel_id=1, source_target_pairs={{0,254},{2,4},{4,2},{6,8},{8,6},{10,12},{12,10},{14,16},{16,14},{1... | collective-permute-start | bytes 294920 | tf_op jit(solution)/shard_map/ppermute | solution.py:432
  10.0 3.4 %collective-permute-start.1 = (bf16[32,1536]{1,0:T(8,128)(2,1)}, bf16[32,1536]{1,0:T(8,128)(2,1)S(1)}, u32[]{:S(2)}, u32[]{:S(2)}) collective-permute-start(bf16[32,1536]{1,0:T(8,128)(2,1)} %refs_6_.5), channel_id=1, source_target_pairs={{0,254},{2,4},{4,2},{6,8},{8,6},{10,12},{12,10},{14,16},{16,14},{1... | collective-permute-start | bytes 294920 | tf_op jit(solution)/shard_map/ppermute | solution.py:432
  13.6 3.9 %collective-permute-start.3 = (bf16[32,1536]{1,0:T(8,128)(2,1)}, bf16[32,1536]{1,0:T(8,128)(2,1)S(1)}, u32[]{:S(2)}, u32[]{:S(2)}) collective-permute-start(bf16[32,1536]{1,0:T(8,128)(2,1)} %refs_9_.1), channel_id=1, source_target_pairs={{0,254},{2,4},{4,2},{6,8},{8,6},{10,12},{12,10},{14,16},{16,14},{1... | collective-permute-start | bytes 294920 | tf_op jit(solution)/shard_map/ppermute | solution.py:432
  19.1 2.4 %collective-permute-done.8.refs_4_ = bf16[32,1536]{1,0:T(8,128)(2,1)S(1)} collective-permute-done((bf16[32,1536]{1,0:T(8,128)(2,1)}, bf16[32,1536]{1,0:T(8,128)(2,1)S(1)}, u32[]{:S(2)}, u32[]{:S(2)}) %collective-permute-start.8) | collective-permute-done | bytes 98336 | tf_op jit(solution)/shard_map/ppermute | solution.py:429
  24.5 4.5 %shard_map.248 = (bf16[32,1664]{1,0:T(8,128)(2,1)S(1)}, bf16[32,1664]{1,0:T(8,128)(2,1)S(1)}, f32[32,1536]{1,0:T(8,128)S(1)}, f32[32,128]{1,0:T(8,128)S(1)}) custom-call(s32[1]{0:T(128)} %bitcast.refs_0_.idx, s32[128,2]{1,0:T(8,128)S(1)} %copy.29.refs_1_, s32[128]{0:T(128)S(1)} %copy-done.13, bf16[32,1536]{1,0:T(8,128)(2,1)S(1)} %copy-done.7, ...), custom_call_target="tpu_custom_call" | custom-call | flops 150994944 | bytes 1867776 | tf_op jit(solution)/shard_map/pallas_call | solution.py:29
  29.7 6.2 %collective-permute-start.11 = (bf16[32,1664]{1,0:T(8,128)(2,1)S(1)}, bf16[32,1664]{1,0:T(8,128)(2,1)S(1)}, u32[]{:S(2)}, u32[]{:S(2)}) collective-permute-start(bf16[32,1664]{1,0:T(8,128)(2,1)S(1)} %get-tuple-element.46), channel_id=1, source_target_pairs={{0,254},{2,4},{4,2},{6,8},{8,6},{10,12},{12,10},{14,16},{16,14},{1... | collective-permute-start | bytes 319496 | tf_op jit(solution)/shard_map/ppermute | solution.py:432
  36.0 2.7 %shard_map.247 = (bf16[256,1536]{1,0:T(8,128)(2,1)S(1)}, f32[16,256]{1,0:T(8,128)S(1)}, bf16[64,1536]{1,0:T(8,128)(2,1)S(1)}, bf16[64,1536]{1,0:T(8,128)(2,1)S(1)}) custom-call(s32[1]{0:T(128)} %bitcast.refs_0_.idx, s32[128,2]{1,0:T(8,128)S(1)} %copy.28.refs_1_, s32[128]{0:T(128)S(1)} %copy-done.12, bf16[256,1536]{1,0:T(8,128)(2,1)S(1)} %copy-done.5, ...), custom_call_target="tpu_custom_call" | custom-call | flops 150994944 | bytes 1376256 | tf_op jit(solution)/shard_map/pallas_call | solution.py:29
  38.8 2.9 %collective-permute-start.5 = (bf16[64,1536]{1,0:T(8,128)(2,1)S(1)}, bf16[64,1536]{1,0:T(8,128)(2,1)S(1)}, u32[]{:S(2)}, u32[]{:S(2)}) collective-permute-start(bf16[64,1536]{1,0:T(8,128)(2,1)S(1)} %get-tuple-element.42), channel_id=1, source_target_pairs={{0,254},{2,4},{4,2},{6,8},{8,6},{10,12},{12,10},{14,16},{16,14},{1... | collective-permute-start | bytes 589832 | tf_op jit(solution)/shard_map/ppermute | solution.py:432
  41.7 4.8 %collective-permute-start.7 = (bf16[32,1536]{1,0:T(8,128)(2,1)S(1)}, bf16[32,1536]{1,0:T(8,128)(2,1)S(1)}, u32[]{:S(2)}, u32[]{:S(2)}) collective-permute-start(bf16[32,1536]{1,0:T(8,128)(2,1)S(1)} %get-tuple-element.70), channel_id=1, source_target_pairs={{0,254},{2,4},{4,2},{6,8},{8,6},{10,12},{12,10},{14,16},{16,14},{1... | collective-permute-start | bytes 294920 | tf_op jit(solution)/shard_map/ppermute | solution.py:432
  46.9 3.1 %collective-permute-start.6 = (bf16[32,1536]{1,0:T(8,128)(2,1)S(1)}, bf16[32,1536]{1,0:T(8,128)(2,1)S(1)}, u32[]{:S(2)}, u32[]{:S(2)}) collective-permute-start(bf16[32,1536]{1,0:T(8,128)(2,1)S(1)} %get-tuple-element.71), channel_id=1, source_target_pairs={{0,2},{2,0},{4,6},{6,4},{8,10},{10,8},{12,14},{14,12},{16,18},{18,... | collective-permute-start | bytes 294920 | tf_op jit(solution)/shard_map/ppermute | solution.py:429
  53.0 4.4 %collective-permute-start.13 = (bf16[16,1536]{1,0:T(8,128)(2,1)S(1)}, bf16[16,1536]{1,0:T(8,128)(2,1)S(1)}, u32[]{:S(2)}, u32[]{:S(2)}) collective-permute-start(bf16[16,1536]{1,0:T(8,128)(2,1)S(1)} %get-tuple-element.49), channel_id=1, source_target_pairs={{0,254},{2,4},{4,2},{6,8},{8,6},{10,12},{12,10},{14,16},{16,14},{1... | collective-permute-start | bytes 147464 | tf_op jit(solution)/shard_map/ppermute | solution.py:432
  57.9 4.4 %collective-permute-done.13.refs_9_.refs_11_ = bf16[16,1536]{1,0:T(8,128)(2,1)S(1)} collective-permute-done((bf16[16,1536]{1,0:T(8,128)(2,1)S(1)}, bf16[16,1536]{1,0:T(8,128)(2,1)S(1)}, u32[]{:S(2)}, u32[]{:S(2)}) %collective-permute-start.13) | collective-permute-done | bytes 49184 | tf_op jit(solution)/shard_map/ppermute | solution.py:432
  65.0 2.9 %collective-permute-done.16.refs_2_ = f32[80,128]{1,0:T(8,128)S(1)} collective-permute-done((f32[80,128]{1,0:T(8,128)S(1)}, f32[80,128]{1,0:T(8,128)S(1)}, u32[]{:S(2)}, u32[]{:S(2)}) %collective-permute-start.16) | collective-permute-done | bytes 40992 | tf_op jit(solution)/shard_map/ppermute | solution.py:496
  68.0 3.4 %shard_map.251 = (bf16[256,1536]{1,0:T(8,128)(2,1)}, bf16[256,1536]{1,0:T(8,128)(2,1)S(1)}, bf16[32,1536]{1,0:T(8,128)(2,1)}, bf16[32,1536]{1,0:T(8,128)(2,1)S(1...) custom-call(s32[1]{0:T(128)} %bitcast.refs_0_.idx, ...), custom_call_target="tpu_custom_call" | custom-call | flops 10000000 | bytes 2703360 | tf_op jit(solution)/shard_map/pallas_call | solution.py:29
  71.4 5.8 %shard_map.252 = (bf16[256,1536]{1,0:T(8,128)(2,1)}, f32[64,1536]{1,0:T(8,128)S(1)}, bf16[64,1536]{1,0:T(8,128)(2,1)S(1)}, bf16[64,1536]{1,0:T(8,128)(2,1)S(1)}) custom-call(s32[1]{0:T(128)} %bitcast.refs_0_.idx, s32[128,2]{1,0:T(8,128)S(1)} %copy.28.refs_1_, s32[128]{0:T(128)S(1)} %copy-done.12, bf16[256,1536]{1,0:T(8,128)(2,1)S(1)} %copy-done.5, ...), custom_call_target="tpu_custom_call" | custom-call | flops 377487360 | bytes 2179072 | tf_op jit(solution)/shard_map/pallas_call | solution.py:29
  77.2 3.5 %collective-permute-start.21 = (bf16[64,1536]{1,0:T(8,128)(2,1)S(1)}, bf16[64,1536]{1,0:T(8,128)(2,1)S(1)}, u32[]{:S(2)}, u32[]{:S(2)}) collective-permute-start(bf16[64,1536]{1,0:T(8,128)(2,1)S(1)} %get-tuple-element.65), channel_id=1, source_target_pairs={{0,2},{2,0},{4,6},{6,4},{8,10},{10,8},{12,14},{14,12},{16,18},{18,... | collective-permute-start | bytes 589832 | tf_op jit(solution)/shard_map/ppermute | solution.py:429
  80.7 2.4 %collective-permute-start.22 = (bf16[64,1536]{1,0:T(8,128)(2,1)S(1)}, bf16[64,1536]{1,0:T(8,128)(2,1)S(1)}, u32[]{:S(2)}, u32[]{:S(2)}) collective-permute-start(bf16[64,1536]{1,0:T(8,128)(2,1)S(1)} %get-tuple-element.66), channel_id=1, source_target_pairs={{0,254},{2,4},{4,2},{6,8},{8,6},{10,12},{12,10},{14,16},{16,14},{1... | collective-permute-start | bytes 589832 | tf_op jit(solution)/shard_map/ppermute | solution.py:432
  83.2 5.2 %collective-permute-start.18 = (bf16[32,1664]{1,0:T(8,128)(2,1)S(1)}, bf16[32,1664]{1,0:T(8,128)(2,1)S(1)}, u32[]{:S(2)}, u32[]{:S(2)}) collective-permute-start(bf16[32,1664]{1,0:T(8,128)(2,1)S(1)} %get-tuple-element.57), channel_id=1, source_target_pairs={{0,254},{2,4},{4,2},{6,8},{8,6},{10,12},{12,10},{14,16},{16,14},{1... | collective-permute-start | bytes 319496 | tf_op jit(solution)/shard_map/ppermute | solution.py:432
  88.5 5.0 %collective-permute-done.25 = f32[8,1536]{1,0:T(8,128)S(1)} collective-permute-done((f32[8,1536]{1,0:T(8,128)S(1)}, f32[8,1536]{1,0:T(8,128)S(1)}, u32[]{:S(2)}, u32[]{:S(2)}) %collective-permute-start.25) | collective-permute-done | bytes 49184 | tf_op jit(solution)/shard_map/ppermute | solution.py:517
  94.6 5.9 %shard_map.253 = (bf16[256,1536]{1,0:T(8,128)(2,1)}, bf16[256,1536]{1,0:T(8,128)(2,1)}, f32[32,1536]{1,0:T(8,128)S(1)}, bf16[32,1536]{1,0:T(8,128)(2,1)S(1)}, bf16[32,1536]{1,0:T(8,128)(2,1)S(1)}) custom-call(s32[1]{0:T(128)} %bitcast.refs_0_.idx, s32[128,2]{1,0:T(8,128)S(1)} %copy.29.refs_1_, s32[128]{0:T(128)S(1)} %copy-done.13, ...), custom_call_target="tpu_custom_call" | custom-call | flops 377487360 | bytes 2211840 | tf_op jit(solution)/shard_map/pallas_call | solution.py:29
  100.6 2.8 %collective-permute-start.19 = (bf16[32,1536]{1,0:T(8,128)(2,1)S(1)}, bf16[32,1536]{1,0:T(8,128)(2,1)S(1)}, u32[]{:S(2)}, u32[]{:S(2)}) collective-permute-start(bf16[32,1536]{1,0:T(8,128)(2,1)S(1)} %get-tuple-element.62), channel_id=1, source_target_pairs={{0,2},{2,0},{4,6},{6,4},{8,10},{10,8},{12,14},{14,12},{16,18},{18,... | collective-permute-start | bytes 294920 | tf_op jit(solution)/shard_map/ppermute | solution.py:429
  103.4 2.1 %collective-permute-start.20 = (bf16[32,1536]{1,0:T(8,128)(2,1)S(1)}, bf16[32,1536]{1,0:T(8,128)(2,1)S(1)}, u32[]{:S(2)}, u32[]{:S(2)}) collective-permute-start(bf16[32,1536]{1,0:T(8,128)(2,1)S(1)} %get-tuple-element.63), channel_id=1, source_target_pairs={{0,254},{2,4},{4,2},{6,8},{8,6},{10,12},{12,10},{14,16},{16,14},{1... | collective-permute-start | bytes 294920 | tf_op jit(solution)/shard_map/ppermute | solution.py:432
  107.9 3.4 %collective-permute-done.28 = f32[8,1536]{1,0:T(8,128)S(1)} collective-permute-done((f32[8,1536]{1,0:T(8,128)S(1)}, f32[8,1536]{1,0:T(8,128)S(1)}, u32[]{:S(2)}, u32[]{:S(2)}) %collective-permute-start.28) | collective-permute-done | bytes 49184 | tf_op jit(solution)/shard_map/ppermute | solution.py:517
  113.8 2.8 %collective-permute-done.29 = f32[8,1536]{1,0:T(8,128)S(1)} collective-permute-done((f32[8,1536]{1,0:T(8,128)S(1)}, f32[8,1536]{1,0:T(8,128)S(1)}, u32[]{:S(2)}, u32[]{:S(2)}) %collective-permute-start.29) | collective-permute-done | bytes 49184 | tf_op jit(solution)/shard_map/ppermute | solution.py:517
  (97 shorter events, 19.6 us)
Async XLA Ops:
  0.6 16.9 %collective-permute-start.9 = (bf16[32,1536]{1,0:T(8,128)(2,1)}, bf16[32,1536]{1,0:T(8,128)(2,1)S(1)}, u32[]{:S(2)}, u32[]{:S(2)}) collective-permute-start(bf16[32,1536]{1,0:T(8,128)(2,1)} %refs_3_.7), channel_id=1, source_target_pairs={{0,254},{2,4},{4,2},{6,8},{8,6},{10,12},{12,10},{14,16},{16,14},{1... | collective-permute-start | bytes 294920 | tf_op jit(solution)/shard_map/ppermute | solution.py:432
  10.0 11.4 %collective-permute-start.8 = (bf16[32,1536]{1,0:T(8,128)(2,1)}, bf16[32,1536]{1,0:T(8,128)(2,1)S(1)}, u32[]{:S(2)}, u32[]{:S(2)}) collective-permute-start(bf16[32,1536]{1,0:T(8,128)(2,1)} %refs_3_.7), channel_id=1, source_target_pairs={{0,2},{2,0},{4,6},{6,4},{8,10},{10,8},{12,14},{14,12},{16,18},{18,... | collective-permute-start | bytes 294920 | tf_op jit(solution)/shard_map/ppermute | solution.py:429
  10.0 19.0 %collective-permute-start.1 = (bf16[32,1536]{1,0:T(8,128)(2,1)}, bf16[32,1536]{1,0:T(8,128)(2,1)S(1)}, u32[]{:S(2)}, u32[]{:S(2)}) collective-permute-start(bf16[32,1536]{1,0:T(8,128)(2,1)} %refs_6_.5), channel_id=1, source_target_pairs={{0,254},{2,4},{4,2},{6,8},{8,6},{10,12},{12,10},{14,16},{16,14},{1... | collective-permute-start | bytes 294920 | tf_op jit(solution)/shard_map/ppermute | solution.py:432
  13.5 16.3 %collective-permute-start = (bf16[32,1536]{1,0:T(8,128)(2,1)}, bf16[32,1536]{1,0:T(8,128)(2,1)S(1)}, u32[]{:S(2)}, u32[]{:S(2)}) collective-permute-start(bf16[32,1536]{1,0:T(8,128)(2,1)} %refs_6_.5), channel_id=1, source_target_pairs={{0,2},{2,0},{4,6},{6,4},{8,10},{10,8},{12,14},{14,12},{16,18},{18,... | collective-permute-start | bytes 294920 | tf_op jit(solution)/shard_map/ppermute | solution.py:429
  13.6 22.4 %collective-permute-start.3 = (bf16[32,1536]{1,0:T(8,128)(2,1)}, bf16[32,1536]{1,0:T(8,128)(2,1)S(1)}, u32[]{:S(2)}, u32[]{:S(2)}) collective-permute-start(bf16[32,1536]{1,0:T(8,128)(2,1)} %refs_9_.1), channel_id=1, source_target_pairs={{0,254},{2,4},{4,2},{6,8},{8,6},{10,12},{12,10},{14,16},{16,14},{1... | collective-permute-start | bytes 294920 | tf_op jit(solution)/shard_map/ppermute | solution.py:432
  17.5 18.4 %collective-permute-start.2 = (bf16[32,1536]{1,0:T(8,128)(2,1)}, bf16[32,1536]{1,0:T(8,128)(2,1)S(1)}, u32[]{:S(2)}, u32[]{:S(2)}) collective-permute-start(bf16[32,1536]{1,0:T(8,128)(2,1)} %refs_9_.1), channel_id=1, source_target_pairs={{0,2},{2,0},{4,6},{6,4},{8,10},{10,8},{12,14},{14,12},{16,18},{18,... | collective-permute-start | bytes 294920 | tf_op jit(solution)/shard_map/ppermute | solution.py:429
  21.5 20.2 %collective-permute-start.15 = (bf16[16,1536]{1,0:T(8,128)(2,1)S(1)}, bf16[16,1536]{1,0:T(8,128)(2,1)S(1)}, u32[]{:S(2)}, u32[]{:S(2)}) collective-permute-start(bf16[16,1536]{1,0:T(8,128)(2,1)S(1)} %get-tuple-element.74), channel_id=1, source_target_pairs={{0,254},{2,4},{4,2},{6,8},{8,6},{10,12},{12,10},{14,16},{16,14},{1... | collective-permute-start | bytes 147464 | tf_op jit(solution)/shard_map/ppermute | solution.py:432
  29.1 17.4 %collective-permute-start.10 = (bf16[32,1664]{1,0:T(8,128)(2,1)S(1)}, bf16[32,1664]{1,0:T(8,128)(2,1)S(1)}, u32[]{:S(2)}, u32[]{:S(2)}) collective-permute-start(bf16[32,1664]{1,0:T(8,128)(2,1)S(1)} %get-tuple-element.45), channel_id=1, source_target_pairs={{0,2},{2,0},{4,6},{6,4},{8,10},{10,8},{12,14},{14,12},{16,18},{18,... | collective-permute-start | bytes 319496 | tf_op jit(solution)/shard_map/ppermute | solution.py:429
  29.7 17.2 %collective-permute-start.11 = (bf16[32,1664]{1,0:T(8,128)(2,1)S(1)}, bf16[32,1664]{1,0:T(8,128)(2,1)S(1)}, u32[]{:S(2)}, u32[]{:S(2)}) collective-permute-start(bf16[32,1664]{1,0:T(8,128)(2,1)S(1)} %get-tuple-element.46), channel_id=1, source_target_pairs={{0,254},{2,4},{4,2},{6,8},{8,6},{10,12},{12,10},{14,16},{16,14},{1... | collective-permute-start | bytes 319496 | tf_op jit(solution)/shard_map/ppermute | solution.py:432
  38.7 23.5 %collective-permute-start.4 = (bf16[64,1536]{1,0:T(8,128)(2,1)S(1)}, bf16[64,1536]{1,0:T(8,128)(2,1)S(1)}, u32[]{:S(2)}, u32[]{:S(2)}) collective-permute-start(bf16[64,1536]{1,0:T(8,128)(2,1)S(1)} %get-tuple-element.41), channel_id=1, source_target_pairs={{0,2},{2,0},{4,6},{6,4},{8,10},{10,8},{12,14},{14,12},{16,18},{18,... | collective-permute-start | bytes 589832 | tf_op jit(solution)/shard_map/ppermute | solution.py:429
  38.8 23.4 %collective-permute-start.5 = (bf16[64,1536]{1,0:T(8,128)(2,1)S(1)}, bf16[64,1536]{1,0:T(8,128)(2,1)S(1)}, u32[]{:S(2)}, u32[]{:S(2)}) collective-permute-start(bf16[64,1536]{1,0:T(8,128)(2,1)S(1)} %get-tuple-element.42), channel_id=1, source_target_pairs={{0,254},{2,4},{4,2},{6,8},{8,6},{10,12},{12,10},{14,16},{16,14},{1... | collective-permute-start | bytes 589832 | tf_op jit(solution)/shard_map/ppermute | solution.py:432
  41.7 11.3 %collective-permute-start.7 = (bf16[32,1536]{1,0:T(8,128)(2,1)S(1)}, bf16[32,1536]{1,0:T(8,128)(2,1)S(1)}, u32[]{:S(2)}, u32[]{:S(2)}) collective-permute-start(bf16[32,1536]{1,0:T(8,128)(2,1)S(1)} %get-tuple-element.70), channel_id=1, source_target_pairs={{0,254},{2,4},{4,2},{6,8},{8,6},{10,12},{12,10},{14,16},{16,14},{1... | collective-permute-start | bytes 294920 | tf_op jit(solution)/shard_map/ppermute | solution.py:432
  46.5 5.8 %collective-permute-start.14 = (bf16[16,1536]{1,0:T(8,128)(2,1)S(1)}, bf16[16,1536]{1,0:T(8,128)(2,1)S(1)}, u32[]{:S(2)}, u32[]{:S(2)}) collective-permute-start(bf16[16,1536]{1,0:T(8,128)(2,1)S(1)} %get-tuple-element.75), channel_id=1, source_target_pairs={{0,2},{2,0},{4,6},{6,4},{8,10},{10,8},{12,14},{14,12},{16,18},{18,... | collective-permute-start | bytes 147464 | tf_op jit(solution)/shard_map/ppermute | solution.py:429
  46.9 10.6 %collective-permute-start.6 = (bf16[32,1536]{1,0:T(8,128)(2,1)S(1)}, bf16[32,1536]{1,0:T(8,128)(2,1)S(1)}, u32[]{:S(2)}, u32[]{:S(2)}) collective-permute-start(bf16[32,1536]{1,0:T(8,128)(2,1)S(1)} %get-tuple-element.71), channel_id=1, source_target_pairs={{0,2},{2,0},{4,6},{6,4},{8,10},{10,8},{12,14},{14,12},{16,18},{18,... | collective-permute-start | bytes 294920 | tf_op jit(solution)/shard_map/ppermute | solution.py:429
  52.3 5.6 %collective-permute-start.12 = (bf16[16,1536]{1,0:T(8,128)(2,1)S(1)}, bf16[16,1536]{1,0:T(8,128)(2,1)S(1)}, u32[]{:S(2)}, u32[]{:S(2)}) collective-permute-start(bf16[16,1536]{1,0:T(8,128)(2,1)S(1)} %get-tuple-element.48), channel_id=1, source_target_pairs={{0,2},{2,0},{4,6},{6,4},{8,10},{10,8},{12,14},{14,12},{16,18},{18,... | collective-permute-start | bytes 147464 | tf_op jit(solution)/shard_map/ppermute | solution.py:429
  53.0 9.2 %collective-permute-start.13 = (bf16[16,1536]{1,0:T(8,128)(2,1)S(1)}, bf16[16,1536]{1,0:T(8,128)(2,1)S(1)}, u32[]{:S(2)}, u32[]{:S(2)}) collective-permute-start(bf16[16,1536]{1,0:T(8,128)(2,1)S(1)} %get-tuple-element.49), channel_id=1, source_target_pairs={{0,254},{2,4},{4,2},{6,8},{8,6},{10,12},{12,10},{14,16},{16,14},{1... | collective-permute-start | bytes 147464 | tf_op jit(solution)/shard_map/ppermute | solution.py:432
  71.4 11.7 %collective-permute-start.23 = (f32[8,1536]{1,0:T(8,128)S(1)}, f32[8,1536]{1,0:T(8,128)S(1)}, u32[]{:S(2)}, u32[]{:S(2)}) collective-permute-start(f32[8,1536]{1,0:T(8,128)S(1)} %get-tuple-element.67), channel_id=1, source_target_pairs={{0,2},{2,0},{4,6},{6,4},{8,10},{10,8},{12,14},{14,12},{16,18},{18,... | collective-permute-start | bytes 147464 | tf_op jit(solution)/shard_map/ppermute | solution.py:517
  77.2 29.0 %collective-permute-start.21 = (bf16[64,1536]{1,0:T(8,128)(2,1)S(1)}, bf16[64,1536]{1,0:T(8,128)(2,1)S(1)}, u32[]{:S(2)}, u32[]{:S(2)}) collective-permute-start(bf16[64,1536]{1,0:T(8,128)(2,1)S(1)} %get-tuple-element.65), channel_id=1, source_target_pairs={{0,2},{2,0},{4,6},{6,4},{8,10},{10,8},{12,14},{14,12},{16,18},{18,... | collective-permute-start | bytes 589832 | tf_op jit(solution)/shard_map/ppermute | solution.py:429
  80.7 25.5 %collective-permute-start.22 = (bf16[64,1536]{1,0:T(8,128)(2,1)S(1)}, bf16[64,1536]{1,0:T(8,128)(2,1)S(1)}, u32[]{:S(2)}, u32[]{:S(2)}) collective-permute-start(bf16[64,1536]{1,0:T(8,128)(2,1)S(1)} %get-tuple-element.66), channel_id=1, source_target_pairs={{0,254},{2,4},{4,2},{6,8},{8,6},{10,12},{12,10},{14,16},{16,14},{1... | collective-permute-start | bytes 589832 | tf_op jit(solution)/shard_map/ppermute | solution.py:432
  83.2 10.7 %collective-permute-start.18 = (bf16[32,1664]{1,0:T(8,128)(2,1)S(1)}, bf16[32,1664]{1,0:T(8,128)(2,1)S(1)}, u32[]{:S(2)}, u32[]{:S(2)}) collective-permute-start(bf16[32,1664]{1,0:T(8,128)(2,1)S(1)} %get-tuple-element.57), channel_id=1, source_target_pairs={{0,254},{2,4},{4,2},{6,8},{8,6},{10,12},{12,10},{14,16},{16,14},{1... | collective-permute-start | bytes 319496 | tf_op jit(solution)/shard_map/ppermute | solution.py:432
  88.4 6.2 %collective-permute-start.17 = (bf16[32,1664]{1,0:T(8,128)(2,1)S(1)}, bf16[32,1664]{1,0:T(8,128)(2,1)S(1)}, u32[]{:S(2)}, u32[]{:S(2)}) collective-permute-start(bf16[32,1664]{1,0:T(8,128)(2,1)S(1)} %get-tuple-element.57), channel_id=1, source_target_pairs={{0,2},{2,0},{4,6},{6,4},{8,10},{10,8},{12,14},{14,12},{16,18},{18,... | collective-permute-start | bytes 319496 | tf_op jit(solution)/shard_map/ppermute | solution.py:429
  93.6 11.9 %collective-permute-start.26 = (f32[8,1536]{1,0:T(8,128)S(1)}, f32[8,1536]{1,0:T(8,128)S(1)}, u32[]{:S(2)}, u32[]{:S(2)}) collective-permute-start(f32[8,1536]{1,0:T(8,128)S(1)} %add.59), channel_id=1, source_target_pairs={{0,28},{2,30},{4,24},{6,26},{8,20},{10,22},{12,16},{14,18},{16,12}... | collective-permute-start | bytes 147464 | tf_op jit(solution)/shard_map/ppermute | solution.py:517
  100.6 12.4 %collective-permute-start.19 = (bf16[32,1536]{1,0:T(8,128)(2,1)S(1)}, bf16[32,1536]{1,0:T(8,128)(2,1)S(1)}, u32[]{:S(2)}, u32[]{:S(2)}) collective-permute-start(bf16[32,1536]{1,0:T(8,128)(2,1)S(1)} %get-tuple-element.62), channel_id=1, source_target_pairs={{0,2},{2,0},{4,6},{6,4},{8,10},{10,8},{12,14},{14,12},{16,18},{18,... | collective-permute-start | bytes 294920 | tf_op jit(solution)/shard_map/ppermute | solution.py:429
  103.4 9.8 %collective-permute-start.20 = (bf16[32,1536]{1,0:T(8,128)(2,1)S(1)}, bf16[32,1536]{1,0:T(8,128)(2,1)S(1)}, u32[]{:S(2)}, u32[]{:S(2)}) collective-permute-start(bf16[32,1536]{1,0:T(8,128)(2,1)S(1)} %get-tuple-element.63), channel_id=1, source_target_pairs={{0,254},{2,4},{4,2},{6,8},{8,6},{10,12},{12,10},{14,16},{16,14},{1... | collective-permute-start | bytes 294920 | tf_op jit(solution)/shard_map/ppermute | solution.py:432
  (24 other events, 190.3 us)

commit v2 on v1

v2 whole, which is shorter than its diff:
```python
import jax
import jax.numpy as jnp
from jax import lax
from jax.experimental import pallas as pl
from jax.experimental.pallas import tpu as pltpu
from jax.sharding import PartitionSpec as P

HEAD_DIM = 128
STRIDE = 32
NEGATIVE = -1e30
EPSILON = 1e-06
FACTOR = HEAD_DIM ** (-0.5)
BLOCKS = ("video", "audio")
BF = jnp.bfloat16
F32 = jnp.float32
PAD = 128


def dot(a, b, over_a, over_b):
    return lax.dot_general(
        a, b, (((over_a,), (over_b,)), ((), ())), preferred_element_type=F32
    )


def call(kernel, outs, args, scalars, micros, scratch=()):
    vmem = pl.BlockSpec(memory_space=pltpu.VMEM)
    smem = pl.BlockSpec(memory_space=pltpu.SMEM)
    size = sum(a.size * a.dtype.itemsize for a in args)
    return pl.pallas_call(
        kernel,
        out_shape=[jax.ShapeDtypeStruct(s, d) for s, d in outs],
        in_specs=[smem] * len(scalars) + [vmem] * len(args),
        out_specs=[vmem] * len(outs),
        scratch_shapes=list(scratch),
        compiler_params=pltpu.CompilerParams(vmem_limit_bytes=48 * 1024 * 1024),
        cost_estimate=pl.CostEstimate(
            flops=int(micros * 1.1e9), bytes_accessed=size, transcendentals=0
        ),
    )(*scalars, *args)


def other(i, count):
    return (i + 2 * (i & 1) - 1 + count) & (count - 1)


def columns(h):
    return slice(h * HEAD_DIM, (h + 1) * HEAD_DIM)


def pack_stats(tile):
    high = tile.astype(BF).astype(F32)
    rest = tile - high
    middle = rest.astype(BF).astype(F32)
    low = rest - middle
    return (high + pltpu.roll(middle, 16, 1) + pltpu.roll(low, 32, 1)).astype(BF)


def unpack_stats(packed):
    wide = packed.astype(F32)
    return wide + (pltpu.roll(wide, PAD - 16, 1) + pltpu.roll(wide, PAD - 32, 1))


def audio_bias(i, count, window, valid, rows_q, rows_k):
    row = lax.broadcasted_iota(jnp.int32, (rows_k, 4 * rows_q), 0)
    slot = lax.broadcasted_iota(jnp.int32, (rows_k, 4 * rows_q), 1) // rows_q
    position = i * rows_k + row
    blocks = (i, i ^ 1, other(i, count))
    lower, upper = [
        jnp.where(
            slot == 0,
            window[blocks[0], side],
            jnp.where(slot == 1, window[blocks[1], side], window[blocks[2], side]),
        )
        for side in (0, 1)
    ]
    seen = (position >= lower) & (position < upper) & (row < valid[i]) & (slot < 3)
    return jnp.where(seen, 0.0, NEGATIVE)


def padded(own, e, o, c):
    return jnp.concatenate(
        [own[:, c], e[:, c], o[:, c], jnp.zeros((own.shape[0], HEAD_DIM), BF)], 0
    )


def video_bias(i, count, window, valid, rows_q, rows_k):
    row = lax.broadcasted_iota(jnp.int32, (rows_k, rows_q), 0)
    parts = []
    for c in (i, i ^ 1, other(i, count)):
        position = c * rows_k + row
        seen = (position >= window[i, 0]) & (position < window[i, 1]) & (row < valid[c])
        parts.append(jnp.where(seen, 0.0, NEGATIVE))
    return jnp.concatenate(parts, 0)


def audio_forward(
    count, idx, window, valid, q, qe, qo, k, v, send_e, send_o, own, own_lse, rows_lse
):
    rows = q.shape[0]
    heads = q.shape[1] // HEAD_DIM
    bias = audio_bias(idx[0], count, window, valid, rows, k.shape[0])
    rows_lse[...] = jnp.zeros(rows_lse.shape, F32)
    for h in range(heads):
        c = columns(h)
        scores = dot(k[:, c], padded(q, qe, qo, c), 1, 1) * FACTOR + bias
        peak = jnp.max(scores, 0, keepdims=True)
        weight = jnp.exp(scores - peak)
        total = jnp.sum(weight, 0, keepdims=True)
        part = dot((weight * (1.0 / total)).astype(BF), v[:, c], 0, 0)
        rows_lse[h : h + 1, :] = peak + jnp.log(total)
        own[:, c] = part[:rows]
        send_e[:, c] = part[rows : 2 * rows].astype(BF)
        send_o[:, c] = part[2 * rows : 3 * rows].astype(BF)
    tile = jnp.transpose(rows_lse[...])
    own_lse[...] = tile[:rows]
    tail = slice(heads * HEAD_DIM, heads * HEAD_DIM + PAD)
    send_e[:, tail] = pack_stats(tile[rows : 2 * rows])
    send_o[:, tail] = pack_stats(tile[2 * rows : 3 * rows])


def near_columns(own, e, o, c, part):
    rows = own.shape[0]
    s = slice(part * rows, (part + 1) * rows)
    return jnp.concatenate([own[:, c], e[s, c], o[s, c]], 0)


def video_forward(
    count, idx, window, valid, q, k, v, kve, kvo, att, lse, send_e, send_o
):
    rows = q.shape[0]
    heads = q.shape[1] // HEAD_DIM
    i = idx[0]
    bias = video_bias(i, count, window, valid, rows, k.shape[0])
    lse[...] = jnp.zeros(lse.shape, F32)
    for h in range(heads):
        c = columns(h)
        keys = near_columns(k, kve, kvo, c, 0)
        values = near_columns(v, kve, kvo, c, 1)
        scores = dot(keys, q[:, c], 1, 1) * FACTOR + bias
        peak = jnp.max(scores, 0, keepdims=True)
        weight = jnp.exp(scores - peak)
        total = jnp.sum(weight, 0, keepdims=True)
        prob = (weight * (1.0 / total)).astype(BF)
        att[:, c] = dot(prob, values, 0, 0).astype(BF)
        lse[h : h + 1, :] = peak + jnp.log(total)
    odd = i & 1
    for send, side in ((send_e, 1 - odd), (send_o, odd)):
        start = pl.multiple_of(side * (rows - STRIDE), STRIDE)
        send[...] = att[pl.ds(start, STRIDE), :]


def audio_combine(idx, own, own_lse, re, ro, cot, att, total, send_e, send_o):
    rows = own.shape[0]
    heads = own.shape[1] // HEAD_DIM
    tail = slice(heads * HEAD_DIM, heads * HEAD_DIM + PAD)
    mine = own_lse[...]
    first = unpack_stats(re[:, tail])
    second = unpack_stats(ro[:, tail])
    peak = jnp.maximum(mine, jnp.maximum(first, second))
    whole = peak + jnp.log(
        jnp.exp(mine - peak) + jnp.exp(first - peak) + jnp.exp(second - peak)
    )
    total[...] = whole
    wm, we, wo = jnp.exp(mine - whole), jnp.exp(first - whole), jnp.exp(second - whole)
    odd = (idx[0] & 1) == 1
    for h in range(heads):
        c = columns(h)
        joined = (
            own[:, c] * wm[:, h : h + 1]
            + re[:, c].astype(F32) * we[:, h : h + 1]
            + ro[:, c].astype(F32) * wo[:, h : h + 1]
        )
        att[:, c] = joined.astype(BF)
        incoming = cot[:, c].astype(F32)
        low = jnp.concatenate([joined[0:8], incoming[0:8]], 0)
        high = jnp.concatenate([joined[rows - 8 :], incoming[rows - 8 :]], 0)
        send_e[:, c] = jnp.where(odd, low, high).astype(BF)
        send_o[:, c] = jnp.where(odd, high, low).astype(BF)


class Mix:
    def __init__(self, count, idx, refs):
        self.i = idx[0]
        self.even = (self.i & 1) == 0
        self.has_prev = (self.i > 0).astype(F32)
        self.has_next = (self.i < count - 1).astype(F32)
        (self.att_v, self.hve, self.hvo, self.cot_v,
         self.att_a, self.hae, self.hao, self.cot_a,
         self.conv_v, self.conv_a, self.gain_v, self.gain_a) = refs
        self.chunks = self.att_v.shape[0] // STRIDE

    def before(self, e, o):
        return jnp.where(self.even, o.astype(F32), e.astype(F32)) * self.has_prev

    def after(self, e, o):
        return jnp.where(self.even, e.astype(F32), o.astype(F32)) * self.has_next

    def video_att(self, g, c):
        if g < 0:
            return self.before(self.hve[:, c], self.hvo[:, c])
        if g >= self.chunks:
            return self.after(self.hve[:, c], self.hvo[:, c])
        return self.att_v[g * STRIDE : (g + 1) * STRIDE, c].astype(F32)

    def video_cot(self, g, c):
        return self.cot_v[g * STRIDE : (g + 1) * STRIDE, c].astype(F32)

    def extended(self, own, c, part):
        s = slice(8 * part, 8 * part + 8)
        low = self.before(self.hae[:, c], self.hao[:, c])[s]
        high = self.after(self.hae[:, c], self.hao[:, c])[s]
        return jnp.concatenate([low, own[:, c].astype(F32), high], 0)

    def audio(self, c):
        att = self.extended(self.att_a, c, 0)
        rows = att.shape[0]
        early = pltpu.roll(att, 1, 0)
        late = pltpu.roll(att, rows - 1, 0)
        taps = self.conv_a
        mixed = taps[0:1, c] * early + taps[1:2, c] * att + taps[2:3, c] * late
        cot = self.extended(self.cot_a, c, 1)
        return mixed, cot, early, att, late


def row_sums(count, idx, *refs):
    mix = Mix(count, idx, refs[:-1])
    stats = refs[-1]
    heads = mix.att_v.shape[1] // HEAD_DIM
    rows_a = mix.att_a.shape[0] + 16
    lane = lax.broadcasted_iota(jnp.int32, (STRIDE, PAD), 1)
    tile = jnp.zeros((STRIDE, PAD), F32)
    taps = mix.conv_v
    for g in range(mix.chunks):
        square = jnp.zeros((STRIDE, HEAD_DIM), F32)
        inner = jnp.zeros((STRIDE, HEAD_DIM), F32)
        for h in range(heads):
            c = columns(h)
            mixed = (
                taps[0:1, c] * mix.video_att(g - 1, c)
                + taps[1:2, c] * mix.video_att(g, c)
                + taps[2:3, c] * mix.video_att(g + 1, c)
            )
            square += mixed * mixed
            inner += mix.video_cot(g, c) * mix.gain_v[0:1, c] * mixed
        tile = jnp.where(lane == g, jnp.sum(square, 1, keepdims=True), tile)
        tile = jnp.where(lane == g + 16, jnp.sum(inner, 1, keepdims=True), tile)
    lane_a = lax.broadcasted_iota(jnp.int32, (rows_a, PAD), 1)
    square = jnp.zeros((rows_a, HEAD_DIM), F32)
    inner = jnp.zeros((rows_a, HEAD_DIM), F32)
    for h in range(heads):
        c = columns(h)
        mixed, cot, _, _, _ = mix.audio(c)
        square += mixed * mixed
        inner += cot * mix.gain_a[0:1, c] * mixed
    tile_a = jnp.where(
        lane_a == 0,
        jnp.sum(square, 1, keepdims=True),
        jnp.where(lane_a == 1, jnp.sum(inner, 1, keepdims=True), 0.0),
    )
    stats[0:STRIDE, :] = tile
    stats[STRIDE:, :] = tile_a


def norm_backward(count, width, idx, *refs):
    mix = Mix(count, idx, refs[2:14])
    mine, theirs = refs[0], refs[1]
    total_a = refs[14]
    out_v, grad_v, out_a, up_a, send_e, send_o, dots_a, parts = refs[15:23]
    scale_ref, shrink_ref = refs[23:25]
    heads = mix.att_v.shape[1] // HEAD_DIM
    sums = mine[...] + theirs[...]
    rows_a = mix.att_a.shape[0]
    ext = rows_a + 16
    for g in range(mix.chunks):
        inverse = lax.rsqrt(sums[0:STRIDE, g : g + 1] / width + EPSILON)
        inner = sums[0:STRIDE, g + 16 : g + 17]
        s = slice(g * STRIDE, (g + 1) * STRIDE)
        scale_ref[s, :] = jnp.broadcast_to(inverse, (STRIDE, HEAD_DIM))
        shrink_ref[s, :] = jnp.broadcast_to(
            inverse * inverse * inverse * inner / width, (STRIDE, HEAD_DIM)
        )
    row = lax.broadcasted_iota(jnp.int32, (ext, HEAD_DIM), 0)
    present = jnp.where(row < 8, mix.has_prev, jnp.where(row >= rows_a + 8, mix.has_next, 1.0))
    inverse = lax.rsqrt(sums[STRIDE:, 0:1] / width + EPSILON)
    scale_a = jnp.broadcast_to(inverse, (ext, HEAD_DIM)) * present
    shrink_a = (
        jnp.broadcast_to(
            inverse * inverse * inverse * sums[STRIDE:, 1:2] / width, (ext, HEAD_DIM)
        )
        * present
    )
    lane = lax.broadcasted_iota(jnp.int32, (rows_a, PAD), 1)
    dots = jnp.zeros((rows_a, PAD), F32)
    own = slice(8, 8 + rows_a)
    for h in range(heads):
        c = columns(h)
        taps = [mix.conv_v[k : k + 1, c] for k in range(3)]
        gain = mix.gain_v[0:1, c]
        sum_taps = [jnp.zeros((STRIDE, HEAD_DIM), F32) for _ in range(3)]
        sum_gain = jnp.zeros((STRIDE, HEAD_DIM), F32)
        atts = [mix.video_att(g, c) for g in (-1, 0, 1)]
        for g in range(mix.chunks):
            mixed = taps[0] * atts[0] + taps[1] * atts[1] + taps[2] * atts[2]
            s = slice(g * STRIDE, (g + 1) * STRIDE)
            scale = scale_ref[s, :]
            incoming = mix.video_cot(g, c)
            grad = scale * (incoming * gain) - mixed * shrink_ref[s, :]
            normed = mixed * scale
            out_v[s, c] = (normed * gain).astype(BF)
            grad_v[s, c] = grad
            sum_gain += incoming * normed
            for k in range(3):
                sum_taps[k] += grad * atts[k]
            if g + 1 < mix.chunks:
                atts = atts[1:] + [mix.video_att(g + 2, c)]
        for k in range(3):
            parts[k : k + 1, c] = jnp.sum(sum_taps[k], 0, keepdims=True)
        parts[3:4, c] = jnp.sum(sum_gain, 0, keepdims=True)

        mixed, cot, early, att, late = mix.audio(c)
        gain = mix.gain_a[0:1, c]
        taps = [mix.conv_a[k : k + 1, c] for k in range(3)]
        normed = mixed * scale_a
        grad = scale_a * (cot * gain) - mixed * shrink_a
        out_a[:, c] = (normed * gain)[own].astype(BF)
        upstream = (
            taps[0] * pltpu.roll(grad, ext - 1, 0)
            + taps[1] * grad
            + taps[2] * pltpu.roll(grad, 1, 0)
        )[own].astype(BF)
        up_a[:, c] = upstream
        send_e[0:rows_a, c] = upstream
        send_o[0:rows_a, c] = upstream
        row_dot = jnp.sum(upstream.astype(F32) * att[own], 1, keepdims=True)
        dots = jnp.where(lane == h, row_dot, dots)
        for k, shifted in enumerate((early, att, late)):
            parts[4 + k : 5 + k, c] = jnp.sum((grad * shifted)[own], 0, keepdims=True)
        parts[7:8, c] = jnp.sum((cot * normed)[own], 0, keepdims=True)
    dots_a[...] = dots
    tail = slice(heads * HEAD_DIM, heads * HEAD_DIM + PAD)
    packed = pack_stats(jnp.where(lane < heads, total_a[...], 0.0)).astype(F32)
    packed_dots = pack_stats(dots).astype(F32)
    packed = (packed + pltpu.roll(packed_dots, 64, 1)).astype(BF)
    odd = idx[0] & 1
    body = slice(0, heads * HEAD_DIM)
    for send, side in ((send_e, 1 - odd), (send_o, odd)):
        start = pl.multiple_of(side * (mix.att_v.shape[0] - STRIDE), STRIDE)
        send[0:rows_a, tail] = packed
        send[rows_a:, body] = grad_v[pl.ds(start, STRIDE), :].astype(BF)
        send[rows_a:, tail] = jnp.zeros((STRIDE, PAD), BF)


def video_backward(
    count, idx, window, valid, q, grad, re, ro, conv, lse, k, v, kve, kvo,
    dq, own, send_e, send_o,
):
    rows = q.shape[0]
    heads = q.shape[1] // HEAD_DIM
    near = k.shape[0]
    i = idx[0]
    even = (i & 1) == 0
    has_prev = (i > 0).astype(F32)
    has_next = (i < count - 1).astype(F32)
    bias = video_bias(i, count, window, valid, rows, near)
    halo = slice(near, near + STRIDE)
    for h in range(heads):
        c = columns(h)
        keys = near_columns(k, kve, kvo, c, 0)
        values = near_columns(v, kve, kvo, c, 1)
        queries = q[:, c]
        first, second = re[halo, c].astype(F32), ro[halo, c].astype(F32)
        before = jnp.where(even, second, first) * has_prev
        after = jnp.where(even, first, second) * has_next
        own_grad = grad[:, c]
        wide = jnp.concatenate([before, own_grad, after], 0)
        upstream = (
            conv[0:1, c] * wide[2 * STRIDE :]
            + conv[1:2, c] * own_grad
            + conv[2:3, c] * wide[0:rows]
        ).astype(BF)
        scores = dot(keys, queries, 1, 1) * FACTOR + bias
        prob = jnp.exp(scores - lse[h : h + 1, :])
        prob_grad = dot(values, upstream, 1, 1)
        row_dot = jnp.sum(prob * prob_grad, 0, keepdims=True)
        score_grad = (prob * (prob_grad - row_dot)).astype(BF)
        dq[:, c] = (dot(score_grad, keys, 0, 0) * FACTOR).astype(BF)
        dk = dot(score_grad, queries, 1, 0) * FACTOR
        dv = dot(prob.astype(BF), upstream, 1, 0)
        for part, value in enumerate((dk, dv)):
            s = slice(part * near, (part + 1) * near)
            own[s, c] = value[0:near]
            send_e[s, c] = value[near : 2 * near].astype(BF)
            send_o[s, c] = value[2 * near :].astype(BF)


def audio_backward(
    count, idx, window, valid, q, qe, qo, up, re, ro, total, dots, k, v, part_e, part_o,
    dk, dv, own, send_e, send_o,
):
    rows = q.shape[0]
    heads = q.shape[1] // HEAD_DIM
    tail = slice(heads * HEAD_DIM, heads * HEAD_DIM + PAD)
    bias = audio_bias(idx[0], count, window, valid, rows, k.shape[0])
    totals, row_dots = [total[...]], [dots[...]]
    for r in (re, ro):
        wide = unpack_stats(r[0:rows, tail])
        totals.append(wide)
        row_dots.append(pltpu.roll(wide, 64, 1))
    blank = jnp.zeros((PAD - 3 * rows, PAD), F32)
    totals = jnp.transpose(jnp.concatenate(totals + [blank], 0))
    row_dots = jnp.transpose(jnp.concatenate(row_dots + [blank], 0))
    up_e, up_o = re.at[0:rows], ro.at[0:rows]
    done = slice(0, 2 * rows)
    send_e[done, :] = part_e[...]
    send_o[done, :] = part_o[...]
    for h in range(heads):
        c = columns(h)
        queries = padded(q, qe, qo, c)
        upstream = padded(up, up_e, up_o, c)
        keys, values = k[:, c], v[:, c]
        scores = dot(keys, queries, 1, 1) * FACTOR + bias
        prob = jnp.exp(scores - totals[h : h + 1, :])
        prob_grad = dot(values, upstream, 1, 1)
        score_grad = (prob * (prob_grad - row_dots[h : h + 1, :])).astype(BF)
        dq = dot(score_grad, keys, 0, 0) * FACTOR
        dk[:, c] = (dot(score_grad, queries, 1, 0) * FACTOR).astype(BF)
        dv[:, c] = dot(prob.astype(BF), upstream, 1, 0).astype(BF)
        own[:, c] = dq[:rows]
        send_e[2 * rows :, c] = dq[rows : 2 * rows].astype(BF)
        send_o[2 * rows :, c] = dq[2 * rows : 3 * rows].astype(BF)


def per_device(
    query_video,
    key_video,
    value_video,
    query_audio,
    key_audio,
    value_audio,
    conv_video,
    conv_audio,
    gain_video,
    gain_audio,
    video_window,
    audio_window,
    video_valid,
    audio_valid,
    cotangent_video,
    cotangent_audio,
):
    count = video_window.shape[0]
    block = lax.axis_index(BLOCKS)
    idx = block.astype(jnp.int32).reshape(1)
    rows_v, wide = query_video.shape
    rows_a = query_audio.shape[0]
    heads = wide // HEAD_DIM
    model = wide * lax.axis_size("tp")
    even_route = [(i, i ^ 1) for i in range(count)]
    odd_route = [(i, other(i, count)) for i in range(count)]

    def swap_e(x):
        return lax.ppermute(x, BLOCKS, even_route)

    def swap_o(x):
        return lax.ppermute(x, BLOCKS, odd_route)

    def bind(f, *extra):
        def kernel(*refs):
            return f(*extra, *refs)

        return kernel

    qe, qo = swap_e(query_audio), swap_o(query_audio)
    both = jnp.concatenate([key_audio, value_audio], 0)
    kve, kvo = swap_e(both), swap_o(both)

    packed = ((rows_a, wide + PAD), BF)
    audio_info = (idx, audio_window, video_valid)
    video_info = (idx, video_window, audio_valid)
    send_e, send_o, own_part, own_lse = call(
        bind(audio_forward, count),
        [packed, packed, ((rows_a, wide), F32), ((rows_a, PAD), F32)],
        [query_audio, qe, qo, key_video, value_video],
        audio_info,
        3.0,
        [pltpu.VMEM((PAD, PAD), F32)],
    )
    kve, kvo, own_lse = lax.optimization_barrier((kve, kvo, own_lse))
    pe, po = swap_e(send_e), swap_o(send_o)
    keys_values = [key_audio, value_audio, kve, kvo]
    halo = ((STRIDE, wide), BF)
    att_v, lse_v, hv_e, hv_o = call(
        bind(video_forward, count),
        [((rows_v, wide), BF), (((heads + 7) // 8 * 8, rows_v), F32), halo, halo],
        [query_video] + keys_values,
        video_info,
        2.8,
    )
    hve, hvo = swap_e(hv_e), swap_o(hv_o)
    halo_a = ((16, wide), BF)
    att_a, total_a, ha_e, ha_o = call(
        audio_combine,
        [((rows_a, wide), BF), ((rows_a, PAD), F32), halo_a, halo_a],
        [own_part, own_lse, pe, po, cotangent_audio],
        (idx,),
        0.5,
    )
    hae, hao = swap_e(ha_e), swap_o(ha_o)

    mix_args = [
        att_v, hve, hvo, cotangent_video,
        att_a, hae, hao, cotangent_audio,
        conv_video, conv_audio, gain_video.reshape(1, wide), gain_audio.reshape(1, wide),
    ]
    stats_rows = STRIDE + rows_a + 16
    (stats,) = call(
        bind(row_sums, count), [((stats_rows, PAD), F32)], mix_args, (idx,), 1.3
    )
    tp_size = lax.axis_size("tp")
    stats_other = lax.ppermute(stats, "tp", [(i, i ^ 1) for i in range(tp_size)])
    chunks = rows_v // STRIDE
    both = ((rows_a + STRIDE, wide + PAD), BF)
    out_v, grad_v, out_a, up_a, back_e, back_o, dots_a, parts = call(
        bind(norm_backward, count, model),
        [
            ((rows_v, wide), BF),
            ((rows_v, wide), F32),
            ((rows_a, wide), BF),
            ((rows_a, wide), BF),
            both,
            both,
            ((rows_a, PAD), F32),
            ((8, wide), F32),
        ],
        [stats, stats_other] + mix_args + [total_a],
        (idx,),
        3.0,
        [pltpu.VMEM((rows_v, HEAD_DIM), F32)] * 2,
    )
    re, ro = swap_e(back_e), swap_o(back_o)
    total = parts
    for bits in (16, 32, 2, 1, 96, 4, 14):
        total = total + lax.ppermute(total, BLOCKS, [(i, i ^ bits) for i in range(count)])

    two = ((2 * rows_a, wide), BF)
    dq_v, dkv_own, dkv_e, dkv_o = call(
        bind(video_backward, count),
        [((rows_v, wide), BF), ((2 * rows_a, wide), F32), two, two],
        [query_video, grad_v, re, ro, conv_video, lse_v] + keys_values,
        video_info,
        5.0,
    )
    three = ((3 * rows_a, wide), BF)
    dk_v, dv_v, dq_own, give_e, give_o = call(
        bind(audio_backward, count),
        [((rows_v, wide), BF), ((rows_v, wide), BF), ((rows_a, wide), F32), three, three],
        [query_audio, qe, qo, up_a, re, ro, total_a, dots_a, key_video, value_video,
         dkv_e, dkv_o],
        audio_info,
        5.0,
    )
    got_e, got_o = swap_e(give_e), swap_o(give_o)
    own = jnp.concatenate([dkv_own, dq_own], 0)
    grads = (own + got_e.astype(F32) + got_o.astype(F32)).astype(BF)
    return (
        out_v,
        out_a,
        dq_v,
        dk_v,
        dv_v,
        grads[2 * rows_a :],
        grads[:rows_a],
        grads[rows_a : 2 * rows_a],
        total[0:3],
        total[4:7],
        total[3],
        total[7],
    )


def solution(mesh):
    rows = P(BLOCKS, "tp")
    in_specs = (rows,) * 6 + (P(None, "tp"),) * 2 + (P("tp"),) * 2 + (P(),) * 4 + (rows,) * 2
    out_specs = (rows,) * 8 + (P(None, "tp"),) * 2 + (P("tp"),) * 2
    return jax.shard_map(
        per_device, mesh=mesh, in_specs=in_specs, out_specs=out_specs, check_vma=False
    )
```

time: 118 us -> 112 us (0.949)
  the two profiles are of different devices: /device:TPU:2 before, /device:TPU:1 now
where the time goes in v2:
time: 112 us
  starting transfers between devices  47.4 us (42%)
  waiting for transfers between devices  32.2 us (29%)
  Pallas kernels  21.7 us (19%)
  local copies, waits for them, and re-layouts  9.23 us (8%)
    ppermute x7, starting transfers between devices, swap_o(): return lax.ppermute(x, BLOCKS, odd_route)  30.2 us
    pallas_call x7, Pallas kernels, call(): pl.pallas_call(kernel, out_shape=[jax.ShapeDtypeStruct(s, d) for s, d in...  21.7 us
    ppermute x7, waiting for transfers between devices, per_device(): lax.ppermute(total, BLOCKS, [(i, i ^ bits) for i in range(count)])  13.6 us
    ppermute x7, starting transfers between devices, per_device(): lax.ppermute(total, BLOCKS, [(i, i ^ bits) for i in range(count)])  11.9 us
    ppermute x7, waiting for transfers between devices, swap_o(): return lax.ppermute(x, BLOCKS, odd_route)  8.32 us
    ppermute x7, waiting for transfers between devices, swap_e(): return lax.ppermute(x, BLOCKS, even_route)  8.24 us
    unnamed x39, local copies, waits for them, and re-layouts  6.35 us
    ppermute x7, starting transfers between devices, swap_e(): return lax.ppermute(x, BLOCKS, even_route)  4.16 us
  transfers between devices with their start and end apart: 22, of which 10 were waited for; matrix products, arithmetic and copies ran while one was open for 4% of the time, Pallas kernels for 16%

profile of v2, /device:TPU:1, one launch (start us, length us, event | category | flops | bytes accessed | tf_op | source)
XLA Modules:
  0.0 111.7 jit_solution(12699882963126907813)
XLA Ops:
  0.6 3.7 %collective-permute-start.2 = (bf16[32,1536]{1,0:T(8,128)(2,1)}, bf16[32,1536]{1,0:T(8,128)(2,1)S(1)}, u32[]{:S(2)}, u32[]{:S(2)}) collective-permute-start(bf16[32,1536]{1,0:T(8,128)(2,1)} %refs_3_.7), channel_id=1, source_target_pairs={{0,2},{2,0},{4,6},{6,4},{8,10},{10,8},{12,14},{14,12},{16,18},{18,... | collective-permute-start | bytes 294920 | tf_op jit(solution)/shard_map/ppermute | solution.py:462
  4.3 6.4 %collective-permute-start.3 = (bf16[32,1536]{1,0:T(8,128)(2,1)}, bf16[32,1536]{1,0:T(8,128)(2,1)S(1)}, u32[]{:S(2)}, u32[]{:S(2)}) collective-permute-start(bf16[32,1536]{1,0:T(8,128)(2,1)} %refs_3_.7), channel_id=1, source_target_pairs={{0,254},{2,4},{4,2},{6,8},{8,6},{10,12},{12,10},{14,16},{16,14},{1... | collective-permute-start | bytes 294920 | tf_op jit(solution)/shard_map/ppermute | solution.py:465
  12.5 4.0 %collective-permute-start.1 = (bf16[64,1536]{1,0:T(8,128)(2,1)S(1)}, bf16[64,1536]{1,0:T(8,128)(2,1)S(1)}, u32[]{:S(2)}, u32[]{:S(2)}) collective-permute-start(bf16[64,1536]{1,0:T(8,128)(2,1)S(1)} %constant_dynamic-update-slice_fusion), channel_id=1, source_target_pairs={{0,254},{2,4},{4,2},{6,8},{8,6},{10,12},{12,10},{14,16},{16,14},{1... | collective-permute-start | bytes 589832 | tf_op jit(solution)/shard_map/ppermute | solution.py:465
  21.9 2.8 %shard_map.247 = (bf16[32,1664]{1,0:T(8,128)(2,1)S(1)}, bf16[32,1664]{1,0:T(8,128)(2,1)S(1)}, f32[32,1536]{1,0:T(8,128)S(1)}, f32[32,128]{1,0:T(8,128)S(1)}) custom-call(s32[1]{0:T(128)} %bitcast.refs_0_.idx, s32[128,2]{1,0:T(8,128)S(1)} %copy.28.refs_1_, s32[128]{0:T(128)S(1)} %copy-done.14, bf16[32,1536]{1,0:T(8,128)(2,1)S(1)} %copy-done.9, ...), custom_call_target="tpu_custom_call" | custom-call | flops 3300000000 | bytes 1867776 | tf_op jit(solution)/shard_map/pallas_call | solution.py:29
  24.7 4.0 %collective-permute-start.7 = (bf16[32,1664]{1,0:T(8,128)(2,1)S(1)}, bf16[32,1664]{1,0:T(8,128)(2,1)S(1)}, u32[]{:S(2)}, u32[]{:S(2)}) collective-permute-start(bf16[32,1664]{1,0:T(8,128)(2,1)S(1)} %get-tuple-element.53), channel_id=1, source_target_pairs={{0,254},{2,4},{4,2},{6,8},{8,6},{10,12},{12,10},{14,16},{16,14},{1... | collective-permute-start | bytes 319496 | tf_op jit(solution)/shard_map/ppermute | solution.py:465
  28.8 2.7 %shard_map.248 = (bf16[256,1536]{1,0:T(8,128)(2,1)S(1)}, f32[16,256]{1,0:T(8,128)S(1)}, bf16[32,1536]{1,0:T(8,128)(2,1)S(1)}, bf16[32,1536]{1,0:T(8,128)(2,1)S(1)}) custom-call(s32[1]{0:T(128)} %bitcast.refs_0_.idx, s32[128,2]{1,0:T(8,128)S(1)} %copy.29.refs_1_, s32[128]{0:T(128)S(1)} %copy-done.13, bf16[256,1536]{1,0:T(8,128)(2,1)S(1)} %copy-done.3, ...), custom_call_target="tpu_custom_call" | custom-call | flops 3080000000 | bytes 1376256 | tf_op jit(solution)/shard_map/pallas_call | solution.py:29
  31.6 4.0 %collective-permute-start.5 = (bf16[32,1536]{1,0:T(8,128)(2,1)S(1)}, bf16[32,1536]{1,0:T(8,128)(2,1)S(1)}, u32[]{:S(2)}, u32[]{:S(2)}) collective-permute-start(bf16[32,1536]{1,0:T(8,128)(2,1)S(1)} %get-tuple-element.49), channel_id=1, source_target_pairs={{0,254},{2,4},{4,2},{6,8},{8,6},{10,12},{12,10},{14,16},{16,14},{1... | collective-permute-start | bytes 294920 | tf_op jit(solution)/shard_map/ppermute | solution.py:465
  36.3 3.4 %collective-permute-start.9 = (bf16[16,1536]{1,0:T(8,128)(2,1)S(1)}, bf16[16,1536]{1,0:T(8,128)(2,1)S(1)}, u32[]{:S(2)}, u32[]{:S(2)}) collective-permute-start(bf16[16,1536]{1,0:T(8,128)(2,1)S(1)} %get-tuple-element.56), channel_id=1, source_target_pairs={{0,254},{2,4},{4,2},{6,8},{8,6},{10,12},{12,10},{14,16},{16,14},{1... | collective-permute-start | bytes 147464 | tf_op jit(solution)/shard_map/ppermute | solution.py:465
  39.7 2.0 %collective-permute-done.8.refs_6_.refs_8_ = bf16[16,1536]{1,0:T(8,128)(2,1)S(1)} collective-permute-done((bf16[16,1536]{1,0:T(8,128)(2,1)S(1)}, bf16[16,1536]{1,0:T(8,128)(2,1)S(1)}, u32[]{:S(2)}, u32[]{:S(2)}) %collective-permute-start.8) | collective-permute-done | bytes 49184 | tf_op jit(solution)/shard_map/ppermute | solution.py:462
  41.7 1.7 %collective-permute-done.9.refs_7_.refs_9_ = bf16[16,1536]{1,0:T(8,128)(2,1)S(1)} collective-permute-done((bf16[16,1536]{1,0:T(8,128)(2,1)S(1)}, bf16[16,1536]{1,0:T(8,128)(2,1)S(1)}, u32[]{:S(2)}, u32[]{:S(2)}) %collective-permute-start.9) | collective-permute-done | bytes 49184 | tf_op jit(solution)/shard_map/ppermute | solution.py:465
  45.6 2.1 %collective-permute-done.10.refs_2_ = f32[80,128]{1,0:T(8,128)S(1)} collective-permute-done((f32[80,128]{1,0:T(8,128)S(1)}, f32[80,128]{1,0:T(8,128)S(1)}, u32[]{:S(2)}, u32[]{:S(2)}) %collective-permute-start.10) | collective-permute-done | bytes 40992 | tf_op jit(solution)/shard_map/ppermute | solution.py:520
  47.7 2.9 %shard_map.251 = (bf16[256,1536]{1,0:T(8,128)(2,1)}, f32[256,1536]{1,0:T(8,128)S(1)}, bf16[32,1536]{1,0:T(8,128)(2,1)}, bf16[32,1536]{1,0:T(8,128)(2,1)S(1)}, bf...) custom-call(s32[1]{0:T(128)} %bitcast.refs_0_.idx, ...), custom_call_target="tpu_custom_call" | custom-call | flops 3300000000 | bytes 2211840 | tf_op jit(solution)/shard_map/pallas_call | solution.py:29
  50.6 6.2 %collective-permute-start.15 = (f32[8,1536]{1,0:T(8,128)S(1)}, f32[8,1536]{1,0:T(8,128)S(1)}, u32[]{:S(2)}, u32[]{:S(2)}) collective-permute-start(f32[8,1536]{1,0:T(8,128)S(1)} %get-tuple-element.75), channel_id=1, source_target_pairs={{0,32},{2,34},{4,36},{6,38},{8,40},{10,42},{12,44},{14,46},{16,48}... | collective-permute-start | bytes 147464 | tf_op jit(solution)/shard_map/ppermute | solution.py:543
  57.8 2.9 %collective-permute-done.16 = f32[8,1536]{1,0:T(8,128)S(1)} collective-permute-done((f32[8,1536]{1,0:T(8,128)S(1)}, f32[8,1536]{1,0:T(8,128)S(1)}, u32[]{:S(2)}, u32[]{:S(2)}) %collective-permute-start.16) | collective-permute-done | bytes 49184 | tf_op jit(solution)/shard_map/ppermute | solution.py:543
  60.6 3.7 %collective-permute-start.17 = (f32[8,1536]{1,0:T(8,128)S(1)}, f32[8,1536]{1,0:T(8,128)S(1)}, u32[]{:S(2)}, u32[]{:S(2)}) collective-permute-start(f32[8,1536]{1,0:T(8,128)S(1)} %add.34), channel_id=1, source_target_pairs={{0,4},{2,6},{4,0},{6,2},{8,12},{10,14},{12,8},{14,10},{16,20},{18,... | collective-permute-start | bytes 147464 | tf_op jit(solution)/shard_map/ppermute | solution.py:543
  64.4 2.8 %collective-permute-done.17 = f32[8,1536]{1,0:T(8,128)S(1)} collective-permute-done((f32[8,1536]{1,0:T(8,128)S(1)}, f32[8,1536]{1,0:T(8,128)S(1)}, u32[]{:S(2)}, u32[]{:S(2)}) %collective-permute-start.17) | collective-permute-done | bytes 49184 | tf_op jit(solution)/shard_map/ppermute | solution.py:543
  67.3 4.4 %collective-permute-done.18 = f32[8,1536]{1,0:T(8,128)S(1)} collective-permute-done((f32[8,1536]{1,0:T(8,128)S(1)}, f32[8,1536]{1,0:T(8,128)S(1)}, u32[]{:S(2)}, u32[]{:S(2)}) %collective-permute-start.18) | collective-permute-done | bytes 49184 | tf_op jit(solution)/shard_map/ppermute | solution.py:543
  71.7 1.6 %collective-permute-start.19 = (f32[8,1536]{1,0:T(8,128)S(1)}, f32[8,1536]{1,0:T(8,128)S(1)}, u32[]{:S(2)}, u32[]{:S(2)}) collective-permute-start(f32[8,1536]{1,0:T(8,128)S(1)} %add.36), channel_id=1, source_target_pairs={{0,192},{2,194},{4,196},{6,198},{8,200},{10,202},{12,204},{14,206}... | collective-permute-start | bytes 147464 | tf_op jit(solution)/shard_map/ppermute | solution.py:543
  73.3 2.6 %collective-permute-done.19 = f32[8,1536]{1,0:T(8,128)S(1)} collective-permute-done((f32[8,1536]{1,0:T(8,128)S(1)}, f32[8,1536]{1,0:T(8,128)S(1)}, u32[]{:S(2)}, u32[]{:S(2)}) %collective-permute-start.19) | collective-permute-done | bytes 49184 | tf_op jit(solution)/shard_map/ppermute | solution.py:543
  76.1 5.9 %shard_map.252 = (bf16[256,1536]{1,0:T(8,128)(2,1)}, f32[64,1536]{1,0:T(8,128)S(1)}, bf16[64,1536]{1,0:T(8,128)(2,1)S(1)}, bf16[64,1536]{1,0:T(8,128)(2,1)S(1)}) custom-call(s32[1]{0:T(128)} %bitcast.refs_0_.idx, s32[128,2]{1,0:T(8,128)S(1)} %copy.29.refs_1_, s32[128]{0:T(128)S(1)} %copy-done.13, bf16[256,1536]{1,0:T(8,128)(2,1)S(1)} %copy-done.3, ...), custom_call_target="tpu_custom_call" | custom-call | flops 5500000256 | bytes 3409920 | tf_op jit(solution)/shard_map/pallas_call | solution.py:29
  82.1 6.0 %shard_map.253 = (bf16[256,1536]{1,0:T(8,128)(2,1)}, bf16[256,1536]{1,0:T(8,128)(2,1)}, f32[32,1536]{1,0:T(8,128)S(1)}, bf16[96,1536]{1,0:T(8,128)(2,1)S(1)}, bf16[96,1536]{1,0:T(8,128)(2,1)S(1)}) custom-call(s32[1]{0:T(128)} %bitcast.refs_0_.idx, s32[128,2]{1,0:T(8,128)S(1)} %copy.28.refs_1_, s32[128]{0:T(128)S(1)} %copy-done.15, ...), custom_call_target="tpu_custom_call" | custom-call | flops 5500000256 | bytes 2818048 | tf_op jit(solution)/shard_map/pallas_call | solution.py:29
  88.1 8.6 %collective-permute-start.14 = (bf16[96,1536]{1,0:T(8,128)(2,1)S(1)}, bf16[96,1536]{1,0:T(8,128)(2,1)S(1)}, u32[]{:S(2)}, u32[]{:S(2)}) collective-permute-start(bf16[96,1536]{1,0:T(8,128)(2,1)S(1)} %get-tuple-element.74), channel_id=1, source_target_pairs={{0,254},{2,4},{4,2},{6,8},{8,6},{10,12},{12,10},{14,16},{16,14},{1... | collective-permute-start | bytes 884744 | tf_op jit(solution)/shard_map/ppermute | solution.py:465
  98.0 6.6 %collective-permute-done.14 = bf16[96,1536]{1,0:T(8,128)(2,1)S(1)} collective-permute-done((bf16[96,1536]{1,0:T(8,128)(2,1)S(1)}, bf16[96,1536]{1,0:T(8,128)(2,1)S(1)}, u32[]{:S(2)}, u32[]{:S(2)}) %collective-permute-start.14) | collective-permute-done | bytes 294944 | tf_op jit(solution)/shard_map/ppermute | solution.py:465
  104.7 6.2 %collective-permute-done.13 = bf16[96,1536]{1,0:T(8,128)(2,1)S(1)} collective-permute-done((bf16[96,1536]{1,0:T(8,128)(2,1)S(1)}, bf16[96,1536]{1,0:T(8,128)(2,1)S(1)}, u32[]{:S(2)}, u32[]{:S(2)}) %collective-permute-start.13) | collective-permute-done | bytes 294944 | tf_op jit(solution)/shard_map/ppermute | solution.py:462
  (80 shorter events, 13.7 us)
Async XLA Ops:
  0.6 17.4 %collective-permute-start.2 = (bf16[32,1536]{1,0:T(8,128)(2,1)}, bf16[32,1536]{1,0:T(8,128)(2,1)S(1)}, u32[]{:S(2)}, u32[]{:S(2)}) collective-permute-start(bf16[32,1536]{1,0:T(8,128)(2,1)} %refs_3_.7), channel_id=1, source_target_pairs={{0,2},{2,0},{4,6},{6,4},{8,10},{10,8},{12,14},{14,12},{16,18},{18,... | collective-permute-start | bytes 294920 | tf_op jit(solution)/shard_map/ppermute | solution.py:462
  4.3 13.7 %collective-permute-start.3 = (bf16[32,1536]{1,0:T(8,128)(2,1)}, bf16[32,1536]{1,0:T(8,128)(2,1)S(1)}, u32[]{:S(2)}, u32[]{:S(2)}) collective-permute-start(bf16[32,1536]{1,0:T(8,128)(2,1)} %refs_3_.7), channel_id=1, source_target_pairs={{0,254},{2,4},{4,2},{6,8},{8,6},{10,12},{12,10},{14,16},{16,14},{1... | collective-permute-start | bytes 294920 | tf_op jit(solution)/shard_map/ppermute | solution.py:465
  12.5 16.2 %collective-permute-start = (bf16[64,1536]{1,0:T(8,128)(2,1)S(1)}, bf16[64,1536]{1,0:T(8,128)(2,1)S(1)}, u32[]{:S(2)}, u32[]{:S(2)}) collective-permute-start(bf16[64,1536]{1,0:T(8,128)(2,1)S(1)} %constant_dynamic-update-slice_fusion), channel_id=1, source_target_pairs={{0,2},{2,0},{4,6},{6,4},{8,10},{10,8},{12,14},{14,12},{16,18},{18,... | collective-permute-start | bytes 589832 | tf_op jit(solution)/shard_map/ppermute | solution.py:462
  12.5 16.2 %collective-permute-start.1 = (bf16[64,1536]{1,0:T(8,128)(2,1)S(1)}, bf16[64,1536]{1,0:T(8,128)(2,1)S(1)}, u32[]{:S(2)}, u32[]{:S(2)}) collective-permute-start(bf16[64,1536]{1,0:T(8,128)(2,1)S(1)} %constant_dynamic-update-slice_fusion), channel_id=1, source_target_pairs={{0,254},{2,4},{4,2},{6,8},{8,6},{10,12},{12,10},{14,16},{16,14},{1... | collective-permute-start | bytes 589832 | tf_op jit(solution)/shard_map/ppermute | solution.py:465
  24.6 10.9 %collective-permute-start.6 = (bf16[32,1664]{1,0:T(8,128)(2,1)S(1)}, bf16[32,1664]{1,0:T(8,128)(2,1)S(1)}, u32[]{:S(2)}, u32[]{:S(2)}) collective-permute-start(bf16[32,1664]{1,0:T(8,128)(2,1)S(1)} %get-tuple-element.52), channel_id=1, source_target_pairs={{0,2},{2,0},{4,6},{6,4},{8,10},{10,8},{12,14},{14,12},{16,18},{18,... | collective-permute-start | bytes 319496 | tf_op jit(solution)/shard_map/ppermute | solution.py:462
  24.7 10.8 %collective-permute-start.7 = (bf16[32,1664]{1,0:T(8,128)(2,1)S(1)}, bf16[32,1664]{1,0:T(8,128)(2,1)S(1)}, u32[]{:S(2)}, u32[]{:S(2)}) collective-permute-start(bf16[32,1664]{1,0:T(8,128)(2,1)S(1)} %get-tuple-element.53), channel_id=1, source_target_pairs={{0,254},{2,4},{4,2},{6,8},{8,6},{10,12},{12,10},{14,16},{16,14},{1... | collective-permute-start | bytes 319496 | tf_op jit(solution)/shard_map/ppermute | solution.py:465
  31.5 11.9 %copy-start.2 = (bf16[256,1536]{1,0:T(8,128)(2,1)S(1)}, bf16[256,1536]{1,0:T(8,128)(2,1)}, u32[]{:S(2)}) copy-start(bf16[256,1536]{1,0:T(8,128)(2,1)} %refs_6_.3) | copy-start | bytes 2359300
  31.5 11.9 %copy-start.11 = (f32[3,1536]{1,0:T(4,128)S(1)}, f32[3,1536]{1,0:T(4,128)}, u32[]{:S(2)}) copy-start(f32[3,1536]{1,0:T(4,128)} %refs_12_.2) | copy-start | bytes 55300
  31.5 11.9 %collective-permute-start.4 = (bf16[32,1536]{1,0:T(8,128)(2,1)S(1)}, bf16[32,1536]{1,0:T(8,128)(2,1)S(1)}, u32[]{:S(2)}, u32[]{:S(2)}) collective-permute-start(bf16[32,1536]{1,0:T(8,128)(2,1)S(1)} %get-tuple-element.48), channel_id=1, source_target_pairs={{0,2},{2,0},{4,6},{6,4},{8,10},{10,8},{12,14},{14,12},{16,18},{18,... | collective-permute-start | bytes 294920 | tf_op jit(solution)/shard_map/ppermute | solution.py:462
  31.6 11.8 %collective-permute-start.5 = (bf16[32,1536]{1,0:T(8,128)(2,1)S(1)}, bf16[32,1536]{1,0:T(8,128)(2,1)S(1)}, u32[]{:S(2)}, u32[]{:S(2)}) collective-permute-start(bf16[32,1536]{1,0:T(8,128)(2,1)S(1)} %get-tuple-element.49), channel_id=1, source_target_pairs={{0,254},{2,4},{4,2},{6,8},{8,6},{10,12},{12,10},{14,16},{16,14},{1... | collective-permute-start | bytes 294920 | tf_op jit(solution)/shard_map/ppermute | solution.py:465
  36.0 5.7 %collective-permute-start.8 = (bf16[16,1536]{1,0:T(8,128)(2,1)S(1)}, bf16[16,1536]{1,0:T(8,128)(2,1)S(1)}, u32[]{:S(2)}, u32[]{:S(2)}) collective-permute-start(bf16[16,1536]{1,0:T(8,128)(2,1)S(1)} %get-tuple-element.55), channel_id=1, source_target_pairs={{0,2},{2,0},{4,6},{6,4},{8,10},{10,8},{12,14},{14,12},{16,18},{18,... | collective-permute-start | bytes 147464 | tf_op jit(solution)/shard_map/ppermute | solution.py:462
  36.3 7.1 %collective-permute-start.9 = (bf16[16,1536]{1,0:T(8,128)(2,1)S(1)}, bf16[16,1536]{1,0:T(8,128)(2,1)S(1)}, u32[]{:S(2)}, u32[]{:S(2)}) collective-permute-start(bf16[16,1536]{1,0:T(8,128)(2,1)S(1)} %get-tuple-element.56), channel_id=1, source_target_pairs={{0,254},{2,4},{4,2},{6,8},{8,6},{10,12},{12,10},{14,16},{16,14},{1... | collective-permute-start | bytes 147464 | tf_op jit(solution)/shard_map/ppermute | solution.py:465
  44.5 3.2 %collective-permute-start.10 = (f32[80,128]{1,0:T(8,128)S(1)}, f32[80,128]{1,0:T(8,128)S(1)}, u32[]{:S(2)}, u32[]{:S(2)}) collective-permute-start(f32[80,128]{1,0:T(8,128)S(1)} %shard_map.250.refs_1_), channel_id=1, source_target_pairs={{0,1},{1,0},{2,3},{3,2},{4,5},{5,4},{6,7},{7,6},{8,9},{9,8},{10,11... | collective-permute-start | bytes 122888 | tf_op jit(solution)/shard_map/ppermute | solution.py:520
  50.6 7.0 %collective-permute-start.15 = (f32[8,1536]{1,0:T(8,128)S(1)}, f32[8,1536]{1,0:T(8,128)S(1)}, u32[]{:S(2)}, u32[]{:S(2)}) collective-permute-start(f32[8,1536]{1,0:T(8,128)S(1)} %get-tuple-element.75), channel_id=1, source_target_pairs={{0,32},{2,34},{4,36},{6,38},{8,40},{10,42},{12,44},{14,46},{16,48}... | collective-permute-start | bytes 147464 | tf_op jit(solution)/shard_map/ppermute | solution.py:543
  56.8 19.2 %collective-permute-start.11 = (bf16[64,1664]{1,0:T(8,128)(2,1)S(1)}, bf16[64,1664]{1,0:T(8,128)(2,1)S(1)}, u32[]{:S(2)}, u32[]{:S(2)}) collective-permute-start(bf16[64,1664]{1,0:T(8,128)(2,1)S(1)} %get-tuple-element.61), channel_id=1, source_target_pairs={{0,2},{2,0},{4,6},{6,4},{8,10},{10,8},{12,14},{14,12},{16,18},{18,... | collective-permute-start | bytes 638984 | tf_op jit(solution)/shard_map/ppermute | solution.py:462
  56.8 19.2 %collective-permute-start.12 = (bf16[64,1664]{1,0:T(8,128)(2,1)S(1)}, bf16[64,1664]{1,0:T(8,128)(2,1)S(1)}, u32[]{:S(2)}, u32[]{:S(2)}) collective-permute-start(bf16[64,1664]{1,0:T(8,128)(2,1)S(1)} %get-tuple-element.62), channel_id=1, source_target_pairs={{0,254},{2,4},{4,2},{6,8},{8,6},{10,12},{12,10},{14,16},{16,14},{1... | collective-permute-start | bytes 638984 | tf_op jit(solution)/shard_map/ppermute | solution.py:465
  57.7 2.9 %collective-permute-start.16 = (f32[8,1536]{1,0:T(8,128)S(1)}, f32[8,1536]{1,0:T(8,128)S(1)}, u32[]{:S(2)}, u32[]{:S(2)}) collective-permute-start(f32[8,1536]{1,0:T(8,128)S(1)} %add.33), channel_id=1, source_target_pairs={{0,64},{2,66},{4,68},{6,70},{8,72},{10,74},{12,76},{14,78},{16,80}... | collective-permute-start | bytes 147464 | tf_op jit(solution)/shard_map/ppermute | solution.py:543
  60.6 6.5 %collective-permute-start.17 = (f32[8,1536]{1,0:T(8,128)S(1)}, f32[8,1536]{1,0:T(8,128)S(1)}, u32[]{:S(2)}, u32[]{:S(2)}) collective-permute-start(f32[8,1536]{1,0:T(8,128)S(1)} %add.34), channel_id=1, source_target_pairs={{0,4},{2,6},{4,0},{6,2},{8,12},{10,14},{12,8},{14,10},{16,20},{18,... | collective-permute-start | bytes 147464 | tf_op jit(solution)/shard_map/ppermute | solution.py:543
  67.2 4.5 %collective-permute-start.18 = (f32[8,1536]{1,0:T(8,128)S(1)}, f32[8,1536]{1,0:T(8,128)S(1)}, u32[]{:S(2)}, u32[]{:S(2)}) collective-permute-start(f32[8,1536]{1,0:T(8,128)S(1)} %add.35), channel_id=1, source_target_pairs={{0,2},{2,0},{4,6},{6,4},{8,10},{10,8},{12,14},{14,12},{16,18},{18,... | collective-permute-start | bytes 147464 | tf_op jit(solution)/shard_map/ppermute | solution.py:543
  71.7 4.2 %collective-permute-start.19 = (f32[8,1536]{1,0:T(8,128)S(1)}, f32[8,1536]{1,0:T(8,128)S(1)}, u32[]{:S(2)}, u32[]{:S(2)}) collective-permute-start(f32[8,1536]{1,0:T(8,128)S(1)} %add.36), channel_id=1, source_target_pairs={{0,192},{2,194},{4,196},{6,198},{8,200},{10,202},{12,204},{14,206}... | collective-permute-start | bytes 147464 | tf_op jit(solution)/shard_map/ppermute | solution.py:543
  75.9 6.0 %collective-permute-start.20 = (f32[8,1536]{1,0:T(8,128)S(1)}, f32[8,1536]{1,0:T(8,128)S(1)}, u32[]{:S(2)}, u32[]{:S(2)}) collective-permute-start(f32[8,1536]{1,0:T(8,128)S(1)} %add.37), channel_id=1, source_target_pairs={{0,8},{2,10},{4,12},{6,14},{8,0},{10,2},{12,4},{14,6},{16,24},{18,... | collective-permute-start | bytes 147464 | tf_op jit(solution)/shard_map/ppermute | solution.py:543
  82.0 14.8 %collective-permute-start.21 = (f32[8,1536]{1,0:T(8,128)S(1)}, f32[8,1536]{1,0:T(8,128)S(1)}, u32[]{:S(2)}, u32[]{:S(2)}) collective-permute-start(f32[8,1536]{1,0:T(8,128)S(1)} %add.38), channel_id=1, source_target_pairs={{0,28},{2,30},{4,24},{6,26},{8,20},{10,22},{12,16},{14,18},{16,12}... | collective-permute-start | bytes 147464 | tf_op jit(solution)/shard_map/ppermute | solution.py:543
  88.1 16.5 %collective-permute-start.14 = (bf16[96,1536]{1,0:T(8,128)(2,1)S(1)}, bf16[96,1536]{1,0:T(8,128)(2,1)S(1)}, u32[]{:S(2)}, u32[]{:S(2)}) collective-permute-start(bf16[96,1536]{1,0:T(8,128)(2,1)S(1)} %get-tuple-element.74), channel_id=1, source_target_pairs={{0,254},{2,4},{4,2},{6,8},{8,6},{10,12},{12,10},{14,16},{16,14},{1... | collective-permute-start | bytes 884744 | tf_op jit(solution)/shard_map/ppermute | solution.py:465
  96.8 14.1 %collective-permute-start.13 = (bf16[96,1536]{1,0:T(8,128)(2,1)S(1)}, bf16[96,1536]{1,0:T(8,128)(2,1)S(1)}, u32[]{:S(2)}, u32[]{:S(2)}) collective-permute-start(bf16[96,1536]{1,0:T(8,128)(2,1)S(1)} %get-tuple-element.73), channel_id=1, source_target_pairs={{0,2},{2,0},{4,6},{6,4},{8,10},{10,8},{12,14},{14,12},{16,18},{18,... | collective-permute-start | bytes 884744 | tf_op jit(solution)/shard_map/ppermute | solution.py:462
  (16 other events, 90.5 us)

commit v3 on v2

--- a/solution.py
+++ b/solution.py
@@ -22,15 +22,21 @@
     )
 
 
-def call(kernel, outs, args, scalars, micros, scratch=()):
+def call(kernel, outs, args, scalars, micros, scratch=(), far_args=(), far_outs=(), unread=()):
     vmem = pl.BlockSpec(memory_space=pltpu.VMEM)
     smem = pl.BlockSpec(memory_space=pltpu.SMEM)
+    anywhere = pl.BlockSpec(memory_space=pl.ANY)
+    far = pl.BlockSpec(memory_space=pltpu.HBM)
     size = sum(a.size * a.dtype.itemsize for a in args)
     return pl.pallas_call(
         kernel,
         out_shape=[jax.ShapeDtypeStruct(s, d) for s, d in outs],
-        in_specs=[smem] * len(scalars) + [vmem] * len(args),
-        out_specs=[vmem] * len(outs),
+        in_specs=[smem] * len(scalars)
+        + [
+            anywhere if n in unread else far if n in far_args else vmem
+            for n in range(len(args))
+        ],
+        out_specs=[anywhere if n in far_outs else vmem for n in range(len(outs))],
         scratch_shapes=list(scratch),
         compiler_params=pltpu.CompilerParams(vmem_limit_bytes=48 * 1024 * 1024),
         cost_estimate=pl.CostEstimate(
@@ -39,8 +45,76 @@
     )(*scalars, *args)
 
 
+CHUNK = 6
+
+
+class Stream:
+    def __init__(self, pairs, sems, heads):
+        self.pairs, self.sems = pairs, sems
+        self.parts = heads // CHUNK
+
+    def copies(self, part):
+        c = slice(part * CHUNK * HEAD_DIM, (part + 1) * CHUNK * HEAD_DIM)
+        return [
+            pltpu.make_async_copy(src.at[:, c], dst.at[:, c], self.sems.at[n, part])
+            for n, (src, dst) in enumerate(self.pairs)
+        ]
+
+    def start(self, part):
+        for copy in self.copies(part):
+            copy.start()
+
+    def wait(self, part):
+        for copy in self.copies(part):
+            copy.wait()
+
+    def start_all(self):
+        for part in range(self.parts):
+            self.start(part)
+
+    def wait_all(self):
+        for part in range(self.parts):
+            self.wait(part)
+
+    def before_head(self, h):
+        if h % CHUNK == 0:
+            self.wait(h // CHUNK)
+
+    def after_head(self, h):
+        if h % CHUNK == CHUNK - 1:
+            self.start(h // CHUNK)
+
+
+def pack_rows(k, v, both, sems):
+    rows = k.shape[0]
+    copies = [
+        pltpu.make_async_copy(k, both.at[0:rows], sems.at[0]),
+        pltpu.make_async_copy(v, both.at[rows:], sems.at[1]),
+    ]
+    for copy in copies:
+        copy.start()
+    for copy in copies:
+        copy.wait()
+
+
+def plus(*refs):
+    refs[-1][...] = refs[0][...] + refs[1][...]
+
+
+def split_sums(mine, theirs, taps_v, taps_a, gain_v, gain_a):
+    total = mine[...] + theirs[...]
+    taps_v[...] = total[0:3]
+    gain_v[...] = total[3]
+    taps_a[...] = total[4:7]
+    gain_a[...] = total[7]
+
+
 def other(i, count):
     return (i + 2 * (i & 1) - 1 + count) & (count - 1)
+
+
+def groups(heads, size):
+    return [range(g, min(g + size, heads)) for g in range(0, heads, size)]
 
 
 def columns(h):
@@ -68,8 +142,8 @@
     lower, upper = [
         jnp.where(
             slot == 0,
-            window[blocks[0], side],
-            jnp.where(slot == 1, window[blocks[1], side], window[blocks[2], side]),
+            window[side, blocks[0]],
+            jnp.where(slot == 1, window[side, blocks[1]], window[side, blocks[2]]),
         )
         for side in (0, 1)
     ]
@@ -88,29 +162,36 @@
     parts = []
     for c in (i, i ^ 1, other(i, count)):
         position = c * rows_k + row
-        seen = (position >= window[i, 0]) & (position < window[i, 1]) & (row < valid[c])
+        seen = (position >= window[0, i]) & (position < window[1, i]) & (row < valid[c])
         parts.append(jnp.where(seen, 0.0, NEGATIVE))
     return jnp.concatenate(parts, 0)
 
 
 def audio_forward(
-    count, idx, window, valid, q, qe, qo, k, v, send_e, send_o, own, own_lse, rows_lse
+    count, idx, window, valid, q, qe, qo, k, v, send_e, send_o, own, own_lse,
+    rows_lse,
 ):
     rows = q.shape[0]
     heads = q.shape[1] // HEAD_DIM
     bias = audio_bias(idx[0], count, window, valid, rows, k.shape[0])
     rows_lse[...] = jnp.zeros(rows_lse.shape, F32)
-    for h in range(heads):
-        c = columns(h)
-        scores = dot(k[:, c], padded(q, qe, qo, c), 1, 1) * FACTOR + bias
-        peak = jnp.max(scores, 0, keepdims=True)
-        weight = jnp.exp(scores - peak)
-        total = jnp.sum(weight, 0, keepdims=True)
-        part = dot((weight * (1.0 / total)).astype(BF), v[:, c], 0, 0)
-        rows_lse[h : h + 1, :] = peak + jnp.log(total)
-        own[:, c] = part[:rows]
-        send_e[:, c] = part[rows : 2 * rows].astype(BF)
-        send_o[:, c] = part[2 * rows : 3 * rows].astype(BF)
+    for group in groups(heads, heads):
+        scores, probs = {}, {}
+        for h in group:
+            c = columns(h)
+            scores[h] = dot(k[:, c], padded(q, qe, qo, c), 1, 1) * FACTOR + bias
+        for h in group:
+            peak = jnp.max(scores[h], 0, keepdims=True)
+            weight = jnp.exp(scores[h] - peak)
+            total = jnp.sum(weight, 0, keepdims=True)
+            rows_lse[h : h + 1, :] = peak + jnp.log(total)
+            probs[h] = (weight * (1.0 / total)).astype(BF)
+        for h in group:
+            c = columns(h)
+            part = dot(probs[h], v[:, c], 0, 0)
+            own[:, c] = part[:rows]
+            send_e[:, c] = part[rows : 2 * rows].astype(BF)
+            send_o[:, c] = part[2 * rows : 3 * rows].astype(BF)
     tile = jnp.transpose(rows_lse[...])
     own_lse[...] = tile[:rows]
     tail = slice(heads * HEAD_DIM, heads * HEAD_DIM + PAD)
@@ -125,24 +206,28 @@
 
 
 def video_forward(
-    count, idx, window, valid, q, k, v, kve, kvo, att, lse, send_e, send_o
+    count, idx, window, valid, q, k, v, kve, kvo, _, att, lse, send_e, send_o
 ):
     rows = q.shape[0]
     heads = q.shape[1] // HEAD_DIM
     i = idx[0]
     bias = video_bias(i, count, window, valid, rows, k.shape[0])
     lse[...] = jnp.zeros(lse.shape, F32)
-    for h in range(heads):
-        c = columns(h)
-        keys = near_columns(k, kve, kvo, c, 0)
-        values = near_columns(v, kve, kvo, c, 1)
-        scores = dot(keys, q[:, c], 1, 1) * FACTOR + bias
-        peak = jnp.max(scores, 0, keepdims=True)
-        weight = jnp.exp(scores - peak)
-        total = jnp.sum(weight, 0, keepdims=True)
-        prob = (weight * (1.0 / total)).astype(BF)
-        att[:, c] = dot(prob, values, 0, 0).astype(BF)
-        lse[h : h + 1, :] = peak + jnp.log(total)
+    for group in groups(heads, heads):
+        scores, probs = {}, {}
+        for h in group:
+            c = columns(h)
+            keys = near_columns(k, kve, kvo, c, 0)
+            scores[h] = dot(keys, q[:, c], 1, 1) * FACTOR + bias
+        for h in group:
+            peak = jnp.max(scores[h], 0, keepdims=True)
+            weight = jnp.exp(scores[h] - peak)
+            total = jnp.sum(weight, 0, keepdims=True)
+            lse[h : h + 1, :] = peak + jnp.log(total)
+            probs[h] = (weight * (1.0 / total)).astype(BF)
+        for h in group:
+            c = columns(h)
+            att[:, c] = dot(probs[h], near_columns(v, kve, kvo, c, 1), 0, 0).astype(BF)
     odd = i & 1
     for send, side in ((send_e, 1 - odd), (send_o, odd)):
         start = pl.multiple_of(side * (rows - STRIDE), STRIDE)
@@ -265,8 +350,8 @@
     mix = Mix(count, idx, refs[2:14])
     mine, theirs = refs[0], refs[1]
     total_a = refs[14]
-    out_v, grad_v, out_a, up_a, send_e, send_o, dots_a, parts = refs[15:23]
-    scale_ref, shrink_ref = refs[23:25]
+    grad_v, up_a, send_e, send_o, dots_a, parts = refs[15:21]
+    scale_ref, shrink_ref = refs[21:23]
     heads = mix.att_v.shape[1] // HEAD_DIM
     sums = mine[...] + theirs[...]
     rows_a = mix.att_a.shape[0]
@@ -306,7 +391,6 @@
             incoming = mix.video_cot(g, c)
             grad = scale * (incoming * gain) - mixed * shrink_ref[s, :]
             normed = mixed * scale
-            out_v[s, c] = (normed * gain).astype(BF)
             grad_v[s, c] = grad
             sum_gain += incoming * normed
             for k in range(3):
@@ -322,7 +406,6 @@
         taps = [mix.conv_a[k : k + 1, c] for k in range(3)]
         normed = mixed * scale_a
         grad = scale_a * (cot * gain) - mixed * shrink_a
-        out_a[:, c] = (normed * gain)[own].astype(BF)
         upstream = (
             taps[0] * pltpu.roll(grad, ext - 1, 0)
             + taps[1] * grad
@@ -350,12 +433,41 @@
         send[rows_a:, tail] = jnp.zeros((STRIDE, PAD), BF)
 
 
+def outputs(count, width, idx, *refs):
+    mix = Mix(count, idx, refs[2:14])
+    sums = refs[0][...] + refs[1][...]
+    out_v, out_a, token = refs[15:18]
+    token[...] = jnp.zeros(token.shape, F32)
+    heads = mix.att_v.shape[1] // HEAD_DIM
+    rows_a = mix.att_a.shape[0]
+    scales = [
+        jnp.broadcast_to(
+            lax.rsqrt(sums[0:STRIDE, g : g + 1] / width + EPSILON), (STRIDE, HEAD_DIM)
+        )
+        for g in range(mix.chunks)
+    ]
+    scale_a = jnp.broadcast_to(
+        lax.rsqrt(sums[STRIDE:, 0:1] / width + EPSILON), (rows_a + 16, HEAD_DIM)
+    )
+    for h in range(heads):
+        c = columns(h)
+        taps = [mix.conv_v[k : k + 1, c] for k in range(3)]
+        gain = mix.gain_v[0:1, c]
+        for g in range(mix.chunks):
+            mixed = sum(taps[k] * mix.video_att(g + k - 1, c) for k in range(3))
+            s = slice(g * STRIDE, (g + 1) * STRIDE)
+            out_v[s, c] = (mixed * scales[g] * gain).astype(BF)
+        normed = mix.audio(c)[0] * scale_a
+        out_a[:, c] = (normed * mix.gain_a[0:1, c])[8 : 8 + rows_a].astype(BF)
+
+
 def video_backward(
     count, idx, window, valid, q, grad, re, ro, conv, lse, k, v, kve, kvo,
-    dq, own, send_e, send_o,
+    dq_far, own, send_e, send_o, dq, sems_out,
 ):
     rows = q.shape[0]
     heads = q.shape[1] // HEAD_DIM
+    back = Stream([(dq, dq_far)], sems_out, heads)
     near = k.shape[0]
     i = idx[0]
     even = (i & 1) == 0
@@ -363,42 +475,52 @@
     has_next = (i < count - 1).astype(F32)
     bias = video_bias(i, count, window, valid, rows, near)
     halo = slice(near, near + STRIDE)
-    for h in range(heads):
-        c = columns(h)
-        keys = near_columns(k, kve, kvo, c, 0)
-        values = near_columns(v, kve, kvo, c, 1)
-        queries = q[:, c]
-        first, second = re[halo, c].astype(F32), ro[halo, c].astype(F32)
-        before = jnp.where(even, second, first) * has_prev
-        after = jnp.where(even, first, second) * has_next
-        own_grad = grad[:, c]
-        wide = jnp.concatenate([before, own_grad, after], 0)
-        upstream = (
-            conv[0:1, c] * wide[2 * STRIDE :]
-            + conv[1:2, c] * own_grad
-            + conv[2:3, c] * wide[0:rows]
-        ).astype(BF)
-        scores = dot(keys, queries, 1, 1) * FACTOR + bias
-        prob = jnp.exp(scores - lse[h : h + 1, :])
-        prob_grad = dot(values, upstream, 1, 1)
-        row_dot = jnp.sum(prob * prob_grad, 0, keepdims=True)
-        score_grad = (prob * (prob_grad - row_dot)).astype(BF)
-        dq[:, c] = (dot(score_grad, keys, 0, 0) * FACTOR).astype(BF)
-        dk = dot(score_grad, queries, 1, 0) * FACTOR
-        dv = dot(prob.astype(BF), upstream, 1, 0)
-        for part, value in enumerate((dk, dv)):
-            s = slice(part * near, (part + 1) * near)
-            own[s, c] = value[0:near]
-            send_e[s, c] = value[near : 2 * near].astype(BF)
-            send_o[s, c] = value[2 * near :].astype(BF)
+    for group in groups(heads, CHUNK):
+        upstream, scores, prob_grad, prob, score_grad = {}, {}, {}, {}, {}
+        for h in group:
+            c = columns(h)
+            keys = near_columns(k, kve, kvo, c, 0)
+            scores[h] = dot(keys, q[:, c], 1, 1) * FACTOR + bias
+        for h in group:
+            c = columns(h)
+            first, second = re[halo, c].astype(F32), ro[halo, c].astype(F32)
+            before = jnp.where(even, second, first) * has_prev
+            after = jnp.where(even, first, second) * has_next
+            own_grad = grad[:, c]
+            wide = jnp.concatenate([before, own_grad, after], 0)
+            upstream[h] = (
+                conv[0:1, c] * wide[2 * STRIDE :]
+                + conv[1:2, c] * own_grad
+                + conv[2:3, c] * wide[0:rows]
+            ).astype(BF)
+            prob_grad[h] = dot(near_columns(v, kve, kvo, c, 1), upstream[h], 1, 1)
+        for h in group:
+            p = jnp.exp(scores[h] - lse[h : h + 1, :])
+            row_dot = jnp.sum(p * prob_grad[h], 0, keepdims=True)
+            score_grad[h] = (p * (prob_grad[h] - row_dot)).astype(BF)
+            prob[h] = p.astype(BF)
+        for h in group:
+            c = columns(h)
+            keys = near_columns(k, kve, kvo, c, 0)
+            dq[:, c] = (dot(score_grad[h], keys, 0, 0) * FACTOR).astype(BF)
+            dk = dot(score_grad[h], q[:, c], 1, 0) * FACTOR
+            dv = dot(prob[h], upstream[h], 1, 0)
+            for part, value in enumerate((dk, dv)):
+                s = slice(part * near, (part + 1) * near)
+                own[s, c] = value[0:near]
+                send_e[s, c] = value[near : 2 * near].astype(BF)
+                send_o[s, c] = value[2 * near :].astype(BF)
+            back.after_head(h)
+    back.wait_all()
 
 
 def audio_backward(
-    count, idx, window, valid, q, qe, qo, up, re, ro, total, dots, k, v, part_e, part_o,
-    dk, dv, own, send_e, send_o,
+    count, idx, window, valid, q, qe, qo, up, re, ro, total, dots, k, v,
+    part_e, part_o, dk_far, dv_far, own, send_e, send_o, dk, dv, sems_out,
 ):
     rows = q.shape[0]
     heads = q.shape[1] // HEAD_DIM
+    back = Stream([(dk, dk_far), (dv, dv_far)], sems_out, heads)
     tail = slice(heads * HEAD_DIM, heads * HEAD_DIM + PAD)
     bias = audio_bias(idx[0], count, window, valid, rows, k.shape[0])
     totals, row_dots = [total[...]], [dots[...]]
@@ -413,21 +535,26 @@
     done = slice(0, 2 * rows)
     send_e[done, :] = part_e[...]
     send_o[done, :] = part_o[...]
-    for h in range(heads):
-        c = columns(h)
-        queries = padded(q, qe, qo, c)
-        upstream = padded(up, up_e, up_o, c)
-        keys, values = k[:, c], v[:, c]
-        scores = dot(keys, queries, 1, 1) * FACTOR + bias
-        prob = jnp.exp(scores - totals[h : h + 1, :])
-        prob_grad = dot(values, upstream, 1, 1)
-        score_grad = (prob * (prob_grad - row_dots[h : h + 1, :])).astype(BF)
-        dq = dot(score_grad, keys, 0, 0) * FACTOR
-        dk[:, c] = (dot(score_grad, queries, 1, 0) * FACTOR).astype(BF)
-        dv[:, c] = dot(prob.astype(BF), upstream, 1, 0).astype(BF)
-        own[:, c] = dq[:rows]
-        send_e[2 * rows :, c] = dq[rows : 2 * rows].astype(BF)
-        send_o[2 * rows :, c] = dq[2 * rows : 3 * rows].astype(BF)
+    for group in groups(heads, CHUNK):
+        scores, prob_grad, prob, score_grad = {}, {}, {}, {}
+        for h in group:
+            c = columns(h)
+            scores[h] = dot(k[:, c], padded(q, qe, qo, c), 1, 1) * FACTOR + bias
+            prob_grad[h] = dot(v[:, c], padded(up, up_e, up_o, c), 1, 1)
+        for h in group:
+            p = jnp.exp(scores[h] - totals[h : h + 1, :])
+            score_grad[h] = (p * (prob_grad[h] - row_dots[h : h + 1, :])).astype(BF)
+            prob[h] = p.astype(BF)
+        for h in group:
+            c = columns(h)
+            grad = dot(score_grad[h], k[:, c], 0, 0) * FACTOR
+            dk[:, c] = (dot(score_grad[h], padded(q, qe, qo, c), 1, 0) * FACTOR).astype(BF)
+            dv[:, c] = dot(prob[h], padded(up, up_e, up_o, c), 1, 0).astype(BF)
+            own[:, c] = grad[:rows]
+            send_e[2 * rows :, c] = grad[rows : 2 * rows].astype(BF)
+            send_o[2 * rows :, c] = grad[2 * rows : 3 * rows].astype(BF)
+            back.after_head(h)
+    back.wait_all()
 
 
 def per_device(
@@ -471,12 +598,19 @@
         return kernel
 
     qe, qo = swap_e(query_audio), swap_o(query_audio)
-    both = jnp.concatenate([key_audio, value_audio], 0)
+    (both,) = call(
+        pack_rows, [((2 * rows_a, wide), BF)], [key_audio, value_audio], (), 0.5,
+        [pltpu.SemaphoreType.DMA((2,))], (0, 1),
+    )
     kve, kvo = swap_e(both), swap_o(both)
+    big = pltpu.VMEM((rows_v, wide), BF)
+
+    def sems(count):
+        return pltpu.SemaphoreType.DMA((count, heads // CHUNK))
 
     packed = ((rows_a, wide + PAD), BF)
-    audio_info = (idx, audio_window, video_valid)
-    video_info = (idx, video_window, audio_valid)
+    audio_info = (idx, audio_window.T, video_valid)
+    video_info = (idx, video_window.T, audio_valid)
     send_e, send_o, own_part, own_lse = call(
         bind(audio_forward, count),
         [packed, packed, ((rows_a, wide), F32), ((rows_a, PAD), F32)],
@@ -485,16 +619,19 @@
         3.0,
         [pltpu.VMEM((PAD, PAD), F32)],
     )
-    kve, kvo, own_lse = lax.optimization_barrier((kve, kvo, own_lse))
     pe, po = swap_e(send_e), swap_o(send_o)
     keys_values = [key_audio, value_audio, kve, kvo]
     halo = ((STRIDE, wide), BF)
     att_v, lse_v, hv_e, hv_o = call(
         bind(video_forward, count),
         [((rows_v, wide), BF), (((heads + 7) // 8 * 8, rows_v), F32), halo, halo],
-        [query_video] + keys_values,
+        [query_video] + keys_values + [own_lse],
         video_info,
-        2.8,
+        2.5,
+        (),
+        (),
+        (),
+        (5,),
     )
     hve, hvo = swap_e(hv_e), swap_o(hv_o)
     halo_a = ((16, wide), BF)
@@ -520,12 +657,10 @@
     stats_other = lax.ppermute(stats, "tp", [(i, i ^ 1) for i in range(tp_size)])
     chunks = rows_v // STRIDE
     both = ((rows_a + STRIDE, wide + PAD), BF)
-    out_v, grad_v, out_a, up_a, back_e, back_o, dots_a, parts = call(
+    grad_v, up_a, back_e, back_o, dots_a, parts = call(
         bind(norm_backward, count, model),
         [
-            ((rows_v, wide), BF),
             ((rows_v, wide), F32),
-            ((rows_a, wide), BF),
             ((rows_a, wide), BF),
             both,
             both,
@@ -534,13 +669,35 @@
         ],
         [stats, stats_other] + mix_args + [total_a],
         (idx,),
-        3.0,
+        2.5,
         [pltpu.VMEM((rows_v, HEAD_DIM), F32)] * 2,
     )
     re, ro = swap_e(back_e), swap_o(back_o)
-    total = parts
-    for bits in (16, 32, 2, 1, 96, 4, 14):
-        total = total + lax.ppermute(total, BLOCKS, [(i, i ^ bits) for i in range(count)])
+
+    def moved(x, bits):
+        return lax.ppermute(x, BLOCKS, [(i, i ^ bits) for i in range(count)])
+
+    def summed(x, bits, *after):
+        (y,) = call(
+            plus, [((8, wide), F32)], [x, moved(x, bits)] + list(after), (), 0.5,
+            (), (), (), range(2, 2 + len(after)),
+        )
+        return y
+
+    total = summed(parts, 16)
+    out_v, out_a, token = call(
+        bind(outputs, count, model),
+        [((rows_v, wide), BF), ((rows_a, wide), BF), ((8, PAD), F32)],
+        [stats, stats_other] + mix_args + [total],
+        (idx,),
+        1.5,
+        (),
+        (),
+        (),
+        (14,),
+    )
+    total = summed(total, 32, token)
+    total = summed(total, 2, re, ro)
 
     two = ((2 * rows_a, wide), BF)
     dq_v, dkv_own, dkv_e, dkv_o = call(
@@ -548,8 +705,12 @@
         [((rows_v, wide), BF), ((2 * rows_a, wide), F32), two, two],
         [query_video, grad_v, re, ro, conv_video, lse_v] + keys_values,
         video_info,
-        5.0,
-    )
+        4.5,
+        [big, sems(1)],
+        (),
+        (0,),
+    )
+    total = summed(total, 1, dkv_own)
     three = ((3 * rows_a, wide), BF)
     dk_v, dv_v, dq_own, give_e, give_o = call(
         bind(audio_backward, count),
@@ -557,9 +718,21 @@
         [query_audio, qe, qo, up_a, re, ro, total_a, dots_a, key_video, value_video,
          dkv_e, dkv_o],
         audio_info,
-        5.0,
+        4.5,
+        [big] * 2 + [sems(2)],
+        (),
+        (0, 1),
     )
     got_e, got_o = swap_e(give_e), swap_o(give_o)
+    total = summed(total, 96, dq_own)
+    total = summed(total, 4)
+    taps_v, taps_a, gain_v, gain_a = call(
+        split_sums,
+        [((3, wide), F32), ((3, wide), F32), ((wide,), F32), ((wide,), F32)],
+        [total, moved(total, 14)],
+        (),
+        0.5,
+    )
     own = jnp.concatenate([dkv_own, dq_own], 0)
     grads = (own + got_e.astype(F32) + got_o.astype(F32)).astype(BF)
     return (
@@ -571,10 +744,10 @@
         grads[2 * rows_a :],
         grads[:rows_a],
         grads[rows_a : 2 * rows_a],
-        total[0:3],
-        total[4:7],
-        total[3],
-        total[7],
+        taps_v,
+        taps_a,
+        gain_v,
+        gain_a,
     )
 
 

time: 112 us -> 93.8 us (0.84)
  the two profiles are of different devices: /device:TPU:1 before, /device:TPU:2 now
where the time goes in v3:
time: 93.8 us; the launch traced here: 92.2 us
  starting transfers between devices  40.9 us (44%)
  waiting for transfers between devices  33 us (35%)
  Pallas kernels  14.6 us (16%)
  local copies, waits for them, and re-layouts  2.6 us (3%)
  between operations  1.02 us (1%)
    ppermute x7, starting transfers between devices, swap_o(): return lax.ppermute(x, BLOCKS, odd_route)  25.7 us
    ppermute x7, waiting for transfers between devices, moved(): return lax.ppermute(x, BLOCKS, [(i, i ^ bits) for i in range(count)])  17.7 us
    pallas_call x16, Pallas kernels, call(): pl.pallas_call(kernel, out_shape=[jax.ShapeDtypeStruct(s, d) for s, d in...  14.6 us
    ppermute x7, starting transfers between devices, swap_e(): return lax.ppermute(x, BLOCKS, even_route)  8.76 us
    ppermute x7, waiting for transfers between devices, swap_e(): return lax.ppermute(x, BLOCKS, even_route)  6.76 us
    ppermute x7, starting transfers between devices, moved(): return lax.ppermute(x, BLOCKS, [(i, i ^ bits) for i in range(count)])  5.84 us
    ppermute x7, waiting for transfers between devices, swap_o(): return lax.ppermute(x, BLOCKS, odd_route)  5.08 us
    ppermute x1, waiting for transfers between devices, per_device(): lax.ppermute(stats, 'tp', [(i, i ^ 1) for i in range(tp_size)])  3.46 us
  transfers between devices with their start and end apart: 22, of which 10 were waited for; matrix products, arithmetic and copies ran while one was open for 0% of the time, Pallas kernels for 13%

profile of v3, /device:TPU:2, one launch (start us, length us, event | category | flops | bytes accessed | tf_op | source)
XLA Modules:
  0.0 92.2 jit_solution(16585729847379856440)
XLA Ops:
  0.7 2.2 %collective-permute-start.2 = (bf16[32,1536]{1,0:T(8,128)(2,1)}, bf16[32,1536]{1,0:T(8,128)(2,1)S(1)}, u32[]{:S(2)}, u32[]{:S(2)}) collective-permute-start(bf16[32,1536]{1,0:T(8,128)(2,1)} %refs_3_.7), channel_id=1, source_target_pairs={{0,2},{2,0},{4,6},{6,4},{8,10},{10,8},{12,14},{14,12},{16,18},{18,... | collective-permute-start | bytes 294920 | tf_op jit(solution)/shard_map/ppermute | solution.py:589
  2.9 8.3 %collective-permute-start.3 = (bf16[32,1536]{1,0:T(8,128)(2,1)}, bf16[32,1536]{1,0:T(8,128)(2,1)S(1)}, u32[]{:S(2)}, u32[]{:S(2)}) collective-permute-start(bf16[32,1536]{1,0:T(8,128)(2,1)} %refs_3_.7), channel_id=1, source_target_pairs={{0,254},{2,4},{4,2},{6,8},{8,6},{10,12},{12,10},{14,16},{16,14},{1... | collective-permute-start | bytes 294920 | tf_op jit(solution)/shard_map/ppermute | solution.py:592
  13.4 3.4 %collective-permute-start.1 = (bf16[64,1536]{1,0:T(8,128)(2,1)S(1)}, bf16[64,1536]{1,0:T(8,128)(2,1)S(1)}, u32[]{:S(2)}, u32[]{:S(2)}) collective-permute-start(bf16[64,1536]{1,0:T(8,128)(2,1)S(1)} %shard_map.247), channel_id=1, source_target_pairs={{0,254},{2,4},{4,2},{6,8},{8,6},{10,12},{12,10},{14,16},{16,14},{1... | collective-permute-start | bytes 589832 | tf_op jit(solution)/shard_map/ppermute | solution.py:592
  16.9 1.5 %shard_map.248 = (bf16[32,1664]{1,0:T(8,128)(2,1)S(1)}, bf16[32,1664]{1,0:T(8,128)(2,1)S(1)}, f32[32,1536]{1,0:T(8,128)S(1)}, f32[32,128]{1,0:T(8,128)S(1)}) custom-call(s32[1]{0:T(128)} %bitcast.refs_0_.idx, s32[2,128]{1,0:T(2,128)S(1)} %bitcast.5, s32[128]{0:T(128)S(1)} %copy-done.15, bf16[32,1536]{1,0:T(8,128)(2,1)S(1)} %copy-done.9, ...), custom_call_target="tpu_custom_call" | custom-call | flops 3300000000 | bytes 1867776 | tf_op jit(solution)/shard_map/pallas_call | solution.py:31
  18.6 4.5 %collective-permute-start.7 = (bf16[32,1664]{1,0:T(8,128)(2,1)S(1)}, bf16[32,1664]{1,0:T(8,128)(2,1)S(1)}, u32[]{:S(2)}, u32[]{:S(2)}) collective-permute-start(bf16[32,1664]{1,0:T(8,128)(2,1)S(1)} %get-tuple-element.52), channel_id=1, source_target_pairs={{0,254},{2,4},{4,2},{6,8},{8,6},{10,12},{12,10},{14,16},{16,14},{1... | collective-permute-start | bytes 319496 | tf_op jit(solution)/shard_map/ppermute | solution.py:592
  23.1 5.1 %collective-permute-done.refs_6_.refs_11_ = bf16[64,1536]{1,0:T(8,128)(2,1)S(1)} collective-permute-done((bf16[64,1536]{1,0:T(8,128)(2,1)S(1)}, bf16[64,1536]{1,0:T(8,128)(2,1)S(1)}, u32[]{:S(2)}, u32[]{:S(2)}) %collective-permute-start) | collective-permute-done | bytes 196640 | tf_op jit(solution)/shard_map/ppermute | solution.py:589
  28.2 1.5 %shard_map.249 = (bf16[256,1536]{1,0:T(8,128)(2,1)S(1)}, f32[16,256]{1,0:T(8,128)S(1)}, bf16[32,1536]{1,0:T(8,128)(2,1)S(1)}, bf16[32,1536]{1,0:T(8,128)(2,1)S(1)}) custom-call(s32[1]{0:T(128)} %bitcast.refs_0_.idx, s32[2,128]{1,0:T(2,128)S(1)} %bitcast.3, s32[128]{0:T(128)S(1)} %copy-done.14, bf16[256,1536]{1,0:T(8,128)(2,1)S(1)} %copy-done.1, ...), custom_call_target="tpu_custom_call" | custom-call | flops 2750000128 | bytes 1392640 | tf_op jit(solution)/shard_map/pallas_call | solution.py:31
  30.3 3.5 %collective-permute-start.8 = (bf16[16,1536]{1,0:T(8,128)(2,1)S(1)}, bf16[16,1536]{1,0:T(8,128)(2,1)S(1)}, u32[]{:S(2)}, u32[]{:S(2)}) collective-permute-start(bf16[16,1536]{1,0:T(8,128)(2,1)S(1)} %get-tuple-element.54), channel_id=1, source_target_pairs={{0,2},{2,0},{4,6},{6,4},{8,10},{10,8},{12,14},{14,12},{16,18},{18,... | collective-permute-start | bytes 147464 | tf_op jit(solution)/shard_map/ppermute | solution.py:589
  33.8 4.1 %collective-permute-start.9 = (bf16[16,1536]{1,0:T(8,128)(2,1)S(1)}, bf16[16,1536]{1,0:T(8,128)(2,1)S(1)}, u32[]{:S(2)}, u32[]{:S(2)}) collective-permute-start(bf16[16,1536]{1,0:T(8,128)(2,1)S(1)} %get-tuple-element.55), channel_id=1, source_target_pairs={{0,254},{2,4},{4,2},{6,8},{8,6},{10,12},{12,10},{14,16},{16,14},{1... | collective-permute-start | bytes 147464 | tf_op jit(solution)/shard_map/ppermute | solution.py:592
  38.0 5.1 %collective-permute-done.9.refs_7_.refs_9_ = bf16[16,1536]{1,0:T(8,128)(2,1)S(1)} collective-permute-done((bf16[16,1536]{1,0:T(8,128)(2,1)S(1)}, bf16[16,1536]{1,0:T(8,128)(2,1)S(1)}, u32[]{:S(2)}, u32[]{:S(2)}) %collective-permute-start.9) | collective-permute-done | bytes 49184 | tf_op jit(solution)/shard_map/ppermute | solution.py:592
  44.7 3.5 %collective-permute-done.10.refs_2_ = f32[80,128]{1,0:T(8,128)S(1)} collective-permute-done((f32[80,128]{1,0:T(8,128)S(1)}, f32[80,128]{1,0:T(8,128)S(1)}, u32[]{:S(2)}, u32[]{:S(2)}) %collective-permute-start.10) | collective-permute-done | bytes 40992 | tf_op jit(solution)/shard_map/ppermute | solution.py:657
  48.2 2.0 %shard_map.252 = (f32[256,1536]{1,0:T(8,128)S(1)}, bf16[32,1536]{1,0:T(8,128)(2,1)S(1)}, bf16[64,1664]{1,0:T(8,128)(2,1)S(1)}, bf16[64,1664]{1,0:T(8,128)(2,1)S(...) custom-call(s32[1]{0:T(128)} %bitcast.refs_0_.idx, f32[80,128]{1,0:T(8,128)S(1)} %shard_map.251.refs_1_, ...), custom_call_target="tpu_custom_call" | custom-call | flops 2750000128 | bytes 2211840 | tf_op jit(solution)/shard_map/pallas_call | solution.py:31
  50.6 3.8 %collective-permute-start.13 = (bf16[64,1664]{1,0:T(8,128)(2,1)S(1)}, bf16[64,1664]{1,0:T(8,128)(2,1)S(1)}, u32[]{:S(2)}, u32[]{:S(2)}) collective-permute-start(bf16[64,1664]{1,0:T(8,128)(2,1)S(1)} %get-tuple-element.62), channel_id=1, source_target_pairs={{0,254},{2,4},{4,2},{6,8},{8,6},{10,12},{12,10},{14,16},{16,14},{1... | collective-permute-start | bytes 638984 | tf_op jit(solution)/shard_map/ppermute | solution.py:592
  54.5 1.5 %shard_map.254 = (bf16[256,1536]{1,0:T(8,128)(2,1)}, bf16[32,1536]{1,0:T(8,128)(2,1)}, f32[8,128]{1,0:T(8,128)S(1)}) custom-call(s32[1]{0:T(128)} %bitcast.refs_0_.idx, f32[80,128]{1,0:T(8,128)S(1)} %shard_map.251.refs_1_, f32[80,128]{1,0:T(8,128)S(1)} %collective-permute-done.10.refs_2_, bf16[256,1536]{1,0:T(8,128)(2,1)S(1)} %get-tuple-element.47.refs_1_.refs_3_, ...), custom_call_target="tpu_custom_call" | custom-call | flops 1650000000 | bytes 2244608 | tf_op jit(solution)/shard_map/pallas_call | solution.py:31
  56.1 2.5 %collective-permute-done.16.refs_1_ = f32[8,1536]{1,0:T(8,128)S(1)} collective-permute-done((f32[8,1536]{1,0:T(8,128)S(1)}, f32[8,1536]{1,0:T(8,128)S(1)}, u32[]{:S(2)}, u32[]{:S(2)}) %collective-permute-start.16) | collective-permute-done | bytes 49184 | tf_op jit(solution)/shard_map/ppermute | solution.py:678
  59.8 2.9 %collective-permute-done.17.refs_1_ = f32[8,1536]{1,0:T(8,128)S(1)} collective-permute-done((f32[8,1536]{1,0:T(8,128)S(1)}, f32[8,1536]{1,0:T(8,128)S(1)}, u32[]{:S(2)}, u32[]{:S(2)}) %collective-permute-start.17) | collective-permute-done | bytes 49184 | tf_op jit(solution)/shard_map/ppermute | solution.py:678
  64.4 2.9 %shard_map.255 = (bf16[256,1536]{1,0:T(8,128)(2,1)}, f32[64,1536]{1,0:T(8,128)S(1)}, bf16[64,1536]{1,0:T(8,128)(2,1)S(1)}, bf16[64,1536]{1,0:T(8,128)(2,1)S(1)}) custom-call(s32[1]{0:T(128)} %bitcast.refs_0_.idx, s32[2,128]{1,0:T(2,128)S(1)} %bitcast.4, s32[128]{0:T(128)S(1)} %copy-done.14, bf16[256,1536]{1,0:T(8,128)(2,1)S(1)} %copy-done.1, ...), custom_call_target="tpu_custom_call" | custom-call | flops 4950000128 | bytes 3409920 | tf_op jit(solution)/shard_map/pallas_call | solution.py:31
  67.3 2.1 %collective-permute-done.18.refs_1_ = f32[8,1536]{1,0:T(8,128)S(1)} collective-permute-done((f32[8,1536]{1,0:T(8,128)S(1)}, f32[8,1536]{1,0:T(8,128)S(1)}, u32[]{:S(2)}, u32[]{:S(2)}) %collective-permute-start.18) | collective-permute-done | bytes 49184 | tf_op jit(solution)/shard_map/ppermute | solution.py:678
  70.3 2.8 %shard_map.256 = (bf16[256,1536]{1,0:T(8,128)(2,1)}, bf16[256,1536]{1,0:T(8,128)(2,1)}, f32[32,1536]{1,0:T(8,128)S(1)}, bf16[96,1536]{1,0:T(8,128)(2,1)S(1)}, bf16[96,1536]{1,0:T(8,128)(2,1)S(1)}) custom-call(s32[1]{0:T(128)} %bitcast.refs_0_.idx, s32[2,128]{1,0:T(2,128)S(1)} %bitcast.6, s32[128]{0:T(128)S(1)} %copy-done.15, bf16[32,1536]{1,0:T(8,128)(2,1)S(1)} %copy-done.9, ...), custom_call_target="tpu_custom_call" | custom-call | flops 4950000128 | bytes 2818048 | tf_op jit(solution)/shard_map/pallas_call | solution.py:31
  73.1 1.5 %collective-permute-start.15 = (bf16[96,1536]{1,0:T(8,128)(2,1)S(1)}, bf16[96,1536]{1,0:T(8,128)(2,1)S(1)}, u32[]{:S(2)}, u32[]{:S(2)}) collective-permute-start(bf16[96,1536]{1,0:T(8,128)(2,1)S(1)} %get-tuple-element.74), channel_id=1, source_target_pairs={{0,254},{2,4},{4,2},{6,8},{8,6},{10,12},{12,10},{14,16},{16,14},{1... | collective-permute-start | bytes 884744 | tf_op jit(solution)/shard_map/ppermute | solution.py:592
  74.6 2.4 %collective-permute-start.14 = (bf16[96,1536]{1,0:T(8,128)(2,1)S(1)}, bf16[96,1536]{1,0:T(8,128)(2,1)S(1)}, u32[]{:S(2)}, u32[]{:S(2)}) collective-permute-start(bf16[96,1536]{1,0:T(8,128)(2,1)S(1)} %get-tuple-element.73), channel_id=1, source_target_pairs={{0,2},{2,0},{4,6},{6,4},{8,10},{10,8},{12,14},{14,12},{16,18},{18,... | collective-permute-start | bytes 884744 | tf_op jit(solution)/shard_map/ppermute | solution.py:589
  77.0 2.9 %collective-permute-start.20 = (f32[8,1536]{1,0:T(8,128)S(1)}, f32[8,1536]{1,0:T(8,128)S(1)}, u32[]{:S(2)}, u32[]{:S(2)}) collective-permute-start(f32[8,1536]{1,0:T(8,128)S(1)} %shard_map.260.refs_0_), channel_id=1, source_target_pairs={{0,8},{2,10},{4,12},{6,14},{8,0},{10,2},{12,4},{14,6},{16,24},{18,... | collective-permute-start | bytes 147464 | tf_op jit(solution)/shard_map/ppermute | solution.py:678
  79.9 4.8 %collective-permute-done.20.refs_1_ = f32[8,1536]{1,0:T(8,128)S(1)} collective-permute-done((f32[8,1536]{1,0:T(8,128)S(1)}, f32[8,1536]{1,0:T(8,128)S(1)}, u32[]{:S(2)}, u32[]{:S(2)}) %collective-permute-start.20) | collective-permute-done | bytes 49184 | tf_op jit(solution)/shard_map/ppermute | solution.py:678
  84.8 5.3 %collective-permute-done.21.theirs = f32[8,1536]{1,0:T(8,128)S(1)} collective-permute-done((f32[8,1536]{1,0:T(8,128)S(1)}, f32[8,1536]{1,0:T(8,128)S(1)}, u32[]{:S(2)}, u32[]{:S(2)}) %collective-permute-start.21) | collective-permute-done | bytes 49184 | tf_op jit(solution)/shard_map/ppermute | solution.py:678
  (76 shorter events, 11.1 us)
Async XLA Ops:
  0.6 16.1 %copy-start.2 = (bf16[256,1536]{1,0:T(8,128)(2,1)S(1)}, bf16[256,1536]{1,0:T(8,128)(2,1)}, u32[]{:S(2)}) copy-start(bf16[256,1536]{1,0:T(8,128)(2,1)} %refs_11_.5) | copy-start | bytes 2359300
  0.7 16.1 %copy-start.3 = (bf16[256,1536]{1,0:T(8,128)(2,1)S(1)}, bf16[256,1536]{1,0:T(8,128)(2,1)}, u32[]{:S(2)}) copy-start(bf16[256,1536]{1,0:T(8,128)(2,1)} %refs_12_.5) | copy-start | bytes 2359300
  0.7 16.1 %collective-permute-start.2 = (bf16[32,1536]{1,0:T(8,128)(2,1)}, bf16[32,1536]{1,0:T(8,128)(2,1)S(1)}, u32[]{:S(2)}, u32[]{:S(2)}) collective-permute-start(bf16[32,1536]{1,0:T(8,128)(2,1)} %refs_3_.7), channel_id=1, source_target_pairs={{0,2},{2,0},{4,6},{6,4},{8,10},{10,8},{12,14},{14,12},{16,18},{18,... | collective-permute-start | bytes 294920 | tf_op jit(solution)/shard_map/ppermute | solution.py:589
  2.9 13.9 %collective-permute-start.3 = (bf16[32,1536]{1,0:T(8,128)(2,1)}, bf16[32,1536]{1,0:T(8,128)(2,1)S(1)}, u32[]{:S(2)}, u32[]{:S(2)}) collective-permute-start(bf16[32,1536]{1,0:T(8,128)(2,1)} %refs_3_.7), channel_id=1, source_target_pairs={{0,254},{2,4},{4,2},{6,8},{8,6},{10,12},{12,10},{14,16},{16,14},{1... | collective-permute-start | bytes 294920 | tf_op jit(solution)/shard_map/ppermute | solution.py:592
  13.3 14.9 %collective-permute-start = (bf16[64,1536]{1,0:T(8,128)(2,1)S(1)}, bf16[64,1536]{1,0:T(8,128)(2,1)S(1)}, u32[]{:S(2)}, u32[]{:S(2)}) collective-permute-start(bf16[64,1536]{1,0:T(8,128)(2,1)S(1)} %shard_map.247), channel_id=1, source_target_pairs={{0,2},{2,0},{4,6},{6,4},{8,10},{10,8},{12,14},{14,12},{16,18},{18,... | collective-permute-start | bytes 589832 | tf_op jit(solution)/shard_map/ppermute | solution.py:589
  13.4 14.8 %collective-permute-start.1 = (bf16[64,1536]{1,0:T(8,128)(2,1)S(1)}, bf16[64,1536]{1,0:T(8,128)(2,1)S(1)}, u32[]{:S(2)}, u32[]{:S(2)}) collective-permute-start(bf16[64,1536]{1,0:T(8,128)(2,1)S(1)} %shard_map.247), channel_id=1, source_target_pairs={{0,254},{2,4},{4,2},{6,8},{8,6},{10,12},{12,10},{14,16},{16,14},{1... | collective-permute-start | bytes 589832 | tf_op jit(solution)/shard_map/ppermute | solution.py:592
  18.4 11.5 %collective-permute-start.6 = (bf16[32,1664]{1,0:T(8,128)(2,1)S(1)}, bf16[32,1664]{1,0:T(8,128)(2,1)S(1)}, u32[]{:S(2)}, u32[]{:S(2)}) collective-permute-start(bf16[32,1664]{1,0:T(8,128)(2,1)S(1)} %get-tuple-element.51), channel_id=1, source_target_pairs={{0,2},{2,0},{4,6},{6,4},{8,10},{10,8},{12,14},{14,12},{16,18},{18,... | collective-permute-start | bytes 319496 | tf_op jit(solution)/shard_map/ppermute | solution.py:589
  18.6 11.3 %collective-permute-start.7 = (bf16[32,1664]{1,0:T(8,128)(2,1)S(1)}, bf16[32,1664]{1,0:T(8,128)(2,1)S(1)}, u32[]{:S(2)}, u32[]{:S(2)}) collective-permute-start(bf16[32,1664]{1,0:T(8,128)(2,1)S(1)} %get-tuple-element.52), channel_id=1, source_target_pairs={{0,254},{2,4},{4,2},{6,8},{8,6},{10,12},{12,10},{14,16},{16,14},{1... | collective-permute-start | bytes 319496 | tf_op jit(solution)/shard_map/ppermute | solution.py:592
  29.7 13.3 %collective-permute-start.4 = (bf16[32,1536]{1,0:T(8,128)(2,1)S(1)}, bf16[32,1536]{1,0:T(8,128)(2,1)S(1)}, u32[]{:S(2)}, u32[]{:S(2)}) collective-permute-start(bf16[32,1536]{1,0:T(8,128)(2,1)S(1)} %get-tuple-element.48), channel_id=1, source_target_pairs={{0,2},{2,0},{4,6},{6,4},{8,10},{10,8},{12,14},{14,12},{16,18},{18,... | collective-permute-start | bytes 294920 | tf_op jit(solution)/shard_map/ppermute | solution.py:589
  29.8 13.2 %collective-permute-start.5 = (bf16[32,1536]{1,0:T(8,128)(2,1)S(1)}, bf16[32,1536]{1,0:T(8,128)(2,1)S(1)}, u32[]{:S(2)}, u32[]{:S(2)}) collective-permute-start(bf16[32,1536]{1,0:T(8,128)(2,1)S(1)} %get-tuple-element.49), channel_id=1, source_target_pairs={{0,254},{2,4},{4,2},{6,8},{8,6},{10,12},{12,10},{14,16},{16,14},{1... | collective-permute-start | bytes 294920 | tf_op jit(solution)/shard_map/ppermute | solution.py:592
  30.3 7.7 %collective-permute-start.8 = (bf16[16,1536]{1,0:T(8,128)(2,1)S(1)}, bf16[16,1536]{1,0:T(8,128)(2,1)S(1)}, u32[]{:S(2)}, u32[]{:S(2)}) collective-permute-start(bf16[16,1536]{1,0:T(8,128)(2,1)S(1)} %get-tuple-element.54), channel_id=1, source_target_pairs={{0,2},{2,0},{4,6},{6,4},{8,10},{10,8},{12,14},{14,12},{16,18},{18,... | collective-permute-start | bytes 147464 | tf_op jit(solution)/shard_map/ppermute | solution.py:589
  33.8 9.2 %collective-permute-start.9 = (bf16[16,1536]{1,0:T(8,128)(2,1)S(1)}, bf16[16,1536]{1,0:T(8,128)(2,1)S(1)}, u32[]{:S(2)}, u32[]{:S(2)}) collective-permute-start(bf16[16,1536]{1,0:T(8,128)(2,1)S(1)} %get-tuple-element.55), channel_id=1, source_target_pairs={{0,254},{2,4},{4,2},{6,8},{8,6},{10,12},{12,10},{14,16},{16,14},{1... | collective-permute-start | bytes 147464 | tf_op jit(solution)/shard_map/ppermute | solution.py:592
  44.1 4.1 %collective-permute-start.10 = (f32[80,128]{1,0:T(8,128)S(1)}, f32[80,128]{1,0:T(8,128)S(1)}, u32[]{:S(2)}, u32[]{:S(2)}) collective-permute-start(f32[80,128]{1,0:T(8,128)S(1)} %shard_map.251.refs_1_), channel_id=1, source_target_pairs={{0,1},{1,0},{2,3},{3,2},{4,5},{5,4},{6,7},{7,6},{8,9},{9,8},{10,11... | collective-permute-start | bytes 122888 | tf_op jit(solution)/shard_map/ppermute | solution.py:657
  50.2 4.2 %collective-permute-start.11 = (f32[8,1536]{1,0:T(8,128)S(1)}, f32[8,1536]{1,0:T(8,128)S(1)}, u32[]{:S(2)}, u32[]{:S(2)}) collective-permute-start(f32[8,1536]{1,0:T(8,128)S(1)} %get-tuple-element.57.refs_0_), channel_id=1, source_target_pairs={{0,32},{2,34},{4,36},{6,38},{8,40},{10,42},{12,44},{14,46},{16,48}... | collective-permute-start | bytes 147464 | tf_op jit(solution)/shard_map/ppermute | solution.py:678
  50.3 13.5 %collective-permute-start.12 = (bf16[64,1664]{1,0:T(8,128)(2,1)S(1)}, bf16[64,1664]{1,0:T(8,128)(2,1)S(1)}, u32[]{:S(2)}, u32[]{:S(2)}) collective-permute-start(bf16[64,1664]{1,0:T(8,128)(2,1)S(1)} %get-tuple-element.61), channel_id=1, source_target_pairs={{0,2},{2,0},{4,6},{6,4},{8,10},{10,8},{12,14},{14,12},{16,18},{18,... | collective-permute-start | bytes 638984 | tf_op jit(solution)/shard_map/ppermute | solution.py:589
  50.6 13.2 %collective-permute-start.13 = (bf16[64,1664]{1,0:T(8,128)(2,1)S(1)}, bf16[64,1664]{1,0:T(8,128)(2,1)S(1)}, u32[]{:S(2)}, u32[]{:S(2)}) collective-permute-start(bf16[64,1664]{1,0:T(8,128)(2,1)S(1)} %get-tuple-element.62), channel_id=1, source_target_pairs={{0,254},{2,4},{4,2},{6,8},{8,6},{10,12},{12,10},{14,16},{16,14},{1... | collective-permute-start | bytes 638984 | tf_op jit(solution)/shard_map/ppermute | solution.py:592
  54.4 4.2 %collective-permute-start.16 = (f32[8,1536]{1,0:T(8,128)S(1)}, f32[8,1536]{1,0:T(8,128)S(1)}, u32[]{:S(2)}, u32[]{:S(2)}) collective-permute-start(f32[8,1536]{1,0:T(8,128)S(1)} %shard_map.253.refs_15_.refs_0_), channel_id=1, source_target_pairs={{0,64},{2,66},{4,68},{6,70},{8,72},{10,74},{12,76},{14,78},{16,80}... | collective-permute-start | bytes 147464 | tf_op jit(solution)/shard_map/ppermute | solution.py:678
  58.6 4.2 %collective-permute-start.17 = (f32[8,1536]{1,0:T(8,128)S(1)}, f32[8,1536]{1,0:T(8,128)S(1)}, u32[]{:S(2)}, u32[]{:S(2)}) collective-permute-start(f32[8,1536]{1,0:T(8,128)S(1)} %shard_map.257.refs_0_), channel_id=1, source_target_pairs={{0,4},{2,6},{4,0},{6,2},{8,12},{10,14},{12,8},{14,10},{16,20},{18,... | collective-permute-start | bytes 147464 | tf_op jit(solution)/shard_map/ppermute | solution.py:678
  63.8 5.7 %collective-permute-start.18 = (f32[8,1536]{1,0:T(8,128)S(1)}, f32[8,1536]{1,0:T(8,128)S(1)}, u32[]{:S(2)}, u32[]{:S(2)}) collective-permute-start(f32[8,1536]{1,0:T(8,128)S(1)} %shard_map.258.refs_0_), channel_id=1, source_target_pairs={{0,2},{2,0},{4,6},{6,4},{8,10},{10,8},{12,14},{14,12},{16,18},{18,... | collective-permute-start | bytes 147464 | tf_op jit(solution)/shard_map/ppermute | solution.py:678
  69.5 7.5 %collective-permute-start.19 = (f32[8,1536]{1,0:T(8,128)S(1)}, f32[8,1536]{1,0:T(8,128)S(1)}, u32[]{:S(2)}, u32[]{:S(2)}) collective-permute-start(f32[8,1536]{1,0:T(8,128)S(1)} %shard_map.259.refs_0_), channel_id=1, source_target_pairs={{0,192},{2,194},{4,196},{6,198},{8,200},{10,202},{12,204},{14,206}... | collective-permute-start | bytes 147464 | tf_op jit(solution)/shard_map/ppermute | solution.py:678
  73.1 17.6 %collective-permute-start.15 = (bf16[96,1536]{1,0:T(8,128)(2,1)S(1)}, bf16[96,1536]{1,0:T(8,128)(2,1)S(1)}, u32[]{:S(2)}, u32[]{:S(2)}) collective-permute-start(bf16[96,1536]{1,0:T(8,128)(2,1)S(1)} %get-tuple-element.74), channel_id=1, source_target_pairs={{0,254},{2,4},{4,2},{6,8},{8,6},{10,12},{12,10},{14,16},{16,14},{1... | collective-permute-start | bytes 884744 | tf_op jit(solution)/shard_map/ppermute | solution.py:592
  74.6 16.7 %collective-permute-start.14 = (bf16[96,1536]{1,0:T(8,128)(2,1)S(1)}, bf16[96,1536]{1,0:T(8,128)(2,1)S(1)}, u32[]{:S(2)}, u32[]{:S(2)}) collective-permute-start(bf16[96,1536]{1,0:T(8,128)(2,1)S(1)} %get-tuple-element.73), channel_id=1, source_target_pairs={{0,2},{2,0},{4,6},{6,4},{8,10},{10,8},{12,14},{14,12},{16,18},{18,... | collective-permute-start | bytes 884744 | tf_op jit(solution)/shard_map/ppermute | solution.py:589
  77.0 7.7 %collective-permute-start.20 = (f32[8,1536]{1,0:T(8,128)S(1)}, f32[8,1536]{1,0:T(8,128)S(1)}, u32[]{:S(2)}, u32[]{:S(2)}) collective-permute-start(f32[8,1536]{1,0:T(8,128)S(1)} %shard_map.260.refs_0_), channel_id=1, source_target_pairs={{0,8},{2,10},{4,12},{6,14},{8,0},{10,2},{12,4},{14,6},{16,24},{18,... | collective-permute-start | bytes 147464 | tf_op jit(solution)/shard_map/ppermute | solution.py:678
  84.7 5.4 %collective-permute-start.21 = (f32[8,1536]{1,0:T(8,128)S(1)}, f32[8,1536]{1,0:T(8,128)S(1)}, u32[]{:S(2)}, u32[]{:S(2)}) collective-permute-start(f32[8,1536]{1,0:T(8,128)S(1)} %shard_map.261.mine), channel_id=1, source_target_pairs={{0,28},{2,30},{4,24},{6,26},{8,20},{10,22},{12,16},{14,18},{16,12}... | collective-permute-start | bytes 147464 | tf_op jit(solution)/shard_map/ppermute | solution.py:678
  (16 other events, 128.3 us)

commit v4 on v3

--- a/solution.py
+++ b/solution.py
@@ -101,7 +101,16 @@
     refs[-1][...] = refs[0][...] + refs[1][...]
 
 
-def split_sums(mine, theirs, taps_v, taps_a, gain_v, gain_a):
+def settle(dkv, dq, e, o, dk_out, dv_out, dq_out, token):
+    rows = dq.shape[0]
+    token[...] = jnp.zeros(token.shape, F32)
+    for n, out in enumerate((dk_out, dv_out, dq_out)):
+        s = slice(n * rows, (n + 1) * rows)
+        mine = dkv[s, :] if n < 2 else dq[...]
+        out[...] = (mine + e[s, :].astype(F32) + o[s, :].astype(F32)).astype(BF)
+
+
+def split_sums(mine, theirs, _, taps_v, taps_a, gain_v, gain_a):
     total = mine[...] + theirs[...]
     taps_v[...] = total[0:3]
     gain_v[...] = total[3]
@@ -206,7 +215,7 @@
 
 
 def video_forward(
-    count, idx, window, valid, q, k, v, kve, kvo, _, att, lse, send_e, send_o
+    count, idx, window, valid, q, k, v, kve, kvo, _, att, lse
 ):
     rows = q.shape[0]
     heads = q.shape[1] // HEAD_DIM
@@ -228,26 +237,25 @@
         for h in group:
             c = columns(h)
             att[:, c] = dot(probs[h], near_columns(v, kve, kvo, c, 1), 0, 0).astype(BF)
-    odd = i & 1
-    for send, side in ((send_e, 1 - odd), (send_o, odd)):
-        start = pl.multiple_of(side * (rows - STRIDE), STRIDE)
-        send[...] = att[pl.ds(start, STRIDE), :]
-
-
-def audio_combine(idx, own, own_lse, re, ro, cot, att, total, send_e, send_o):
+
+
+def audio_combine(
+    idx, own, own_lse, re, ro, cot, att_v, att, total, send_e, send_o, first, last
+):
     rows = own.shape[0]
     heads = own.shape[1] // HEAD_DIM
     tail = slice(heads * HEAD_DIM, heads * HEAD_DIM + PAD)
     mine = own_lse[...]
-    first = unpack_stats(re[:, tail])
-    second = unpack_stats(ro[:, tail])
-    peak = jnp.maximum(mine, jnp.maximum(first, second))
+    lse_e = unpack_stats(re[:, tail])
+    lse_o = unpack_stats(ro[:, tail])
+    peak = jnp.maximum(mine, jnp.maximum(lse_e, lse_o))
     whole = peak + jnp.log(
-        jnp.exp(mine - peak) + jnp.exp(first - peak) + jnp.exp(second - peak)
+        jnp.exp(mine - peak) + jnp.exp(lse_e - peak) + jnp.exp(lse_o - peak)
     )
     total[...] = whole
-    wm, we, wo = jnp.exp(mine - whole), jnp.exp(first - whole), jnp.exp(second - whole)
-    odd = (idx[0] & 1) == 1
+    wm, we, wo = jnp.exp(mine - whole), jnp.exp(lse_e - whole), jnp.exp(lse_o - whole)
+    first[...] = jnp.zeros(first.shape, F32)
+    last[...] = jnp.zeros(last.shape, F32)
     for h in range(heads):
         c = columns(h)
         joined = (
@@ -257,10 +265,15 @@
         )
         att[:, c] = joined.astype(BF)
         incoming = cot[:, c].astype(F32)
-        low = jnp.concatenate([joined[0:8], incoming[0:8]], 0)
-        high = jnp.concatenate([joined[rows - 8 :], incoming[rows - 8 :]], 0)
-        send_e[:, c] = jnp.where(odd, low, high).astype(BF)
-        send_o[:, c] = jnp.where(odd, high, low).astype(BF)
+        for edge, pair, only in ((first, 0, 0), (last, rows - 2, rows - 1)):
+            edge[h : h + 1, 0:PAD] = joined[pair : pair + 1]
+            edge[16 + h : 17 + h, 0:PAD] = joined[pair + 1 : pair + 2]
+            edge[h : h + 1, PAD:] = incoming[only : only + 1]
+    odd = idx[0] & 1
+    for send, side in ((send_e, 1 - odd), (send_o, odd)):
+        start = pl.multiple_of(side * (att_v.shape[0] - STRIDE), STRIDE)
+        send[:, 0 : heads * HEAD_DIM] = att_v[pl.ds(start, STRIDE), :]
+        send[:, heads * HEAD_DIM :] = jnp.where(side == 1, last[...], first[...]).astype(BF)
 
 
 class Mix:
@@ -269,10 +282,13 @@
         self.even = (self.i & 1) == 0
         self.has_prev = (self.i > 0).astype(F32)
         self.has_next = (self.i < count - 1).astype(F32)
-        (self.att_v, self.hve, self.hvo, self.cot_v,
-         self.att_a, self.hae, self.hao, self.cot_a,
+        (self.att_v, self.he, self.ho, self.cot_v, self.att_a, self.cot_a,
          self.conv_v, self.conv_a, self.gain_v, self.gain_a) = refs
         self.chunks = self.att_v.shape[0] // STRIDE
+        edges = slice(self.att_v.shape[1], self.att_v.shape[1] + 2 * PAD)
+        self.low = self.before(self.he[:, edges], self.ho[:, edges])
+        self.high = self.after(self.he[:, edges], self.ho[:, edges])
+        self.row = lax.broadcasted_iota(jnp.int32, (8, HEAD_DIM), 0)
 
     def before(self, e, o):
         return jnp.where(self.even, o.astype(F32), e.astype(F32)) * self.has_prev
@@ -282,28 +298,48 @@
 
     def video_att(self, g, c):
         if g < 0:
-            return self.before(self.hve[:, c], self.hvo[:, c])
+            return self.before(self.he[:, c], self.ho[:, c])
         if g >= self.chunks:
-            return self.after(self.hve[:, c], self.hvo[:, c])
+            return self.after(self.he[:, c], self.ho[:, c])
         return self.att_v[g * STRIDE : (g + 1) * STRIDE, c].astype(F32)
 
     def video_cot(self, g, c):
         return self.cot_v[g * STRIDE : (g + 1) * STRIDE, c].astype(F32)
 
-    def extended(self, own, c, part):
-        s = slice(8 * part, 8 * part + 8)
-        low = self.before(self.hae[:, c], self.hao[:, c])[s]
-        high = self.after(self.hae[:, c], self.hao[:, c])[s]
-        return jnp.concatenate([low, own[:, c].astype(F32), high], 0)
+    def placed(self, at, value):
+        return jnp.where(self.row == at, value, 0.0)
+
+    def audio_att(self, c):
+        h = c.start // HEAD_DIM
+        low, high = self.low[:, 0:PAD], self.high[:, 0:PAD]
+        return jnp.concatenate(
+            [
+                self.placed(6, low[h : h + 1]) + self.placed(7, low[16 + h : 17 + h]),
+                self.att_a[:, c].astype(F32),
+                self.placed(0, high[h : h + 1]) + self.placed(1, high[16 + h : 17 + h]),
+            ],
+            0,
+        )
+
+    def audio_cot(self, c):
+        h = c.start // HEAD_DIM
+        return jnp.concatenate(
+            [
+                self.placed(7, self.low[h : h + 1, PAD:]),
+                self.cot_a[:, c].astype(F32),
+                self.placed(0, self.high[h : h + 1, PAD:]),
+            ],
+            0,
+        )
 
     def audio(self, c):
-        att = self.extended(self.att_a, c, 0)
+        att = self.audio_att(c)
         rows = att.shape[0]
         early = pltpu.roll(att, 1, 0)
         late = pltpu.roll(att, rows - 1, 0)
         taps = self.conv_a
         mixed = taps[0:1, c] * early + taps[1:2, c] * att + taps[2:3, c] * late
-        cot = self.extended(self.cot_a, c, 1)
+        cot = self.audio_cot(c)
         return mixed, cot, early, att, late
 
 
@@ -347,11 +383,11 @@
 
 
 def norm_backward(count, width, idx, *refs):
-    mix = Mix(count, idx, refs[2:14])
+    mix = Mix(count, idx, refs[2:12])
     mine, theirs = refs[0], refs[1]
-    total_a = refs[14]
-    grad_v, up_a, send_e, send_o, dots_a, parts = refs[15:21]
-    scale_ref, shrink_ref = refs[21:23]
+    total_a = refs[12]
+    grad_v, up_a, send_e, send_o, dots_a, parts = refs[13:19]
+    scale_ref, shrink_ref = refs[19:21]
     heads = mix.att_v.shape[1] // HEAD_DIM
     sums = mine[...] + theirs[...]
     rows_a = mix.att_a.shape[0]
@@ -434,9 +470,9 @@
 
 
 def outputs(count, width, idx, *refs):
-    mix = Mix(count, idx, refs[2:14])
+    mix = Mix(count, idx, refs[2:12])
     sums = refs[0][...] + refs[1][...]
-    out_v, out_a, token = refs[15:18]
+    out_v, out_a, token = refs[13:16]
     token[...] = jnp.zeros(token.shape, F32)
     heads = mix.att_v.shape[1] // HEAD_DIM
     rows_a = mix.att_a.shape[0]
@@ -462,7 +498,7 @@
 
 
 def video_backward(
-    count, idx, window, valid, q, grad, re, ro, conv, lse, k, v, kve, kvo,
+    count, idx, window, valid, q, grad, re, ro, conv, lse, k, v, kve, kvo, _,
     dq_far, own, send_e, send_o, dq, sems_out,
 ):
     rows = q.shape[0]
@@ -516,7 +552,7 @@
 
 def audio_backward(
     count, idx, window, valid, q, qe, qo, up, re, ro, total, dots, k, v,
-    part_e, part_o, dk_far, dv_far, own, send_e, send_o, dk, dv, sems_out,
+    part_e, part_o, _, dk_far, dv_far, own, send_e, send_o, dk, dv, sems_out,
 ):
     rows = q.shape[0]
     heads = q.shape[1] // HEAD_DIM
@@ -616,37 +652,35 @@
         [packed, packed, ((rows_a, wide), F32), ((rows_a, PAD), F32)],
         [query_audio, qe, qo, key_video, value_video],
         audio_info,
-        3.0,
+        1.5,
         [pltpu.VMEM((PAD, PAD), F32)],
     )
     pe, po = swap_e(send_e), swap_o(send_o)
     keys_values = [key_audio, value_audio, kve, kvo]
-    halo = ((STRIDE, wide), BF)
-    att_v, lse_v, hv_e, hv_o = call(
+    att_v, lse_v = call(
         bind(video_forward, count),
-        [((rows_v, wide), BF), (((heads + 7) // 8 * 8, rows_v), F32), halo, halo],
+        [((rows_v, wide), BF), (((heads + 7) // 8 * 8, rows_v), F32)],
         [query_video] + keys_values + [own_lse],
         video_info,
-        2.5,
+        1.5,
         (),
         (),
         (),
         (5,),
     )
-    hve, hvo = swap_e(hv_e), swap_o(hv_o)
-    halo_a = ((16, wide), BF)
-    att_a, total_a, ha_e, ha_o = call(
+    halo = ((STRIDE, wide + 2 * PAD), BF)
+    att_a, total_a, give_e, give_o = call(
         audio_combine,
-        [((rows_a, wide), BF), ((rows_a, PAD), F32), halo_a, halo_a],
-        [own_part, own_lse, pe, po, cotangent_audio],
+        [((rows_a, wide), BF), ((rows_a, PAD), F32), halo, halo],
+        [own_part, own_lse, pe, po, cotangent_audio, att_v],
         (idx,),
         0.5,
-    )
-    hae, hao = swap_e(ha_e), swap_o(ha_o)
+        [pltpu.VMEM((STRIDE, 2 * PAD), F32)] * 2,
+    )
+    he, ho = swap_e(give_e), swap_o(give_o)
 
     mix_args = [
-        att_v, hve, hvo, cotangent_video,
-        att_a, hae, hao, cotangent_audio,
+        att_v, he, ho, cotangent_video, att_a, cotangent_audio,
         conv_video, conv_audio, gain_video.reshape(1, wide), gain_audio.reshape(1, wide),
     ]
     stats_rows = STRIDE + rows_a + 16
@@ -694,56 +728,68 @@
         (),
         (),
         (),
-        (14,),
+        (12,),
     )
     total = summed(total, 32, token)
-    total = summed(total, 2, re, ro)
+    total = summed(total, 2)
 
     two = ((2 * rows_a, wide), BF)
     dq_v, dkv_own, dkv_e, dkv_o = call(
         bind(video_backward, count),
         [((rows_v, wide), BF), ((2 * rows_a, wide), F32), two, two],
-        [query_video, grad_v, re, ro, conv_video, lse_v] + keys_values,
+        [query_video, grad_v, re, ro, conv_video, lse_v] + keys_values + [total],
         video_info,
-        4.5,
+        3.0,
         [big, sems(1)],
         (),
         (0,),
-    )
+        (10,),
+    )
+    three = ((3 * rows_a, wide), BF)
     total = summed(total, 1, dkv_own)
-    three = ((3 * rows_a, wide), BF)
     dk_v, dv_v, dq_own, give_e, give_o = call(
         bind(audio_backward, count),
         [((rows_v, wide), BF), ((rows_v, wide), BF), ((rows_a, wide), F32), three, three],
         [query_audio, qe, qo, up_a, re, ro, total_a, dots_a, key_video, value_video,
-         dkv_e, dkv_o],
+         dkv_e, dkv_o, total],
         audio_info,
-        4.5,
+        3.0,
         [big] * 2 + [sems(2)],
         (),
         (0, 1),
+        (12,),
     )
     got_e, got_o = swap_e(give_e), swap_o(give_o)
     total = summed(total, 96, dq_own)
-    total = summed(total, 4)
+    total = summed(total, 14)
+    one = ((rows_a, wide), BF)
+    dk_a, dv_a, dq_a, token = call(
+        settle,
+        [one, one, one, ((8, PAD), F32)],
+        [dkv_own, dq_own, got_e, got_o],
+        (),
+        0.5,
+    )
     taps_v, taps_a, gain_v, gain_a = call(
         split_sums,
         [((3, wide), F32), ((3, wide), F32), ((wide,), F32), ((wide,), F32)],
-        [total, moved(total, 14)],
+        [total, moved(total, 4), token],
         (),
         0.5,
-    )
-    own = jnp.concatenate([dkv_own, dq_own], 0)
-    grads = (own + got_e.astype(F32) + got_o.astype(F32)).astype(BF)
+        (),
+        (),
+        (),
+        (2,),
+    )
     return (
         out_v,
         out_a,
         dq_v,
         dk_v,
         dv_v,
-        grads[2 * rows_a :],
-        grads[:rows_a],
-        grads[rows_a : 2 * rows_a],
+        dq_a,
+        dk_a,
+        dv_a,
         taps_v,
         taps_a,
         gain_v,

time: 93.8 us -> 90.4 us (0.964); the launches traced: 92.2 us -> 90.3 us
  starting transfers between devices: 40.9 us -> 37.9 us
  waiting for transfers between devices: 33 us -> 34.2 us
    ppermute x7 -> x6, starting transfers between devices: 8.76 us -> 3.69 us  [swap_e(): return lax.ppermute(x, BLOCKS, even_route)]
    ppermute x7 -> x6, waiting for transfers between devices: 6.76 us -> 11.6 us  [swap_e(): return lax.ppermute(x, BLOCKS, even_route)]
    ppermute x7, starting transfers between devices: 5.84 us -> 8.45 us  [moved(): return lax.ppermute(x, BLOCKS, [(i, i ^ bits) for i in range(count)])]
    ppermute x7 -> x6, waiting for transfers between devices: 5.08 us -> 2.51 us  [swap_o(): return lax.ppermute(x, BLOCKS, odd_route)]
    ppermute x7, waiting for transfers between devices: 17.7 us -> 16.6 us  [moved(): return lax.ppermute(x, BLOCKS, [(i, i ^ bits) for i in range(count)])]
    pallas_call x16 -> x17, Pallas kernels: 14.6 us -> 15.3 us  [call(): pl.pallas_call(kernel, out_shape=[jax.ShapeDtypeStruct(s, d) for s, d in...]
    ppermute x7 -> x6, starting transfers between devices: 25.7 us -> 25.1 us  [swap_o(): return lax.ppermute(x, BLOCKS, odd_route)]
  transfers between devices with their start and end apart: 22 -> 20, of which waited for: 10 -> 11; matrix products, arithmetic and copies ran while one was open for 0% -> 0% of each run, Pallas kernels for 13% -> 9%
where the time goes in v4:
time: 90.4 us; the launch traced here: 90.3 us
  starting transfers between devices  37.9 us (42%)
  waiting for transfers between devices  34.2 us (38%)
  Pallas kernels  15.3 us (17%)
  local copies, waits for them, and re-layouts  1.88 us (2%)
  between operations  0.98 us (1%)
    ppermute x6, starting transfers between devices, swap_o(): return lax.ppermute(x, BLOCKS, odd_route)  25.1 us
    ppermute x7, waiting for transfers between devices, moved(): return lax.ppermute(x, BLOCKS, [(i, i ^ bits) for i in range(count)])  16.6 us
    pallas_call x17, Pallas kernels, call(): pl.pallas_call(kernel, out_shape=[jax.ShapeDtypeStruct(s, d) for s, d in...  15.3 us
    ppermute x6, waiting for transfers between devices, swap_e(): return lax.ppermute(x, BLOCKS, even_route)  11.6 us
    ppermute x7, starting transfers between devices, moved(): return lax.ppermute(x, BLOCKS, [(i, i ^ bits) for i in range(count)])  8.45 us
    ppermute x6, starting transfers between devices, swap_e(): return lax.ppermute(x, BLOCKS, even_route)  3.69 us
    ppermute x1, waiting for transfers between devices, per_device(): lax.ppermute(stats, 'tp', [(i, i ^ 1) for i in range(tp_size)])  3.47 us
    ppermute x6, waiting for transfers between devices, swap_o(): return lax.ppermute(x, BLOCKS, odd_route)  2.51 us
  transfers between devices with their start and end apart: 20, of which 11 were waited for; matrix products, arithmetic and copies ran while one was open for 0% of the time, Pallas kernels for 9%

profile of v4, /device:TPU:2, one launch (start us, length us, event | category | flops | bytes accessed | tf_op | source)
XLA Modules:
  0.0 90.3 jit_solution(16938592215129699470)
XLA Ops:
  0.7 2.2 %collective-permute-start.2 = (bf16[32,1536]{1,0:T(8,128)(2,1)}, bf16[32,1536]{1,0:T(8,128)(2,1)S(1)}, u32[]{:S(2)}, u32[]{:S(2)}) collective-permute-start(bf16[32,1536]{1,0:T(8,128)(2,1)} %refs_3_.7), channel_id=1, source_target_pairs={{0,2},{2,0},{4,6},{6,4},{8,10},{10,8},{12,14},{14,12},{16,18},{18,... | collective-permute-start | bytes 294920 | tf_op jit(solution)/shard_map/ppermute | solution.py:625
  2.9 8.3 %collective-permute-start.3 = (bf16[32,1536]{1,0:T(8,128)(2,1)}, bf16[32,1536]{1,0:T(8,128)(2,1)S(1)}, u32[]{:S(2)}, u32[]{:S(2)}) collective-permute-start(bf16[32,1536]{1,0:T(8,128)(2,1)} %refs_3_.7), channel_id=1, source_target_pairs={{0,254},{2,4},{4,2},{6,8},{8,6},{10,12},{12,10},{14,16},{16,14},{1... | collective-permute-start | bytes 294920 | tf_op jit(solution)/shard_map/ppermute | solution.py:628
  13.4 3.4 %collective-permute-start.1 = (bf16[64,1536]{1,0:T(8,128)(2,1)S(1)}, bf16[64,1536]{1,0:T(8,128)(2,1)S(1)}, u32[]{:S(2)}, u32[]{:S(2)}) collective-permute-start(bf16[64,1536]{1,0:T(8,128)(2,1)S(1)} %shard_map.247), channel_id=1, source_target_pairs={{0,254},{2,4},{4,2},{6,8},{8,6},{10,12},{12,10},{14,16},{16,14},{1... | collective-permute-start | bytes 589832 | tf_op jit(solution)/shard_map/ppermute | solution.py:628
  16.9 1.5 %shard_map.248 = (bf16[32,1664]{1,0:T(8,128)(2,1)S(1)}, bf16[32,1664]{1,0:T(8,128)(2,1)S(1)}, f32[32,1536]{1,0:T(8,128)S(1)}, f32[32,128]{1,0:T(8,128)S(1)}) custom-call(s32[1]{0:T(128)} %bitcast.refs_0_.idx, s32[2,128]{1,0:T(2,128)S(1)} %bitcast.5, s32[128]{0:T(128)S(1)} %copy-done.15, bf16[32,1536]{1,0:T(8,128)(2,1)S(1)} %copy-done.9, ...), custom_call_target="tpu_custom_call" | custom-call | flops 1650000000 | bytes 1867776 | tf_op jit(solution)/shard_map/pallas_call | solution.py:31
  18.6 4.5 %collective-permute-start.5 = (bf16[32,1664]{1,0:T(8,128)(2,1)S(1)}, bf16[32,1664]{1,0:T(8,128)(2,1)S(1)}, u32[]{:S(2)}, u32[]{:S(2)}) collective-permute-start(bf16[32,1664]{1,0:T(8,128)(2,1)S(1)} %get-tuple-element.52), channel_id=1, source_target_pairs={{0,254},{2,4},{4,2},{6,8},{8,6},{10,12},{12,10},{14,16},{16,14},{1... | collective-permute-start | bytes 319496 | tf_op jit(solution)/shard_map/ppermute | solution.py:628
  23.1 5.1 %collective-permute-done.refs_6_.refs_11_ = bf16[64,1536]{1,0:T(8,128)(2,1)S(1)} collective-permute-done((bf16[64,1536]{1,0:T(8,128)(2,1)S(1)}, bf16[64,1536]{1,0:T(8,128)(2,1)S(1)}, u32[]{:S(2)}, u32[]{:S(2)}) %collective-permute-start) | collective-permute-done | bytes 196640 | tf_op jit(solution)/shard_map/ppermute | solution.py:625
  28.2 1.4 %shard_map.249 = (bf16[256,1536]{1,0:T(8,128)(2,1)S(1)}, f32[16,256]{1,0:T(8,128)S(1)}) custom-call(s32[1]{0:T(128)} %bitcast.refs_0_.idx, s32[2,128]{1,0:T(2,128)S(1)} %bitcast.3, s32[128]{0:T(128)S(1)} %copy-done.14, bf16[256,1536]{1,0:T(8,128)(2,1)S(1)} %copy-done.1, bf16[32,1536]{1,0:T(8,128)(2,1)S(1)} %copy-done.6, bf16[32,1536]{1,0:T(8,128)(2,1)S(1)} %copy-done.8, ...), custom_call_target="tpu_custom_call" | custom-call | flops 1650000000 | bytes 1392640 | tf_op jit(solution)/shard_map/pallas_call | solution.py:31
  30.2 3.3 %collective-permute-start.7 = (bf16[32,1792]{1,0:T(8,128)(2,1)S(1)}, bf16[32,1792]{1,0:T(8,128)(2,1)S(1)}, u32[]{:S(2)}, u32[]{:S(2)}) collective-permute-start(bf16[32,1792]{1,0:T(8,128)(2,1)S(1)} %get-tuple-element.54), channel_id=1, source_target_pairs={{0,254},{2,4},{4,2},{6,8},{8,6},{10,12},{12,10},{14,16},{16,14},{1... | collective-permute-start | bytes 344072 | tf_op jit(solution)/shard_map/ppermute | solution.py:628
  33.5 5.1 %collective-permute-done.6.refs_2_.refs_4_ = bf16[32,1792]{1,0:T(8,128)(2,1)S(1)} collective-permute-done((bf16[32,1792]{1,0:T(8,128)(2,1)S(1)}, bf16[32,1792]{1,0:T(8,128)(2,1)S(1)}, u32[]{:S(2)}, u32[]{:S(2)}) %collective-permute-start.6) | collective-permute-done | bytes 114720 | tf_op jit(solution)/shard_map/ppermute | solution.py:625
  38.6 2.5 %collective-permute-done.7.refs_3_.refs_5_ = bf16[32,1792]{1,0:T(8,128)(2,1)S(1)} collective-permute-done((bf16[32,1792]{1,0:T(8,128)(2,1)S(1)}, bf16[32,1792]{1,0:T(8,128)(2,1)S(1)}, u32[]{:S(2)}, u32[]{:S(2)}) %collective-permute-start.7) | collective-permute-done | bytes 114720 | tf_op jit(solution)/shard_map/ppermute | solution.py:628
  42.8 3.5 %collective-permute-done.8.refs_2_ = f32[80,128]{1,0:T(8,128)S(1)} collective-permute-done((f32[80,128]{1,0:T(8,128)S(1)}, f32[80,128]{1,0:T(8,128)S(1)}, u32[]{:S(2)}, u32[]{:S(2)}) %collective-permute-start.8) | collective-permute-done | bytes 40992 | tf_op jit(solution)/shard_map/ppermute | solution.py:691
  46.2 2.0 %shard_map.252 = (f32[256,1536]{1,0:T(8,128)S(1)}, bf16[32,1536]{1,0:T(8,128)(2,1)S(1)}, bf16[64,1664]{1,0:T(8,128)(2,1)S(1)}, bf16[64,1664]{1,0:T(8,128)(2,1)S(...) custom-call(s32[1]{0:T(128)} %bitcast.refs_0_.idx, f32[80,128]{1,0:T(8,128)S(1)} %shard_map.251.refs_1_, ...), custom_call_target="tpu_custom_call" | custom-call | flops 2750000128 | bytes 2146304 | tf_op jit(solution)/shard_map/pallas_call | solution.py:31
  48.4 3.2 %collective-permute-start.11 = (bf16[64,1664]{1,0:T(8,128)(2,1)S(1)}, bf16[64,1664]{1,0:T(8,128)(2,1)S(1)}, u32[]{:S(2)}, u32[]{:S(2)}) collective-permute-start(bf16[64,1664]{1,0:T(8,128)(2,1)S(1)} %get-tuple-element.62), channel_id=1, source_target_pairs={{0,254},{2,4},{4,2},{6,8},{8,6},{10,12},{12,10},{14,16},{16,14},{1... | collective-permute-start | bytes 638984 | tf_op jit(solution)/shard_map/ppermute | solution.py:628
  51.9 1.5 %shard_map.254 = (bf16[256,1536]{1,0:T(8,128)(2,1)}, bf16[32,1536]{1,0:T(8,128)(2,1)}, f32[8,128]{1,0:T(8,128)S(1)}) custom-call(s32[1]{0:T(128)} %bitcast.refs_0_.idx, f32[80,128]{1,0:T(8,128)S(1)} %shard_map.251.refs_1_, f32[80,128]{1,0:T(8,128)S(1)} %collective-permute-done.8.refs_2_, bf16[256,1536]{1,0:T(8,128)(2,1)S(1)} %get-tuple-element.49.att_v.refs_1_.refs_3_, ...), custom_call_target="tpu_custom_call" | custom-call | flops 1650000000 | bytes 2179072 | tf_op jit(solution)/shard_map/pallas_call | solution.py:31
  53.5 2.5 %collective-permute-done.12.refs_1_ = f32[8,1536]{1,0:T(8,128)S(1)} collective-permute-done((f32[8,1536]{1,0:T(8,128)S(1)}, f32[8,1536]{1,0:T(8,128)S(1)}, u32[]{:S(2)}, u32[]{:S(2)}) %collective-permute-start.12) | collective-permute-done | bytes 49184 | tf_op jit(solution)/shard_map/ppermute | solution.py:712
  56.0 1.9 %collective-permute-start.13 = (f32[8,1536]{1,0:T(8,128)S(1)}, f32[8,1536]{1,0:T(8,128)S(1)}, u32[]{:S(2)}, u32[]{:S(2)}) collective-permute-start(f32[8,1536]{1,0:T(8,128)S(1)} %shard_map.255.refs_0_), channel_id=1, source_target_pairs={{0,4},{2,6},{4,0},{6,2},{8,12},{10,14},{12,8},{14,10},{16,20},{18,... | collective-permute-start | bytes 147464 | tf_op jit(solution)/shard_map/ppermute | solution.py:712
  57.9 2.3 %collective-permute-done.13.refs_1_ = f32[8,1536]{1,0:T(8,128)S(1)} collective-permute-done((f32[8,1536]{1,0:T(8,128)S(1)}, f32[8,1536]{1,0:T(8,128)S(1)}, u32[]{:S(2)}, u32[]{:S(2)}) %collective-permute-start.13) | collective-permute-done | bytes 49184 | tf_op jit(solution)/shard_map/ppermute | solution.py:712
  60.6 1.5 %collective-permute-done.10.refs_5_.refs_7_ = bf16[64,1664]{1,0:T(8,128)(2,1)S(1)} collective-permute-done((bf16[64,1664]{1,0:T(8,128)(2,1)S(1)}, bf16[64,1664]{1,0:T(8,128)(2,1)S(1)}, u32[]{:S(2)}, u32[]{:S(2)}) %collective-permute-start.10) | collective-permute-done | bytes 213024 | tf_op jit(solution)/shard_map/ppermute | solution.py:625
  62.1 2.9 %shard_map.257 = (bf16[256,1536]{1,0:T(8,128)(2,1)}, f32[64,1536]{1,0:T(8,128)S(1)}, bf16[64,1536]{1,0:T(8,128)(2,1)S(1)}, bf16[64,1536]{1,0:T(8,128)(2,1)S(1)}) custom-call(s32[1]{0:T(128)} %bitcast.refs_0_.idx, s32[2,128]{1,0:T(2,128)S(1)} %bitcast.4, s32[128]{0:T(128)S(1)} %copy-done.14, bf16[256,1536]{1,0:T(8,128)(2,1)S(1)} %copy-done.1, ...), custom_call_target="tpu_custom_call" | custom-call | flops 3300000000 | bytes 3459072 | tf_op jit(solution)/shard_map/pallas_call | solution.py:31
  65.9 2.8 %shard_map.259 = (bf16[256,1536]{1,0:T(8,128)(2,1)}, bf16[256,1536]{1,0:T(8,128)(2,1)}, f32[32,1536]{1,0:T(8,128)S(1)}, bf16[96,1536]{1,0:T(8,128)(2,1)S(1)}, bf16[96,1536]{1,0:T(8,128)(2,1)S(1)}) custom-call(s32[1]{0:T(128)} %bitcast.refs_0_.idx, s32[2,128]{1,0:T(2,128)S(1)} %bitcast.6, s32[128]{0:T(128)S(1)} %copy-done.15, bf16[32,1536]{1,0:T(8,128)(2,1)S(1)} %copy-done.9, ...), custom_call_target="tpu_custom_call" | custom-call | flops 3300000000 | bytes 2867200 | tf_op jit(solution)/shard_map/pallas_call | solution.py:31
  69.7 2.5 %collective-permute-start.16 = (bf16[96,1536]{1,0:T(8,128)(2,1)S(1)}, bf16[96,1536]{1,0:T(8,128)(2,1)S(1)}, u32[]{:S(2)}, u32[]{:S(2)}) collective-permute-start(bf16[96,1536]{1,0:T(8,128)(2,1)S(1)} %get-tuple-element.75), channel_id=1, source_target_pairs={{0,254},{2,4},{4,2},{6,8},{8,6},{10,12},{12,10},{14,16},{16,14},{1... | collective-permute-start | bytes 884744 | tf_op jit(solution)/shard_map/ppermute | solution.py:628
  73.3 4.6 %collective-permute-done.17.refs_1_ = f32[8,1536]{1,0:T(8,128)S(1)} collective-permute-done((f32[8,1536]{1,0:T(8,128)S(1)}, f32[8,1536]{1,0:T(8,128)S(1)}, u32[]{:S(2)}, u32[]{:S(2)}) %collective-permute-start.17) | collective-permute-done | bytes 49184 | tf_op jit(solution)/shard_map/ppermute | solution.py:712
  78.3 5.0 %collective-permute-done.18.refs_1_ = f32[8,1536]{1,0:T(8,128)S(1)} collective-permute-done((f32[8,1536]{1,0:T(8,128)S(1)}, f32[8,1536]{1,0:T(8,128)S(1)}, u32[]{:S(2)}, u32[]{:S(2)}) %collective-permute-start.18) | collective-permute-done | bytes 49184 | tf_op jit(solution)/shard_map/ppermute | solution.py:712
  83.3 4.3 %collective-permute-start.19 = (f32[8,1536]{1,0:T(8,128)S(1)}, f32[8,1536]{1,0:T(8,128)S(1)}, u32[]{:S(2)}, u32[]{:S(2)}) collective-permute-start(f32[8,1536]{1,0:T(8,128)S(1)} %shard_map.262.mine), channel_id=1, source_target_pairs={{0,8},{2,10},{4,12},{6,14},{8,0},{10,2},{12,4},{14,6},{16,24},{18,... | collective-permute-start | bytes 147464 | tf_op jit(solution)/shard_map/ppermute | solution.py:712
  (71 shorter events, 11.6 us)
Async XLA Ops:
  0.6 16.1 %copy-start.2 = (bf16[256,1536]{1,0:T(8,128)(2,1)S(1)}, bf16[256,1536]{1,0:T(8,128)(2,1)}, u32[]{:S(2)}) copy-start(bf16[256,1536]{1,0:T(8,128)(2,1)} %refs_11_.1) | copy-start | bytes 2359300
  0.7 16.1 %copy-start.3 = (bf16[256,1536]{1,0:T(8,128)(2,1)S(1)}, bf16[256,1536]{1,0:T(8,128)(2,1)}, u32[]{:S(2)}) copy-start(bf16[256,1536]{1,0:T(8,128)(2,1)} %refs_12_.1) | copy-start | bytes 2359300
  0.7 16.1 %collective-permute-start.2 = (bf16[32,1536]{1,0:T(8,128)(2,1)}, bf16[32,1536]{1,0:T(8,128)(2,1)S(1)}, u32[]{:S(2)}, u32[]{:S(2)}) collective-permute-start(bf16[32,1536]{1,0:T(8,128)(2,1)} %refs_3_.7), channel_id=1, source_target_pairs={{0,2},{2,0},{4,6},{6,4},{8,10},{10,8},{12,14},{14,12},{16,18},{18,... | collective-permute-start | bytes 294920 | tf_op jit(solution)/shard_map/ppermute | solution.py:625
  2.9 13.9 %collective-permute-start.3 = (bf16[32,1536]{1,0:T(8,128)(2,1)}, bf16[32,1536]{1,0:T(8,128)(2,1)S(1)}, u32[]{:S(2)}, u32[]{:S(2)}) collective-permute-start(bf16[32,1536]{1,0:T(8,128)(2,1)} %refs_3_.7), channel_id=1, source_target_pairs={{0,254},{2,4},{4,2},{6,8},{8,6},{10,12},{12,10},{14,16},{16,14},{1... | collective-permute-start | bytes 294920 | tf_op jit(solution)/shard_map/ppermute | solution.py:628
  13.2 14.9 %collective-permute-start = (bf16[64,1536]{1,0:T(8,128)(2,1)S(1)}, bf16[64,1536]{1,0:T(8,128)(2,1)S(1)}, u32[]{:S(2)}, u32[]{:S(2)}) collective-permute-start(bf16[64,1536]{1,0:T(8,128)(2,1)S(1)} %shard_map.247), channel_id=1, source_target_pairs={{0,2},{2,0},{4,6},{6,4},{8,10},{10,8},{12,14},{14,12},{16,18},{18,... | collective-permute-start | bytes 589832 | tf_op jit(solution)/shard_map/ppermute | solution.py:625
  13.4 14.8 %collective-permute-start.1 = (bf16[64,1536]{1,0:T(8,128)(2,1)S(1)}, bf16[64,1536]{1,0:T(8,128)(2,1)S(1)}, u32[]{:S(2)}, u32[]{:S(2)}) collective-permute-start(bf16[64,1536]{1,0:T(8,128)(2,1)S(1)} %shard_map.247), channel_id=1, source_target_pairs={{0,254},{2,4},{4,2},{6,8},{8,6},{10,12},{12,10},{14,16},{16,14},{1... | collective-permute-start | bytes 589832 | tf_op jit(solution)/shard_map/ppermute | solution.py:628
  18.4 11.3 %collective-permute-start.4 = (bf16[32,1664]{1,0:T(8,128)(2,1)S(1)}, bf16[32,1664]{1,0:T(8,128)(2,1)S(1)}, u32[]{:S(2)}, u32[]{:S(2)}) collective-permute-start(bf16[32,1664]{1,0:T(8,128)(2,1)S(1)} %get-tuple-element.51), channel_id=1, source_target_pairs={{0,2},{2,0},{4,6},{6,4},{8,10},{10,8},{12,14},{14,12},{16,18},{18,... | collective-permute-start | bytes 319496 | tf_op jit(solution)/shard_map/ppermute | solution.py:625
  18.6 11.1 %collective-permute-start.5 = (bf16[32,1664]{1,0:T(8,128)(2,1)S(1)}, bf16[32,1664]{1,0:T(8,128)(2,1)S(1)}, u32[]{:S(2)}, u32[]{:S(2)}) collective-permute-start(bf16[32,1664]{1,0:T(8,128)(2,1)S(1)} %get-tuple-element.52), channel_id=1, source_target_pairs={{0,254},{2,4},{4,2},{6,8},{8,6},{10,12},{12,10},{14,16},{16,14},{1... | collective-permute-start | bytes 319496 | tf_op jit(solution)/shard_map/ppermute | solution.py:628
  29.7 11.4 %copy-start = (bf16[256,1536]{1,0:T(8,128)(2,1)S(1)}, bf16[256,1536]{1,0:T(8,128)(2,1)}, u32[]{:S(2)}) copy-start(bf16[256,1536]{1,0:T(8,128)(2,1)} %refs_6_.7) | copy-start | bytes 2359300
  29.7 11.4 %copy-start.10 = (f32[3,1536]{1,0:T(4,128)S(1)}, f32[3,1536]{1,0:T(4,128)}, u32[]{:S(2)}) copy-start(f32[3,1536]{1,0:T(4,128)} %refs_10_.4) | copy-start | bytes 55300
  30.1 8.5 %collective-permute-start.6 = (bf16[32,1792]{1,0:T(8,128)(2,1)S(1)}, bf16[32,1792]{1,0:T(8,128)(2,1)S(1)}, u32[]{:S(2)}, u32[]{:S(2)}) collective-permute-start(bf16[32,1792]{1,0:T(8,128)(2,1)S(1)} %get-tuple-element.53), channel_id=1, source_target_pairs={{0,2},{2,0},{4,6},{6,4},{8,10},{10,8},{12,14},{14,12},{16,18},{18,... | collective-permute-start | bytes 344072 | tf_op jit(solution)/shard_map/ppermute | solution.py:625
  30.2 10.9 %collective-permute-start.7 = (bf16[32,1792]{1,0:T(8,128)(2,1)S(1)}, bf16[32,1792]{1,0:T(8,128)(2,1)S(1)}, u32[]{:S(2)}, u32[]{:S(2)}) collective-permute-start(bf16[32,1792]{1,0:T(8,128)(2,1)S(1)} %get-tuple-element.54), channel_id=1, source_target_pairs={{0,254},{2,4},{4,2},{6,8},{8,6},{10,12},{12,10},{14,16},{16,14},{1... | collective-permute-start | bytes 344072 | tf_op jit(solution)/shard_map/ppermute | solution.py:628
  42.1 4.1 %collective-permute-start.8 = (f32[80,128]{1,0:T(8,128)S(1)}, f32[80,128]{1,0:T(8,128)S(1)}, u32[]{:S(2)}, u32[]{:S(2)}) collective-permute-start(f32[80,128]{1,0:T(8,128)S(1)} %shard_map.251.refs_1_), channel_id=1, source_target_pairs={{0,1},{1,0},{2,3},{3,2},{4,5},{5,4},{6,7},{7,6},{8,9},{9,8},{10,11... | collective-permute-start | bytes 122888 | tf_op jit(solution)/shard_map/ppermute | solution.py:691
  48.2 3.4 %collective-permute-start.9 = (f32[8,1536]{1,0:T(8,128)S(1)}, f32[8,1536]{1,0:T(8,128)S(1)}, u32[]{:S(2)}, u32[]{:S(2)}) collective-permute-start(f32[8,1536]{1,0:T(8,128)S(1)} %get-tuple-element.57.refs_0_), channel_id=1, source_target_pairs={{0,32},{2,34},{4,36},{6,38},{8,40},{10,42},{12,44},{14,46},{16,48}... | collective-permute-start | bytes 147464 | tf_op jit(solution)/shard_map/ppermute | solution.py:712
  48.3 13.7 %collective-permute-start.10 = (bf16[64,1664]{1,0:T(8,128)(2,1)S(1)}, bf16[64,1664]{1,0:T(8,128)(2,1)S(1)}, u32[]{:S(2)}, u32[]{:S(2)}) collective-permute-start(bf16[64,1664]{1,0:T(8,128)(2,1)S(1)} %get-tuple-element.61), channel_id=1, source_target_pairs={{0,2},{2,0},{4,6},{6,4},{8,10},{10,8},{12,14},{14,12},{16,18},{18,... | collective-permute-start | bytes 638984 | tf_op jit(solution)/shard_map/ppermute | solution.py:625
  48.4 13.6 %collective-permute-start.11 = (bf16[64,1664]{1,0:T(8,128)(2,1)S(1)}, bf16[64,1664]{1,0:T(8,128)(2,1)S(1)}, u32[]{:S(2)}, u32[]{:S(2)}) collective-permute-start(bf16[64,1664]{1,0:T(8,128)(2,1)S(1)} %get-tuple-element.62), channel_id=1, source_target_pairs={{0,254},{2,4},{4,2},{6,8},{8,6},{10,12},{12,10},{14,16},{16,14},{1... | collective-permute-start | bytes 638984 | tf_op jit(solution)/shard_map/ppermute | solution.py:628
  51.6 4.4 %collective-permute-start.12 = (f32[8,1536]{1,0:T(8,128)S(1)}, f32[8,1536]{1,0:T(8,128)S(1)}, u32[]{:S(2)}, u32[]{:S(2)}) collective-permute-start(f32[8,1536]{1,0:T(8,128)S(1)} %shard_map.253.refs_13_.refs_0_), channel_id=1, source_target_pairs={{0,64},{2,66},{4,68},{6,70},{8,72},{10,74},{12,76},{14,78},{16,80}... | collective-permute-start | bytes 147464 | tf_op jit(solution)/shard_map/ppermute | solution.py:712
  56.0 4.2 %collective-permute-start.13 = (f32[8,1536]{1,0:T(8,128)S(1)}, f32[8,1536]{1,0:T(8,128)S(1)}, u32[]{:S(2)}, u32[]{:S(2)}) collective-permute-start(f32[8,1536]{1,0:T(8,128)S(1)} %shard_map.255.refs_0_), channel_id=1, source_target_pairs={{0,4},{2,6},{4,0},{6,2},{8,12},{10,14},{12,8},{14,10},{16,20},{18,... | collective-permute-start | bytes 147464 | tf_op jit(solution)/shard_map/ppermute | solution.py:712
  60.2 5.7 %collective-permute-start.14 = (f32[8,1536]{1,0:T(8,128)S(1)}, f32[8,1536]{1,0:T(8,128)S(1)}, u32[]{:S(2)}, u32[]{:S(2)}) collective-permute-start(f32[8,1536]{1,0:T(8,128)S(1)} %shard_map.256.refs_13_.refs_0_), channel_id=1, source_target_pairs={{0,2},{2,0},{4,6},{6,4},{8,10},{10,8},{12,14},{14,12},{16,18},{18,... | collective-permute-start | bytes 147464 | tf_op jit(solution)/shard_map/ppermute | solution.py:712
  68.7 18.9 %collective-permute-start.15 = (bf16[96,1536]{1,0:T(8,128)(2,1)S(1)}, bf16[96,1536]{1,0:T(8,128)(2,1)S(1)}, u32[]{:S(2)}, u32[]{:S(2)}) collective-permute-start(bf16[96,1536]{1,0:T(8,128)(2,1)S(1)} %get-tuple-element.74), channel_id=1, source_target_pairs={{0,2},{2,0},{4,6},{6,4},{8,10},{10,8},{12,14},{14,12},{16,18},{18,... | collective-permute-start | bytes 884744 | tf_op jit(solution)/shard_map/ppermute | solution.py:625
  69.7 17.9 %collective-permute-start.16 = (bf16[96,1536]{1,0:T(8,128)(2,1)S(1)}, bf16[96,1536]{1,0:T(8,128)(2,1)S(1)}, u32[]{:S(2)}, u32[]{:S(2)}) collective-permute-start(bf16[96,1536]{1,0:T(8,128)(2,1)S(1)} %get-tuple-element.75), channel_id=1, source_target_pairs={{0,254},{2,4},{4,2},{6,8},{8,6},{10,12},{12,10},{14,16},{16,14},{1... | collective-permute-start | bytes 884744 | tf_op jit(solution)/shard_map/ppermute | solution.py:628
  72.1 5.8 %collective-permute-start.17 = (f32[8,1536]{1,0:T(8,128)S(1)}, f32[8,1536]{1,0:T(8,128)S(1)}, u32[]{:S(2)}, u32[]{:S(2)}) collective-permute-start(f32[8,1536]{1,0:T(8,128)S(1)} %shard_map.258.refs_15_.refs_0_), channel_id=1, source_target_pairs={{0,192},{2,194},{4,196},{6,198},{8,200},{10,202},{12,204},{14,206}... | collective-permute-start | bytes 147464 | tf_op jit(solution)/shard_map/ppermute | solution.py:712
  77.9 5.4 %collective-permute-start.18 = (f32[8,1536]{1,0:T(8,128)S(1)}, f32[8,1536]{1,0:T(8,128)S(1)}, u32[]{:S(2)}, u32[]{:S(2)}) collective-permute-start(f32[8,1536]{1,0:T(8,128)S(1)} %shard_map.261.refs_0_), channel_id=1, source_target_pairs={{0,28},{2,30},{4,24},{6,26},{8,20},{10,22},{12,16},{14,18},{16,12}... | collective-permute-start | bytes 147464 | tf_op jit(solution)/shard_map/ppermute | solution.py:712
  83.3 6.3 %collective-permute-start.19 = (f32[8,1536]{1,0:T(8,128)S(1)}, f32[8,1536]{1,0:T(8,128)S(1)}, u32[]{:S(2)}, u32[]{:S(2)}) collective-permute-start(f32[8,1536]{1,0:T(8,128)S(1)} %shard_map.262.mine), channel_id=1, source_target_pairs={{0,8},{2,10},{4,12},{6,14},{8,0},{10,2},{12,4},{14,6},{16,24},{18,... | collective-permute-start | bytes 147464 | tf_op jit(solution)/shard_map/ppermute | solution.py:712
  (14 other events, 90.6 us)

commit v5 on v4

--- a/solution.py
+++ b/solution.py
@@ -177,8 +177,7 @@
 
 
 def audio_forward(
-    count, idx, window, valid, q, qe, qo, k, v, send_e, send_o, own, own_lse,
-    rows_lse,
+    count, idx, window, valid, q, qe, qo, k, v, send_e, send_o, own, own_lse, rows_lse, kept,
 ):
     rows = q.shape[0]
     heads = q.shape[1] // HEAD_DIM
@@ -197,6 +196,7 @@
             probs[h] = (weight * (1.0 / total)).astype(BF)
         for h in group:
             c = columns(h)
+            kept[h * k.shape[0] : (h + 1) * k.shape[0], :] = probs[h]
             part = dot(probs[h], v[:, c], 0, 0)
             own[:, c] = part[:rows]
             send_e[:, c] = part[rows : 2 * rows].astype(BF)
@@ -215,13 +215,12 @@
 
 
 def video_forward(
-    count, idx, window, valid, q, k, v, kve, kvo, _, att, lse
+    count, idx, window, valid, q, k, v, kve, kvo, _, att, kept
 ):
     rows = q.shape[0]
     heads = q.shape[1] // HEAD_DIM
     i = idx[0]
     bias = video_bias(i, count, window, valid, rows, k.shape[0])
-    lse[...] = jnp.zeros(lse.shape, F32)
     for group in groups(heads, heads):
         scores, probs = {}, {}
         for h in group:
@@ -232,8 +231,8 @@
             peak = jnp.max(scores[h], 0, keepdims=True)
             weight = jnp.exp(scores[h] - peak)
             total = jnp.sum(weight, 0, keepdims=True)
-            lse[h : h + 1, :] = peak + jnp.log(total)
             probs[h] = (weight * (1.0 / total)).astype(BF)
+            kept[h * weight.shape[0] : (h + 1) * weight.shape[0], :] = probs[h]
         for h in group:
             c = columns(h)
             att[:, c] = dot(probs[h], near_columns(v, kve, kvo, c, 1), 0, 0).astype(BF)
@@ -343,28 +342,46 @@
         return mixed, cot, early, att, late
 
 
-def row_sums(count, idx, *refs):
-    mix = Mix(count, idx, refs[:-1])
-    stats = refs[-1]
-    heads = mix.att_v.shape[1] // HEAD_DIM
-    rows_a = mix.att_a.shape[0] + 16
+def video_sums(chunks, att, cot, conv, gain, heads, tile):
     lane = lax.broadcasted_iota(jnp.int32, (STRIDE, PAD), 1)
-    tile = jnp.zeros((STRIDE, PAD), F32)
-    taps = mix.conv_v
-    for g in range(mix.chunks):
+    for g in chunks:
         square = jnp.zeros((STRIDE, HEAD_DIM), F32)
         inner = jnp.zeros((STRIDE, HEAD_DIM), F32)
         for h in range(heads):
             c = columns(h)
             mixed = (
-                taps[0:1, c] * mix.video_att(g - 1, c)
-                + taps[1:2, c] * mix.video_att(g, c)
-                + taps[2:3, c] * mix.video_att(g + 1, c)
+                conv[0:1, c] * att(g - 1, c)
+                + conv[1:2, c] * att(g, c)
+                + conv[2:3, c] * att(g + 1, c)
             )
             square += mixed * mixed
-            inner += mix.video_cot(g, c) * mix.gain_v[0:1, c] * mixed
+            inner += cot(g, c) * gain[0:1, c] * mixed
         tile = jnp.where(lane == g, jnp.sum(square, 1, keepdims=True), tile)
         tile = jnp.where(lane == g + 16, jnp.sum(inner, 1, keepdims=True), tile)
+    return tile
+
+
+def middle_sums(att_v, cot_v, conv, gain, out):
+    def chunk(ref):
+        return lambda g, c: ref[g * STRIDE : (g + 1) * STRIDE, c].astype(F32)
+
+    chunks = att_v.shape[0] // STRIDE
+    heads = att_v.shape[1] // HEAD_DIM
+    out[...] = video_sums(
+        range(1, chunks - 1), chunk(att_v), chunk(cot_v), conv, gain, heads,
+        jnp.zeros((STRIDE, PAD), F32),
+    )
+
+
+def row_sums(count, idx, *refs):
+    mix = Mix(count, idx, refs[1:-1])
+    stats = refs[-1]
+    heads = mix.att_v.shape[1] // HEAD_DIM
+    rows_a = mix.att_a.shape[0] + 16
+    tile = video_sums(
+        (0, mix.chunks - 1), mix.video_att, mix.video_cot, mix.conv_v, mix.gain_v, heads,
+        refs[0][...],
+    )
     lane_a = lax.broadcasted_iota(jnp.int32, (rows_a, PAD), 1)
     square = jnp.zeros((rows_a, HEAD_DIM), F32)
     inner = jnp.zeros((rows_a, HEAD_DIM), F32)
@@ -498,7 +515,7 @@
 
 
 def video_backward(
-    count, idx, window, valid, q, grad, re, ro, conv, lse, k, v, kve, kvo, _,
+    count, idx, q, grad, re, ro, conv, kept, k, v, kve, kvo, _,
     dq_far, own, send_e, send_o, dq, sems_out,
 ):
     rows = q.shape[0]
@@ -509,14 +526,9 @@
     even = (i & 1) == 0
     has_prev = (i > 0).astype(F32)
     has_next = (i < count - 1).astype(F32)
-    bias = video_bias(i, count, window, valid, rows, near)
     halo = slice(near, near + STRIDE)
     for group in groups(heads, CHUNK):
-        upstream, scores, prob_grad, prob, score_grad = {}, {}, {}, {}, {}
-        for h in group:
-            c = columns(h)
-            keys = near_columns(k, kve, kvo, c, 0)
-            scores[h] = dot(keys, q[:, c], 1, 1) * FACTOR + bias
+        upstream, prob_grad, prob, score_grad = {}, {}, {}, {}
         for h in group:
             c = columns(h)
             first, second = re[halo, c].astype(F32), ro[halo, c].astype(F32)
@@ -531,10 +543,10 @@
             ).astype(BF)
             prob_grad[h] = dot(near_columns(v, kve, kvo, c, 1), upstream[h], 1, 1)
         for h in group:
-            p = jnp.exp(scores[h] - lse[h : h + 1, :])
+            prob[h] = kept[h * 3 * near : (h + 1) * 3 * near, :]
+            p = prob[h].astype(F32)
             row_dot = jnp.sum(p * prob_grad[h], 0, keepdims=True)
             score_grad[h] = (p * (prob_grad[h] - row_dot)).astype(BF)
-            prob[h] = p.astype(BF)
         for h in group:
             c = columns(h)
             keys = near_columns(k, kve, kvo, c, 0)
@@ -551,14 +563,13 @@
 
 
 def audio_backward(
-    count, idx, window, valid, q, qe, qo, up, re, ro, total, dots, k, v,
-    part_e, part_o, _, dk_far, dv_far, own, send_e, send_o, dk, dv, sems_out,
+    q, qe, qo, up, re, ro, total, dots, k, v, rows_lse, kept,
+    part_e, part_o, dk_far, dv_far, own, send_e, send_o, dk, dv, sems_out,
 ):
     rows = q.shape[0]
     heads = q.shape[1] // HEAD_DIM
     back = Stream([(dk, dk_far), (dv, dv_far)], sems_out, heads)
     tail = slice(heads * HEAD_DIM, heads * HEAD_DIM + PAD)
-    bias = audio_bias(idx[0], count, window, valid, rows, k.shape[0])
     totals, row_dots = [total[...]], [dots[...]]
     for r in (re, ro):
         wide = unpack_stats(r[0:rows, tail])
@@ -566,19 +577,19 @@
         row_dots.append(pltpu.roll(wide, 64, 1))
     blank = jnp.zeros((PAD - 3 * rows, PAD), F32)
     totals = jnp.transpose(jnp.concatenate(totals + [blank], 0))
+    share = jnp.exp(rows_lse[...] - totals)
     row_dots = jnp.transpose(jnp.concatenate(row_dots + [blank], 0))
     up_e, up_o = re.at[0:rows], ro.at[0:rows]
     done = slice(0, 2 * rows)
     send_e[done, :] = part_e[...]
     send_o[done, :] = part_o[...]
     for group in groups(heads, CHUNK):
-        scores, prob_grad, prob, score_grad = {}, {}, {}, {}
+        prob_grad, prob, score_grad = {}, {}, {}
         for h in group:
             c = columns(h)
-            scores[h] = dot(k[:, c], padded(q, qe, qo, c), 1, 1) * FACTOR + bias
             prob_grad[h] = dot(v[:, c], padded(up, up_e, up_o, c), 1, 1)
         for h in group:
-            p = jnp.exp(scores[h] - totals[h : h + 1, :])
+            p = kept[h * k.shape[0] : (h + 1) * k.shape[0], :].astype(F32) * share[h : h + 1, :]
             score_grad[h] = (p * (prob_grad[h] - row_dots[h : h + 1, :])).astype(BF)
             prob[h] = p.astype(BF)
         for h in group:
@@ -647,19 +658,20 @@
     packed = ((rows_a, wide + PAD), BF)
     audio_info = (idx, audio_window.T, video_valid)
     video_info = (idx, video_window.T, audio_valid)
-    send_e, send_o, own_part, own_lse = call(
+    rows_shape = ((PAD, PAD), F32)
+    send_e, send_o, own_part, own_lse, rows_lse, kept_a = call(
         bind(audio_forward, count),
-        [packed, packed, ((rows_a, wide), F32), ((rows_a, PAD), F32)],
+        [packed, packed, ((rows_a, wide), F32), ((rows_a, PAD), F32), rows_shape,
+         ((heads * rows_v, 4 * rows_a), BF)],
         [query_audio, qe, qo, key_video, value_video],
         audio_info,
-        1.5,
-        [pltpu.VMEM((PAD, PAD), F32)],
+        1.6,
     )
     pe, po = swap_e(send_e), swap_o(send_o)
     keys_values = [key_audio, value_audio, kve, kvo]
-    att_v, lse_v = call(
+    att_v, kept_v = call(
         bind(video_forward, count),
-        [((rows_v, wide), BF), (((heads + 7) // 8 * 8, rows_v), F32)],
+        [((rows_v, wide), BF), ((heads * 3 * rows_a, rows_v), BF)],
         [query_video] + keys_values + [own_lse],
         video_info,
         1.5,
@@ -684,8 +696,19 @@
         conv_video, conv_audio, gain_video.reshape(1, wide), gain_audio.reshape(1, wide),
     ]
     stats_rows = STRIDE + rows_a + 16
+    (middle,) = call(
+        middle_sums,
+        [((STRIDE, PAD), F32)],
+        [att_v, cotangent_video, conv_video, mix_args[8]],
+        (),
+        0.7,
+    )
     (stats,) = call(
-        bind(row_sums, count), [((stats_rows, PAD), F32)], mix_args, (idx,), 1.3
+        bind(row_sums, count),
+        [((stats_rows, PAD), F32)],
+        [middle] + mix_args,
+        (idx,),
+        0.5,
     )
     tp_size = lax.axis_size("tp")
     stats_other = lax.ppermute(stats, "tp", [(i, i ^ 1) for i in range(tp_size)])
@@ -737,8 +760,8 @@
     dq_v, dkv_own, dkv_e, dkv_o = call(
         bind(video_backward, count),
         [((rows_v, wide), BF), ((2 * rows_a, wide), F32), two, two],
-        [query_video, grad_v, re, ro, conv_video, lse_v] + keys_values + [total],
-        video_info,
+        [query_video, grad_v, re, ro, conv_video, kept_v] + keys_values + [total],
+        (idx,),
         3.0,
         [big, sems(1)],
         (),
@@ -746,21 +769,20 @@
         (10,),
     )
     three = ((3 * rows_a, wide), BF)
-    total = summed(total, 1, dkv_own)
     dk_v, dv_v, dq_own, give_e, give_o = call(
-        bind(audio_backward, count),
+        audio_backward,
         [((rows_v, wide), BF), ((rows_v, wide), BF), ((rows_a, wide), F32), three, three],
         [query_audio, qe, qo, up_a, re, ro, total_a, dots_a, key_video, value_video,
-         dkv_e, dkv_o, total],
-        audio_info,
+         rows_lse, kept_a, dkv_e, dkv_o],
+        (),
         3.0,
         [big] * 2 + [sems(2)],
         (),
         (0, 1),
-        (12,),
     )
     got_e, got_o = swap_e(give_e), swap_o(give_o)
-    total = summed(total, 96, dq_own)
+    total = summed(total, 1, dq_own)
+    total = summed(total, 96)
     total = summed(total, 14)
     one = ((rows_a, wide), BF)
     dk_a, dv_a, dq_a, token = call(

time: 90.4 us -> 87.5 us (0.968)
  starting transfers between devices: 37.9 us -> 36.2 us
  Pallas kernels: 15.3 us -> 13.9 us
    ppermute x7, starting transfers between devices: 8.45 us -> 6.01 us  [moved(): return lax.ppermute(x, BLOCKS, [(i, i ^ bits) for i in range(count)])]
    pallas_call x17 -> x18, Pallas kernels: 15.3 us -> 13.9 us  [call(): pl.pallas_call(kernel, out_shape=[jax.ShapeDtypeStruct(s, d) for s, d in...]
  transfers between devices with their start and end apart: 20 -> 20, of which waited for: 11 -> 10; matrix products, arithmetic and copies ran while one was open for 0% -> 0% of each run, Pallas kernels for 9% -> 12%
where the time goes in v5:
time: 87.5 us; the launch traced here: 87 us
  starting transfers between devices  36.2 us (41%)
  waiting for transfers between devices  34 us (39%)
  Pallas kernels  13.9 us (16%)
  local copies, waits for them, and re-layouts  1.88 us (2%)
  between operations  0.99 us (1%)
    ppermute x6, starting transfers between devices, swap_o(): return lax.ppermute(x, BLOCKS, odd_route)  25.1 us
    ppermute x7, waiting for transfers between devices, moved(): return lax.ppermute(x, BLOCKS, [(i, i ^ bits) for i in range(count)])  17 us
    pallas_call x18, Pallas kernels, call(): pl.pallas_call(kernel, out_shape=[jax.ShapeDtypeStruct(s, d) for s, d in...  13.9 us
    ppermute x6, waiting for transfers between devices, swap_e(): return lax.ppermute(x, BLOCKS, even_route)  11 us
    ppermute x7, starting transfers between devices, moved(): return lax.ppermute(x, BLOCKS, [(i, i ^ bits) for i in range(count)])  6.01 us
    ppermute x6, starting transfers between devices, swap_e(): return lax.ppermute(x, BLOCKS, even_route)  4.53 us
    ppermute x1, waiting for transfers between devices, per_device(): lax.ppermute(stats, 'tp', [(i, i ^ 1) for i in range(tp_size)])  3.47 us
    ppermute x6, waiting for transfers between devices, swap_o(): return lax.ppermute(x, BLOCKS, odd_route)  2.51 us
  transfers between devices with their start and end apart: 20, of which 10 were waited for; matrix products, arithmetic and copies ran while one was open for 0% of the time, Pallas kernels for 12%

profile of v5, /device:TPU:2, one launch (start us, length us, event | category | flops | bytes accessed | tf_op | source)
XLA Modules:
  0.0 87.0 jit_solution(6775821677646202834)
XLA Ops:
  0.7 2.2 %collective-permute-start.2 = (bf16[32,1536]{1,0:T(8,128)(2,1)}, bf16[32,1536]{1,0:T(8,128)(2,1)S(1)}, u32[]{:S(2)}, u32[]{:S(2)}) collective-permute-start(bf16[32,1536]{1,0:T(8,128)(2,1)} %q.1), channel_id=1, source_target_pairs={{0,2},{2,0},{4,6},{6,4},{8,10},{10,8},{12,14},{14,12},{16,18},{18,... | collective-permute-start | bytes 294920 | tf_op jit(solution)/shard_map/ppermute | solution.py:636
  2.9 8.3 %collective-permute-start.3 = (bf16[32,1536]{1,0:T(8,128)(2,1)}, bf16[32,1536]{1,0:T(8,128)(2,1)S(1)}, u32[]{:S(2)}, u32[]{:S(2)}) collective-permute-start(bf16[32,1536]{1,0:T(8,128)(2,1)} %q.1), channel_id=1, source_target_pairs={{0,254},{2,4},{4,2},{6,8},{8,6},{10,12},{12,10},{14,16},{16,14},{1... | collective-permute-start | bytes 294920 | tf_op jit(solution)/shard_map/ppermute | solution.py:639
  13.4 3.4 %collective-permute-start.1 = (bf16[64,1536]{1,0:T(8,128)(2,1)S(1)}, bf16[64,1536]{1,0:T(8,128)(2,1)S(1)}, u32[]{:S(2)}, u32[]{:S(2)}) collective-permute-start(bf16[64,1536]{1,0:T(8,128)(2,1)S(1)} %shard_map.247), channel_id=1, source_target_pairs={{0,254},{2,4},{4,2},{6,8},{8,6},{10,12},{12,10},{14,16},{16,14},{1... | collective-permute-start | bytes 589832 | tf_op jit(solution)/shard_map/ppermute | solution.py:639
  16.9 1.5 %shard_map.248 = (bf16[32,1664]{1,0:T(8,128)(2,1)S(1)}, bf16[32,1664]{1,0:T(8,128)(2,1)S(1)}, f32[32,1536]{1,0:T(8,128)S(1)}, f32[32,128]{1,0:T(8,128)S(1)}, f32...) custom-call(s32[1]{0:T(128)} %bitcast.refs_0_.idx, s32[2,128]{1,0:T(2,128)S(1)} %bitcast.3, s32[128]{0:T(128)S(1)} %copy-done.14, ...), custom_call_target="tpu_custom_call" | custom-call | flops 1760000000 | bytes 1867776 | tf_op jit(solution)/shard_map/pallas_call | solution.py:31
  18.6 4.5 %collective-permute-start.5 = (bf16[32,1664]{1,0:T(8,128)(2,1)S(1)}, bf16[32,1664]{1,0:T(8,128)(2,1)S(1)}, u32[]{:S(2)}, u32[]{:S(2)}) collective-permute-start(bf16[32,1664]{1,0:T(8,128)(2,1)S(1)} %get-tuple-element.54), channel_id=1, source_target_pairs={{0,254},{2,4},{4,2},{6,8},{8,6},{10,12},{12,10},{14,16},{16,14},{1... | collective-permute-start | bytes 319496 | tf_op jit(solution)/shard_map/ppermute | solution.py:639
  23.1 5.1 %collective-permute-done.refs_6_.refs_9_ = bf16[64,1536]{1,0:T(8,128)(2,1)S(1)} collective-permute-done((bf16[64,1536]{1,0:T(8,128)(2,1)S(1)}, bf16[64,1536]{1,0:T(8,128)(2,1)S(1)}, u32[]{:S(2)}, u32[]{:S(2)}) %collective-permute-start) | collective-permute-done | bytes 196640 | tf_op jit(solution)/shard_map/ppermute | solution.py:636
  30.2 3.3 %collective-permute-start.7 = (bf16[32,1792]{1,0:T(8,128)(2,1)S(1)}, bf16[32,1792]{1,0:T(8,128)(2,1)S(1)}, u32[]{:S(2)}, u32[]{:S(2)}) collective-permute-start(bf16[32,1792]{1,0:T(8,128)(2,1)S(1)} %get-tuple-element.56), channel_id=1, source_target_pairs={{0,254},{2,4},{4,2},{6,8},{8,6},{10,12},{12,10},{14,16},{16,14},{1... | collective-permute-start | bytes 344072 | tf_op jit(solution)/shard_map/ppermute | solution.py:639
  34.2 4.5 %collective-permute-done.6.refs_3_.refs_4_ = bf16[32,1792]{1,0:T(8,128)(2,1)S(1)} collective-permute-done((bf16[32,1792]{1,0:T(8,128)(2,1)S(1)}, bf16[32,1792]{1,0:T(8,128)(2,1)S(1)}, u32[]{:S(2)}, u32[]{:S(2)}) %collective-permute-start.6) | collective-permute-done | bytes 114720 | tf_op jit(solution)/shard_map/ppermute | solution.py:636
  38.6 2.5 %collective-permute-done.7.refs_4_.refs_5_ = bf16[32,1792]{1,0:T(8,128)(2,1)S(1)} collective-permute-done((bf16[32,1792]{1,0:T(8,128)(2,1)S(1)}, bf16[32,1792]{1,0:T(8,128)(2,1)S(1)}, u32[]{:S(2)}, u32[]{:S(2)}) %collective-permute-start.7) | collective-permute-done | bytes 114720 | tf_op jit(solution)/shard_map/ppermute | solution.py:639
  42.2 3.5 %collective-permute-done.8.refs_2_ = f32[80,128]{1,0:T(8,128)S(1)} collective-permute-done((f32[80,128]{1,0:T(8,128)S(1)}, f32[80,128]{1,0:T(8,128)S(1)}, u32[]{:S(2)}, u32[]{:S(2)}) %collective-permute-start.8) | collective-permute-done | bytes 40992 | tf_op jit(solution)/shard_map/ppermute | solution.py:714
  45.7 2.0 %shard_map.253 = (f32[256,1536]{1,0:T(8,128)S(1)}, bf16[32,1536]{1,0:T(8,128)(2,1)S(1)}, bf16[64,1664]{1,0:T(8,128)(2,1)S(1)}, bf16[64,1664]{1,0:T(8,128)(2,1)S(...) custom-call(s32[1]{0:T(128)} %bitcast.refs_0_.idx, f32[80,128]{1,0:T(8,128)S(1)} %shard_map.252.refs_1_, ...), custom_call_target="tpu_custom_call" | custom-call | flops 2750000128 | bytes 2146304 | tf_op jit(solution)/shard_map/pallas_call | solution.py:31
  47.9 3.2 %collective-permute-start.11 = (bf16[64,1664]{1,0:T(8,128)(2,1)S(1)}, bf16[64,1664]{1,0:T(8,128)(2,1)S(1)}, u32[]{:S(2)}, u32[]{:S(2)}) collective-permute-start(bf16[64,1664]{1,0:T(8,128)(2,1)S(1)} %get-tuple-element.64), channel_id=1, source_target_pairs={{0,254},{2,4},{4,2},{6,8},{8,6},{10,12},{12,10},{14,16},{16,14},{1... | collective-permute-start | bytes 638984 | tf_op jit(solution)/shard_map/ppermute | solution.py:639
  51.4 1.5 %shard_map.255 = (bf16[256,1536]{1,0:T(8,128)(2,1)}, bf16[32,1536]{1,0:T(8,128)(2,1)}, f32[8,128]{1,0:T(8,128)S(1)}) custom-call(s32[1]{0:T(128)} %bitcast.refs_0_.idx, f32[80,128]{1,0:T(8,128)S(1)} %shard_map.252.refs_1_, f32[80,128]{1,0:T(8,128)S(1)} %collective-permute-done.8.refs_2_, bf16[256,1536]{1,0:T(8,128)(2,1)S(1)} %get-tuple-element.51.att_v.refs_2_.refs_3_, ...), custom_call_target="tpu_custom_call" | custom-call | flops 1650000000 | bytes 2179072 | tf_op jit(solution)/shard_map/pallas_call | solution.py:31
  52.9 2.5 %collective-permute-done.12.refs_1_ = f32[8,1536]{1,0:T(8,128)S(1)} collective-permute-done((f32[8,1536]{1,0:T(8,128)S(1)}, f32[8,1536]{1,0:T(8,128)S(1)}, u32[]{:S(2)}, u32[]{:S(2)}) %collective-permute-start.12) | collective-permute-done | bytes 49184 | tf_op jit(solution)/shard_map/ppermute | solution.py:735
  55.4 1.9 %collective-permute-start.13 = (f32[8,1536]{1,0:T(8,128)S(1)}, f32[8,1536]{1,0:T(8,128)S(1)}, u32[]{:S(2)}, u32[]{:S(2)}) collective-permute-start(f32[8,1536]{1,0:T(8,128)S(1)} %shard_map.256.refs_0_), channel_id=1, source_target_pairs={{0,4},{2,6},{4,0},{6,2},{8,12},{10,14},{12,8},{14,10},{16,20},{18,... | collective-permute-start | bytes 147464 | tf_op jit(solution)/shard_map/ppermute | solution.py:735
  57.3 2.3 %collective-permute-done.13.refs_1_ = f32[8,1536]{1,0:T(8,128)S(1)} collective-permute-done((f32[8,1536]{1,0:T(8,128)S(1)}, f32[8,1536]{1,0:T(8,128)S(1)}, u32[]{:S(2)}, u32[]{:S(2)}) %collective-permute-start.13) | collective-permute-done | bytes 49184 | tf_op jit(solution)/shard_map/ppermute | solution.py:735
  61.5 2.0 %shard_map.258 = (bf16[256,1536]{1,0:T(8,128)(2,1)}, f32[64,1536]{1,0:T(8,128)S(1)}, bf16[64,1536]{1,0:T(8,128)(2,1)S(1)}, bf16[64,1536]{1,0:T(8,128)(2,1)S(1)}) custom-call(s32[1]{0:T(128)} %bitcast.refs_0_.idx, bf16[256,1536]{1,0:T(8,128)(2,1)S(1)} %copy-done.4, f32[256,1536]{1,0:T(8,128)S(1)} %get-tuple-element.62.refs_2_, ...), custom_call_target="tpu_custom_call" | custom-call | flops 3300000000 | bytes 4032512 | tf_op jit(solution)/shard_map/pallas_call | solution.py:31
  63.5 2.3 %shard_map.259 = (bf16[256,1536]{1,0:T(8,128)(2,1)}, bf16[256,1536]{1,0:T(8,128)(2,1)}, f32[32,1536]{1,0:T(8,128)S(1)}, bf16[96,1536]{1,0:T(8,128)(2,1)S(1)}, bf16[96,1536]{1,0:T(8,128)(2,1)S(1)}) custom-call(bf16[32,1536]{1,0:T(8,128)(2,1)S(1)} %copy-done.11, bf16[32,1536]{1,0:T(8,128)(2,1)S(1)} %collective-permute-done.2.refs_4_.qe, ...), custom_call_target="tpu_custom_call" | custom-call | flops 3300000000 | bytes 3670016 | tf_op jit(solution)/shard_map/pallas_call | solution.py:31
  65.8 1.8 %collective-permute-start.14 = (bf16[96,1536]{1,0:T(8,128)(2,1)S(1)}, bf16[96,1536]{1,0:T(8,128)(2,1)S(1)}, u32[]{:S(2)}, u32[]{:S(2)}) collective-permute-start(bf16[96,1536]{1,0:T(8,128)(2,1)S(1)} %get-tuple-element.78), channel_id=1, source_target_pairs={{0,2},{2,0},{4,6},{6,4},{8,10},{10,8},{12,14},{14,12},{16,18},{18,... | collective-permute-start | bytes 884744 | tf_op jit(solution)/shard_map/ppermute | solution.py:636
  67.6 2.5 %collective-permute-start.15 = (bf16[96,1536]{1,0:T(8,128)(2,1)S(1)}, bf16[96,1536]{1,0:T(8,128)(2,1)S(1)}, u32[]{:S(2)}, u32[]{:S(2)}) collective-permute-start(bf16[96,1536]{1,0:T(8,128)(2,1)S(1)} %get-tuple-element.79), channel_id=1, source_target_pairs={{0,254},{2,4},{4,2},{6,8},{8,6},{10,12},{12,10},{14,16},{16,14},{1... | collective-permute-start | bytes 884744 | tf_op jit(solution)/shard_map/ppermute | solution.py:639
  71.3 4.6 %collective-permute-done.17.refs_1_ = f32[8,1536]{1,0:T(8,128)S(1)} collective-permute-done((f32[8,1536]{1,0:T(8,128)S(1)}, f32[8,1536]{1,0:T(8,128)S(1)}, u32[]{:S(2)}, u32[]{:S(2)}) %collective-permute-start.17) | collective-permute-done | bytes 49184 | tf_op jit(solution)/shard_map/ppermute | solution.py:735
  76.4 5.0 %collective-permute-done.18.refs_1_ = f32[8,1536]{1,0:T(8,128)S(1)} collective-permute-done((f32[8,1536]{1,0:T(8,128)S(1)}, f32[8,1536]{1,0:T(8,128)S(1)}, u32[]{:S(2)}, u32[]{:S(2)}) %collective-permute-start.18) | collective-permute-done | bytes 49184 | tf_op jit(solution)/shard_map/ppermute | solution.py:735
  81.3 1.7 %collective-permute-start.19 = (f32[8,1536]{1,0:T(8,128)S(1)}, f32[8,1536]{1,0:T(8,128)S(1)}, u32[]{:S(2)}, u32[]{:S(2)}) collective-permute-start(f32[8,1536]{1,0:T(8,128)S(1)} %shard_map.263.mine), channel_id=1, source_target_pairs={{0,8},{2,10},{4,12},{6,14},{8,0},{10,2},{12,4},{14,6},{16,24},{18,... | collective-permute-start | bytes 147464 | tf_op jit(solution)/shard_map/ppermute | solution.py:735
  83.8 2.6 %collective-permute-done.19.theirs = f32[8,1536]{1,0:T(8,128)S(1)} collective-permute-done((f32[8,1536]{1,0:T(8,128)S(1)}, f32[8,1536]{1,0:T(8,128)S(1)}, u32[]{:S(2)}, u32[]{:S(2)}) %collective-permute-start.19) | collective-permute-done | bytes 49184 | tf_op jit(solution)/shard_map/ppermute | solution.py:735
  (72 shorter events, 11.5 us)
Async XLA Ops:
  0.6 16.1 %copy-start.5 = (bf16[256,1536]{1,0:T(8,128)(2,1)S(1)}, bf16[256,1536]{1,0:T(8,128)(2,1)}, u32[]{:S(2)}) copy-start(bf16[256,1536]{1,0:T(8,128)(2,1)} %k.3) | copy-start | bytes 2359300
  0.7 16.1 %copy-start.6 = (bf16[256,1536]{1,0:T(8,128)(2,1)S(1)}, bf16[256,1536]{1,0:T(8,128)(2,1)}, u32[]{:S(2)}) copy-start(bf16[256,1536]{1,0:T(8,128)(2,1)} %v.3) | copy-start | bytes 2359300
  0.7 16.1 %collective-permute-start.2 = (bf16[32,1536]{1,0:T(8,128)(2,1)}, bf16[32,1536]{1,0:T(8,128)(2,1)S(1)}, u32[]{:S(2)}, u32[]{:S(2)}) collective-permute-start(bf16[32,1536]{1,0:T(8,128)(2,1)} %q.1), channel_id=1, source_target_pairs={{0,2},{2,0},{4,6},{6,4},{8,10},{10,8},{12,14},{14,12},{16,18},{18,... | collective-permute-start | bytes 294920 | tf_op jit(solution)/shard_map/ppermute | solution.py:636
  2.9 13.9 %collective-permute-start.3 = (bf16[32,1536]{1,0:T(8,128)(2,1)}, bf16[32,1536]{1,0:T(8,128)(2,1)S(1)}, u32[]{:S(2)}, u32[]{:S(2)}) collective-permute-start(bf16[32,1536]{1,0:T(8,128)(2,1)} %q.1), channel_id=1, source_target_pairs={{0,254},{2,4},{4,2},{6,8},{8,6},{10,12},{12,10},{14,16},{16,14},{1... | collective-permute-start | bytes 294920 | tf_op jit(solution)/shard_map/ppermute | solution.py:639
  13.2 14.9 %collective-permute-start = (bf16[64,1536]{1,0:T(8,128)(2,1)S(1)}, bf16[64,1536]{1,0:T(8,128)(2,1)S(1)}, u32[]{:S(2)}, u32[]{:S(2)}) collective-permute-start(bf16[64,1536]{1,0:T(8,128)(2,1)S(1)} %shard_map.247), channel_id=1, source_target_pairs={{0,2},{2,0},{4,6},{6,4},{8,10},{10,8},{12,14},{14,12},{16,18},{18,... | collective-permute-start | bytes 589832 | tf_op jit(solution)/shard_map/ppermute | solution.py:636
  13.4 14.8 %collective-permute-start.1 = (bf16[64,1536]{1,0:T(8,128)(2,1)S(1)}, bf16[64,1536]{1,0:T(8,128)(2,1)S(1)}, u32[]{:S(2)}, u32[]{:S(2)}) collective-permute-start(bf16[64,1536]{1,0:T(8,128)(2,1)S(1)} %shard_map.247), channel_id=1, source_target_pairs={{0,254},{2,4},{4,2},{6,8},{8,6},{10,12},{12,10},{14,16},{16,14},{1... | collective-permute-start | bytes 589832 | tf_op jit(solution)/shard_map/ppermute | solution.py:639
  16.8 11.4 %copy-start.4 = (bf16[256,1536]{1,0:T(8,128)(2,1)S(1)}, bf16[256,1536]{1,0:T(8,128)(2,1)}, u32[]{:S(2)}) copy-start(bf16[256,1536]{1,0:T(8,128)(2,1)} %refs_1_.1) | copy-start | bytes 2359300
  16.8 11.3 %copy-start.8 = (bf16[32,1536]{1,0:T(8,128)(2,1)S(1)}, bf16[32,1536]{1,0:T(8,128)(2,1)}, u32[]{:S(2)}) copy-start(bf16[32,1536]{1,0:T(8,128)(2,1)} %refs_7_.5) | copy-start | bytes 294916
  18.4 11.3 %collective-permute-start.4 = (bf16[32,1664]{1,0:T(8,128)(2,1)S(1)}, bf16[32,1664]{1,0:T(8,128)(2,1)S(1)}, u32[]{:S(2)}, u32[]{:S(2)}) collective-permute-start(bf16[32,1664]{1,0:T(8,128)(2,1)S(1)} %get-tuple-element.53), channel_id=1, source_target_pairs={{0,2},{2,0},{4,6},{6,4},{8,10},{10,8},{12,14},{14,12},{16,18},{18,... | collective-permute-start | bytes 319496 | tf_op jit(solution)/shard_map/ppermute | solution.py:636
  18.6 11.1 %collective-permute-start.5 = (bf16[32,1664]{1,0:T(8,128)(2,1)S(1)}, bf16[32,1664]{1,0:T(8,128)(2,1)S(1)}, u32[]{:S(2)}, u32[]{:S(2)}) collective-permute-start(bf16[32,1664]{1,0:T(8,128)(2,1)S(1)} %get-tuple-element.54), channel_id=1, source_target_pairs={{0,254},{2,4},{4,2},{6,8},{8,6},{10,12},{12,10},{14,16},{16,14},{1... | collective-permute-start | bytes 319496 | tf_op jit(solution)/shard_map/ppermute | solution.py:639
  30.1 8.5 %collective-permute-start.6 = (bf16[32,1792]{1,0:T(8,128)(2,1)S(1)}, bf16[32,1792]{1,0:T(8,128)(2,1)S(1)}, u32[]{:S(2)}, u32[]{:S(2)}) collective-permute-start(bf16[32,1792]{1,0:T(8,128)(2,1)S(1)} %get-tuple-element.55), channel_id=1, source_target_pairs={{0,2},{2,0},{4,6},{6,4},{8,10},{10,8},{12,14},{14,12},{16,18},{18,... | collective-permute-start | bytes 344072 | tf_op jit(solution)/shard_map/ppermute | solution.py:636
  30.2 10.9 %collective-permute-start.7 = (bf16[32,1792]{1,0:T(8,128)(2,1)S(1)}, bf16[32,1792]{1,0:T(8,128)(2,1)S(1)}, u32[]{:S(2)}, u32[]{:S(2)}) collective-permute-start(bf16[32,1792]{1,0:T(8,128)(2,1)S(1)} %get-tuple-element.56), channel_id=1, source_target_pairs={{0,254},{2,4},{4,2},{6,8},{8,6},{10,12},{12,10},{14,16},{16,14},{1... | collective-permute-start | bytes 344072 | tf_op jit(solution)/shard_map/ppermute | solution.py:639
  41.6 4.0 %collective-permute-start.8 = (f32[80,128]{1,0:T(8,128)S(1)}, f32[80,128]{1,0:T(8,128)S(1)}, u32[]{:S(2)}, u32[]{:S(2)}) collective-permute-start(f32[80,128]{1,0:T(8,128)S(1)} %shard_map.252.refs_1_), channel_id=1, source_target_pairs={{0,1},{1,0},{2,3},{3,2},{4,5},{5,4},{6,7},{7,6},{8,9},{9,8},{10,11... | collective-permute-start | bytes 122888 | tf_op jit(solution)/shard_map/ppermute | solution.py:714
  47.7 3.4 %collective-permute-start.9 = (f32[8,1536]{1,0:T(8,128)S(1)}, f32[8,1536]{1,0:T(8,128)S(1)}, u32[]{:S(2)}, u32[]{:S(2)}) collective-permute-start(f32[8,1536]{1,0:T(8,128)S(1)} %get-tuple-element.59.refs_0_), channel_id=1, source_target_pairs={{0,32},{2,34},{4,36},{6,38},{8,40},{10,42},{12,44},{14,46},{16,48}... | collective-permute-start | bytes 147464 | tf_op jit(solution)/shard_map/ppermute | solution.py:735
  47.8 13.7 %collective-permute-start.10 = (bf16[64,1664]{1,0:T(8,128)(2,1)S(1)}, bf16[64,1664]{1,0:T(8,128)(2,1)S(1)}, u32[]{:S(2)}, u32[]{:S(2)}) collective-permute-start(bf16[64,1664]{1,0:T(8,128)(2,1)S(1)} %get-tuple-element.63), channel_id=1, source_target_pairs={{0,2},{2,0},{4,6},{6,4},{8,10},{10,8},{12,14},{14,12},{16,18},{18,... | collective-permute-start | bytes 638984 | tf_op jit(solution)/shard_map/ppermute | solution.py:636
  47.9 13.6 %collective-permute-start.11 = (bf16[64,1664]{1,0:T(8,128)(2,1)S(1)}, bf16[64,1664]{1,0:T(8,128)(2,1)S(1)}, u32[]{:S(2)}, u32[]{:S(2)}) collective-permute-start(bf16[64,1664]{1,0:T(8,128)(2,1)S(1)} %get-tuple-element.64), channel_id=1, source_target_pairs={{0,254},{2,4},{4,2},{6,8},{8,6},{10,12},{12,10},{14,16},{16,14},{1... | collective-permute-start | bytes 638984 | tf_op jit(solution)/shard_map/ppermute | solution.py:639
  51.1 4.4 %collective-permute-start.12 = (f32[8,1536]{1,0:T(8,128)S(1)}, f32[8,1536]{1,0:T(8,128)S(1)}, u32[]{:S(2)}, u32[]{:S(2)}) collective-permute-start(f32[8,1536]{1,0:T(8,128)S(1)} %shard_map.254.refs_13_.refs_0_), channel_id=1, source_target_pairs={{0,64},{2,66},{4,68},{6,70},{8,72},{10,74},{12,76},{14,78},{16,80}... | collective-permute-start | bytes 147464 | tf_op jit(solution)/shard_map/ppermute | solution.py:735
  55.4 4.2 %collective-permute-start.13 = (f32[8,1536]{1,0:T(8,128)S(1)}, f32[8,1536]{1,0:T(8,128)S(1)}, u32[]{:S(2)}, u32[]{:S(2)}) collective-permute-start(f32[8,1536]{1,0:T(8,128)S(1)} %shard_map.256.refs_0_), channel_id=1, source_target_pairs={{0,4},{2,6},{4,0},{6,2},{8,12},{10,14},{12,8},{14,10},{16,20},{18,... | collective-permute-start | bytes 147464 | tf_op jit(solution)/shard_map/ppermute | solution.py:735
  59.6 10.5 %collective-permute-start.16 = (f32[8,1536]{1,0:T(8,128)S(1)}, f32[8,1536]{1,0:T(8,128)S(1)}, u32[]{:S(2)}, u32[]{:S(2)}) collective-permute-start(f32[8,1536]{1,0:T(8,128)S(1)} %shard_map.257.refs_11_.refs_0_), channel_id=1, source_target_pairs={{0,2},{2,0},{4,6},{6,4},{8,10},{10,8},{12,14},{14,12},{16,18},{18,... | collective-permute-start | bytes 147464 | tf_op jit(solution)/shard_map/ppermute | solution.py:735
  65.8 17.3 %collective-permute-start.14 = (bf16[96,1536]{1,0:T(8,128)(2,1)S(1)}, bf16[96,1536]{1,0:T(8,128)(2,1)S(1)}, u32[]{:S(2)}, u32[]{:S(2)}) collective-permute-start(bf16[96,1536]{1,0:T(8,128)(2,1)S(1)} %get-tuple-element.78), channel_id=1, source_target_pairs={{0,2},{2,0},{4,6},{6,4},{8,10},{10,8},{12,14},{14,12},{16,18},{18,... | collective-permute-start | bytes 884744 | tf_op jit(solution)/shard_map/ppermute | solution.py:636
  67.6 15.5 %collective-permute-start.15 = (bf16[96,1536]{1,0:T(8,128)(2,1)S(1)}, bf16[96,1536]{1,0:T(8,128)(2,1)S(1)}, u32[]{:S(2)}, u32[]{:S(2)}) collective-permute-start(bf16[96,1536]{1,0:T(8,128)(2,1)S(1)} %get-tuple-element.79), channel_id=1, source_target_pairs={{0,254},{2,4},{4,2},{6,8},{8,6},{10,12},{12,10},{14,16},{16,14},{1... | collective-permute-start | bytes 884744 | tf_op jit(solution)/shard_map/ppermute | solution.py:639
  70.1 5.8 %collective-permute-start.17 = (f32[8,1536]{1,0:T(8,128)S(1)}, f32[8,1536]{1,0:T(8,128)S(1)}, u32[]{:S(2)}, u32[]{:S(2)}) collective-permute-start(f32[8,1536]{1,0:T(8,128)S(1)} %shard_map.261.refs_0_), channel_id=1, source_target_pairs={{0,192},{2,194},{4,196},{6,198},{8,200},{10,202},{12,204},{14,206}... | collective-permute-start | bytes 147464 | tf_op jit(solution)/shard_map/ppermute | solution.py:735
  75.9 5.4 %collective-permute-start.18 = (f32[8,1536]{1,0:T(8,128)S(1)}, f32[8,1536]{1,0:T(8,128)S(1)}, u32[]{:S(2)}, u32[]{:S(2)}) collective-permute-start(f32[8,1536]{1,0:T(8,128)S(1)} %shard_map.262.refs_0_), channel_id=1, source_target_pairs={{0,28},{2,30},{4,24},{6,26},{8,20},{10,22},{12,16},{14,18},{16,12}... | collective-permute-start | bytes 147464 | tf_op jit(solution)/shard_map/ppermute | solution.py:735
  81.3 5.1 %collective-permute-start.19 = (f32[8,1536]{1,0:T(8,128)S(1)}, f32[8,1536]{1,0:T(8,128)S(1)}, u32[]{:S(2)}, u32[]{:S(2)}) collective-permute-start(f32[8,1536]{1,0:T(8,128)S(1)} %shard_map.263.mine), channel_id=1, source_target_pairs={{0,8},{2,10},{4,12},{6,14},{8,0},{10,2},{12,4},{14,6},{16,24},{18,... | collective-permute-start | bytes 147464 | tf_op jit(solution)/shard_map/ppermute | solution.py:735
  (14 other events, 75.1 us)

commit v6 on v5

--- a/solution.py
+++ b/solution.py
@@ -99,6 +99,13 @@
 
 def plus(*refs):
     refs[-1][...] = refs[0][...] + refs[1][...]
+
+
+def join(kv_e, q_e, kv_o, q_o, _, send_e, send_o):
+    rows = kv_e.shape[0]
+    for send, kv, q in ((send_e, kv_e, q_e), (send_o, kv_o, q_o)):
+        send[0:rows, :] = kv[...]
+        send[rows:, :] = q[...]
 
 
 def settle(dkv, dq, e, o, dk_out, dv_out, dq_out, token):
@@ -564,7 +571,7 @@
 
 def audio_backward(
     q, qe, qo, up, re, ro, total, dots, k, v, rows_lse, kept,
-    part_e, part_o, dk_far, dv_far, own, send_e, send_o, dk, dv, sems_out,
+    dk_far, dv_far, own, send_e, send_o, dk, dv, sems_out,
 ):
     rows = q.shape[0]
     heads = q.shape[1] // HEAD_DIM
@@ -580,9 +587,6 @@
     share = jnp.exp(rows_lse[...] - totals)
     row_dots = jnp.transpose(jnp.concatenate(row_dots + [blank], 0))
     up_e, up_o = re.at[0:rows], ro.at[0:rows]
-    done = slice(0, 2 * rows)
-    send_e[done, :] = part_e[...]
-    send_o[done, :] = part_o[...]
     for group in groups(heads, CHUNK):
         prob_grad, prob, score_grad = {}, {}, {}
         for h in group:
@@ -598,8 +602,8 @@
             dk[:, c] = (dot(score_grad[h], padded(q, qe, qo, c), 1, 0) * FACTOR).astype(BF)
             dv[:, c] = dot(prob[h], padded(up, up_e, up_o, c), 1, 0).astype(BF)
             own[:, c] = grad[:rows]
-            send_e[2 * rows :, c] = grad[rows : 2 * rows].astype(BF)
-            send_o[2 * rows :, c] = grad[2 * rows : 3 * rows].astype(BF)
+            send_e[:, c] = grad[rows : 2 * rows].astype(BF)
+            send_o[:, c] = grad[2 * rows : 3 * rows].astype(BF)
             back.after_head(h)
     back.wait_all()
 
@@ -734,9 +738,9 @@
     def moved(x, bits):
         return lax.ppermute(x, BLOCKS, [(i, i ^ bits) for i in range(count)])
 
-    def summed(x, bits, *after):
+    def summed(x, bits, *after, micros=0.5):
         (y,) = call(
-            plus, [((8, wide), F32)], [x, moved(x, bits)] + list(after), (), 0.5,
+            plus, [((8, wide), F32)], [x, moved(x, bits)] + list(after), (), micros,
             (), (), (), range(2, 2 + len(after)),
         )
         return y
@@ -768,22 +772,27 @@
         (0,),
         (10,),
     )
-    three = ((3 * rows_a, wide), BF)
-    dk_v, dv_v, dq_own, give_e, give_o = call(
+    one = ((rows_a, wide), BF)
+    dk_v, dv_v, dq_own, dq_e, dq_o = call(
         audio_backward,
-        [((rows_v, wide), BF), ((rows_v, wide), BF), ((rows_a, wide), F32), three, three],
+        [((rows_v, wide), BF), ((rows_v, wide), BF), ((rows_a, wide), F32), one, one],
         [query_audio, qe, qo, up_a, re, ro, total_a, dots_a, key_video, value_video,
-         rows_lse, kept_a, dkv_e, dkv_o],
+         rows_lse, kept_a],
         (),
         3.0,
         [big] * 2 + [sems(2)],
         (),
         (0, 1),
     )
+    total = summed(total, 1, dq_own, dkv_own)
+    three = ((3 * rows_a, wide), BF)
+    give_e, give_o = call(
+        join, [three, three], [dkv_e, dq_e, dkv_o, dq_o, total], (), 0.4,
+        (), (), (), (4,),
+    )
     got_e, got_o = swap_e(give_e), swap_o(give_o)
-    total = summed(total, 1, dq_own)
-    total = summed(total, 96)
-    total = summed(total, 14)
+    total = summed(total, 96, micros=1.0)
+    total = summed(total, 14, micros=1.0)
     one = ((rows_a, wide), BF)
     dk_a, dv_a, dq_a, token = call(
         settle,

time: 87.5 us -> 86.8 us (level)
  waiting for transfers between devices: 34 us -> 30.1 us
  starting transfers between devices: 36.2 us -> 38.6 us
    ppermute x7, waiting for transfers between devices: 17 us -> 11.9 us  [moved(): return lax.ppermute(x, BLOCKS, [(i, i ^ bits) for i in range(count)])]
    ppermute x7, starting transfers between devices: 6.01 us -> 8.63 us  [moved(): return lax.ppermute(x, BLOCKS, [(i, i ^ bits) for i in range(count)])]
    pallas_call x18 -> x19, Pallas kernels: 13.9 us -> 14 us  [call(): pl.pallas_call(kernel, out_shape=[jax.ShapeDtypeStruct(s, d) for s, d in...]
  transfers between devices with their start and end apart: 20 -> 20, of which waited for: 10 -> 12; matrix products, arithmetic and copies ran while one was open for 0% -> 0% of each run, Pallas kernels for 12% -> 12%
where the time goes in v6:
time: 86.8 us; the launch traced here: 85.6 us
  starting transfers between devices  38.6 us (44%)
  waiting for transfers between devices  30.1 us (35%)
  Pallas kernels  14 us (16%)
  local copies, waits for them, and re-layouts  1.88 us (2%)
  between operations  1.01 us (1%)
    ppermute x6, starting transfers between devices, swap_o(): return lax.ppermute(x, BLOCKS, odd_route)  24.8 us
    pallas_call x19, Pallas kernels, call(): pl.pallas_call(kernel, out_shape=[jax.ShapeDtypeStruct(s, d) for s, d in...  14 us
    ppermute x7, waiting for transfers between devices, moved(): return lax.ppermute(x, BLOCKS, [(i, i ^ bits) for i in range(count)])  11.9 us
    ppermute x6, waiting for transfers between devices, swap_e(): return lax.ppermute(x, BLOCKS, even_route)  11.8 us
    ppermute x7, starting transfers between devices, moved(): return lax.ppermute(x, BLOCKS, [(i, i ^ bits) for i in range(count)])  8.63 us
    ppermute x6, starting transfers between devices, swap_e(): return lax.ppermute(x, BLOCKS, even_route)  4.54 us
    ppermute x1, waiting for transfers between devices, per_device(): lax.ppermute(stats, 'tp', [(i, i ^ 1) for i in range(tp_size)])  3.47 us
    ppermute x6, waiting for transfers between devices, swap_o(): return lax.ppermute(x, BLOCKS, odd_route)  2.95 us
  transfers between devices with their start and end apart: 20, of which 12 were waited for; matrix products, arithmetic and copies ran while one was open for 0% of the time, Pallas kernels for 12%

profile of v6, /device:TPU:2, one launch (start us, length us, event | category | flops | bytes accessed | tf_op | source)
XLA Modules:
  0.0 85.6 jit_solution(10290787108270698490)
XLA Ops:
  0.7 2.2 %collective-permute-start.2 = (bf16[32,1536]{1,0:T(8,128)(2,1)}, bf16[32,1536]{1,0:T(8,128)(2,1)S(1)}, u32[]{:S(2)}, u32[]{:S(2)}) collective-permute-start(bf16[32,1536]{1,0:T(8,128)(2,1)} %q.1), channel_id=1, source_target_pairs={{0,2},{2,0},{4,6},{6,4},{8,10},{10,8},{12,14},{14,12},{16,18},{18,... | collective-permute-start | bytes 294920 | tf_op jit(solution)/shard_map/ppermute | solution.py:640
  2.9 8.3 %collective-permute-start.3 = (bf16[32,1536]{1,0:T(8,128)(2,1)}, bf16[32,1536]{1,0:T(8,128)(2,1)S(1)}, u32[]{:S(2)}, u32[]{:S(2)}) collective-permute-start(bf16[32,1536]{1,0:T(8,128)(2,1)} %q.1), channel_id=1, source_target_pairs={{0,254},{2,4},{4,2},{6,8},{8,6},{10,12},{12,10},{14,16},{16,14},{1... | collective-permute-start | bytes 294920 | tf_op jit(solution)/shard_map/ppermute | solution.py:643
  13.4 3.4 %collective-permute-start.1 = (bf16[64,1536]{1,0:T(8,128)(2,1)S(1)}, bf16[64,1536]{1,0:T(8,128)(2,1)S(1)}, u32[]{:S(2)}, u32[]{:S(2)}) collective-permute-start(bf16[64,1536]{1,0:T(8,128)(2,1)S(1)} %shard_map.247), channel_id=1, source_target_pairs={{0,254},{2,4},{4,2},{6,8},{8,6},{10,12},{12,10},{14,16},{16,14},{1... | collective-permute-start | bytes 589832 | tf_op jit(solution)/shard_map/ppermute | solution.py:643
  16.9 1.5 %shard_map.248 = (bf16[32,1664]{1,0:T(8,128)(2,1)S(1)}, bf16[32,1664]{1,0:T(8,128)(2,1)S(1)}, f32[32,1536]{1,0:T(8,128)S(1)}, f32[32,128]{1,0:T(8,128)S(1)}, f32...) custom-call(s32[1]{0:T(128)} %bitcast.refs_0_.idx, s32[2,128]{1,0:T(2,128)S(1)} %bitcast.3, s32[128]{0:T(128)S(1)} %copy-done.14, ...), custom_call_target="tpu_custom_call" | custom-call | flops 1760000000 | bytes 1867776 | tf_op jit(solution)/shard_map/pallas_call | solution.py:31
  18.6 4.5 %collective-permute-start.5 = (bf16[32,1664]{1,0:T(8,128)(2,1)S(1)}, bf16[32,1664]{1,0:T(8,128)(2,1)S(1)}, u32[]{:S(2)}, u32[]{:S(2)}) collective-permute-start(bf16[32,1664]{1,0:T(8,128)(2,1)S(1)} %get-tuple-element.56), channel_id=1, source_target_pairs={{0,254},{2,4},{4,2},{6,8},{8,6},{10,12},{12,10},{14,16},{16,14},{1... | collective-permute-start | bytes 319496 | tf_op jit(solution)/shard_map/ppermute | solution.py:643
  23.1 5.1 %collective-permute-done.refs_6_.refs_9_ = bf16[64,1536]{1,0:T(8,128)(2,1)S(1)} collective-permute-done((bf16[64,1536]{1,0:T(8,128)(2,1)S(1)}, bf16[64,1536]{1,0:T(8,128)(2,1)S(1)}, u32[]{:S(2)}, u32[]{:S(2)}) %collective-permute-start) | collective-permute-done | bytes 196640 | tf_op jit(solution)/shard_map/ppermute | solution.py:640
  30.2 3.3 %collective-permute-start.7 = (bf16[32,1792]{1,0:T(8,128)(2,1)S(1)}, bf16[32,1792]{1,0:T(8,128)(2,1)S(1)}, u32[]{:S(2)}, u32[]{:S(2)}) collective-permute-start(bf16[32,1792]{1,0:T(8,128)(2,1)S(1)} %get-tuple-element.58), channel_id=1, source_target_pairs={{0,254},{2,4},{4,2},{6,8},{8,6},{10,12},{12,10},{14,16},{16,14},{1... | collective-permute-start | bytes 344072 | tf_op jit(solution)/shard_map/ppermute | solution.py:643
  34.2 4.5 %collective-permute-done.6.refs_3_.refs_4_ = bf16[32,1792]{1,0:T(8,128)(2,1)S(1)} collective-permute-done((bf16[32,1792]{1,0:T(8,128)(2,1)S(1)}, bf16[32,1792]{1,0:T(8,128)(2,1)S(1)}, u32[]{:S(2)}, u32[]{:S(2)}) %collective-permute-start.6) | collective-permute-done | bytes 114720 | tf_op jit(solution)/shard_map/ppermute | solution.py:640
  38.6 2.5 %collective-permute-done.7.refs_4_.refs_5_ = bf16[32,1792]{1,0:T(8,128)(2,1)S(1)} collective-permute-done((bf16[32,1792]{1,0:T(8,128)(2,1)S(1)}, bf16[32,1792]{1,0:T(8,128)(2,1)S(1)}, u32[]{:S(2)}, u32[]{:S(2)}) %collective-permute-start.7) | collective-permute-done | bytes 114720 | tf_op jit(solution)/shard_map/ppermute | solution.py:643
  42.2 3.5 %collective-permute-done.8.refs_2_ = f32[80,128]{1,0:T(8,128)S(1)} collective-permute-done((f32[80,128]{1,0:T(8,128)S(1)}, f32[80,128]{1,0:T(8,128)S(1)}, u32[]{:S(2)}, u32[]{:S(2)}) %collective-permute-start.8) | collective-permute-done | bytes 40992 | tf_op jit(solution)/shard_map/ppermute | solution.py:718
  45.7 2.0 %shard_map.253 = (f32[256,1536]{1,0:T(8,128)S(1)}, bf16[32,1536]{1,0:T(8,128)(2,1)S(1)}, bf16[64,1664]{1,0:T(8,128)(2,1)S(1)}, bf16[64,1664]{1,0:T(8,128)(2,1)S(...) custom-call(s32[1]{0:T(128)} %bitcast.refs_0_.idx, f32[80,128]{1,0:T(8,128)S(1)} %shard_map.252.refs_1_, ...), custom_call_target="tpu_custom_call" | custom-call | flops 2750000128 | bytes 2146304 | tf_op jit(solution)/shard_map/pallas_call | solution.py:31
  47.9 3.2 %collective-permute-start.11 = (bf16[64,1664]{1,0:T(8,128)(2,1)S(1)}, bf16[64,1664]{1,0:T(8,128)(2,1)S(1)}, u32[]{:S(2)}, u32[]{:S(2)}) collective-permute-start(bf16[64,1664]{1,0:T(8,128)(2,1)S(1)} %get-tuple-element.66), channel_id=1, source_target_pairs={{0,254},{2,4},{4,2},{6,8},{8,6},{10,12},{12,10},{14,16},{16,14},{1... | collective-permute-start | bytes 638984 | tf_op jit(solution)/shard_map/ppermute | solution.py:643
  51.4 1.5 %shard_map.255 = (bf16[256,1536]{1,0:T(8,128)(2,1)}, bf16[32,1536]{1,0:T(8,128)(2,1)}, f32[8,128]{1,0:T(8,128)S(1)}) custom-call(s32[1]{0:T(128)} %bitcast.refs_0_.idx, f32[80,128]{1,0:T(8,128)S(1)} %shard_map.252.refs_1_, f32[80,128]{1,0:T(8,128)S(1)} %collective-permute-done.8.refs_2_, bf16[256,1536]{1,0:T(8,128)(2,1)S(1)} %get-tuple-element.53.att_v.refs_2_.refs_3_, ...), custom_call_target="tpu_custom_call" | custom-call | flops 1650000000 | bytes 2179072 | tf_op jit(solution)/shard_map/pallas_call | solution.py:31
  52.9 2.5 %collective-permute-done.12.refs_1_ = f32[8,1536]{1,0:T(8,128)S(1)} collective-permute-done((f32[8,1536]{1,0:T(8,128)S(1)}, f32[8,1536]{1,0:T(8,128)S(1)}, u32[]{:S(2)}, u32[]{:S(2)}) %collective-permute-start.12) | collective-permute-done | bytes 49184 | tf_op jit(solution)/shard_map/ppermute | solution.py:739
  55.4 1.9 %collective-permute-start.13 = (f32[8,1536]{1,0:T(8,128)S(1)}, f32[8,1536]{1,0:T(8,128)S(1)}, u32[]{:S(2)}, u32[]{:S(2)}) collective-permute-start(f32[8,1536]{1,0:T(8,128)S(1)} %shard_map.256.refs_0_), channel_id=1, source_target_pairs={{0,4},{2,6},{4,0},{6,2},{8,12},{10,14},{12,8},{14,10},{16,20},{18,... | collective-permute-start | bytes 147464 | tf_op jit(solution)/shard_map/ppermute | solution.py:739
  57.3 2.3 %collective-permute-done.13.refs_1_ = f32[8,1536]{1,0:T(8,128)S(1)} collective-permute-done((f32[8,1536]{1,0:T(8,128)S(1)}, f32[8,1536]{1,0:T(8,128)S(1)}, u32[]{:S(2)}, u32[]{:S(2)}) %collective-permute-start.13) | collective-permute-done | bytes 49184 | tf_op jit(solution)/shard_map/ppermute | solution.py:739
  60.0 1.5 %collective-permute-done.10.refs_3_.re = bf16[64,1664]{1,0:T(8,128)(2,1)S(1)} collective-permute-done((bf16[64,1664]{1,0:T(8,128)(2,1)S(1)}, bf16[64,1664]{1,0:T(8,128)(2,1)S(1)}, u32[]{:S(2)}, u32[]{:S(2)}) %collective-permute-start.10) | collective-permute-done | bytes 213024 | tf_op jit(solution)/shard_map/ppermute | solution.py:640
  61.5 2.0 %shard_map.258 = (bf16[256,1536]{1,0:T(8,128)(2,1)}, f32[64,1536]{1,0:T(8,128)S(1)}, bf16[64,1536]{1,0:T(8,128)(2,1)S(1)}, bf16[64,1536]{1,0:T(8,128)(2,1)S(1)}) custom-call(s32[1]{0:T(128)} %bitcast.refs_0_.idx, bf16[256,1536]{1,0:T(8,128)(2,1)S(1)} %copy-done.4, f32[256,1536]{1,0:T(8,128)S(1)} %get-tuple-element.64.refs_2_, ...), custom_call_target="tpu_custom_call" | custom-call | flops 3300000000 | bytes 4032512 | tf_op jit(solution)/shard_map/pallas_call | solution.py:31
  63.5 2.3 %shard_map.259 = (bf16[256,1536]{1,0:T(8,128)(2,1)}, bf16[256,1536]{1,0:T(8,128)(2,1)}, f32[32,1536]{1,0:T(8,128)S(1)}, bf16[32,1536]{1,0:T(8,128)(2,1)S(1)}, bf16[32,1536]{1,0:T(8,128)(2,1)S(1)}) custom-call(bf16[32,1536]{1,0:T(8,128)(2,1)S(1)} %copy-done.11, bf16[32,1536]{1,0:T(8,128)(2,1)S(1)} %collective-permute-done.2.refs_4_.qe, ...), custom_call_target="tpu_custom_call" | custom-call | flops 3300000000 | bytes 3276800 | tf_op jit(solution)/shard_map/pallas_call | solution.py:31
  66.7 1.8 %collective-permute-start.15 = (bf16[96,1536]{1,0:T(8,128)(2,1)S(1)}, bf16[96,1536]{1,0:T(8,128)(2,1)S(1)}, u32[]{:S(2)}, u32[]{:S(2)}) collective-permute-start(bf16[96,1536]{1,0:T(8,128)(2,1)S(1)} %get-tuple-element.82), channel_id=1, source_target_pairs={{0,2},{2,0},{4,6},{6,4},{8,10},{10,8},{12,14},{14,12},{16,18},{18,... | collective-permute-start | bytes 884744 | tf_op jit(solution)/shard_map/ppermute | solution.py:640
  68.5 2.2 %collective-permute-start.16 = (bf16[96,1536]{1,0:T(8,128)(2,1)S(1)}, bf16[96,1536]{1,0:T(8,128)(2,1)S(1)}, u32[]{:S(2)}, u32[]{:S(2)}) collective-permute-start(bf16[96,1536]{1,0:T(8,128)(2,1)S(1)} %get-tuple-element.83), channel_id=1, source_target_pairs={{0,254},{2,4},{4,2},{6,8},{8,6},{10,12},{12,10},{14,16},{16,14},{1... | collective-permute-start | bytes 884744 | tf_op jit(solution)/shard_map/ppermute | solution.py:643
  71.2 2.1 %collective-permute-start.18 = (f32[8,1536]{1,0:T(8,128)S(1)}, f32[8,1536]{1,0:T(8,128)S(1)}, u32[]{:S(2)}, u32[]{:S(2)}) collective-permute-start(f32[8,1536]{1,0:T(8,128)S(1)} %shard_map.263.refs_0_), channel_id=1, source_target_pairs={{0,28},{2,30},{4,24},{6,26},{8,20},{10,22},{12,16},{14,18},{16,12}... | collective-permute-start | bytes 147464 | tf_op jit(solution)/shard_map/ppermute | solution.py:739
  73.3 5.7 %collective-permute-done.18.refs_1_ = f32[8,1536]{1,0:T(8,128)S(1)} collective-permute-done((f32[8,1536]{1,0:T(8,128)S(1)}, f32[8,1536]{1,0:T(8,128)S(1)}, u32[]{:S(2)}, u32[]{:S(2)}) %collective-permute-start.18) | collective-permute-done | bytes 49184 | tf_op jit(solution)/shard_map/ppermute | solution.py:739
  79.0 3.1 %collective-permute-start.19 = (f32[8,1536]{1,0:T(8,128)S(1)}, f32[8,1536]{1,0:T(8,128)S(1)}, u32[]{:S(2)}, u32[]{:S(2)}) collective-permute-start(f32[8,1536]{1,0:T(8,128)S(1)} %shard_map.264.mine), channel_id=1, source_target_pairs={{0,8},{2,10},{4,12},{6,14},{8,0},{10,2},{12,4},{14,6},{16,24},{18,... | collective-permute-start | bytes 147464 | tf_op jit(solution)/shard_map/ppermute | solution.py:739
  (73 shorter events, 11.9 us)
Async XLA Ops:
  0.6 16.1 %copy-start.5 = (bf16[256,1536]{1,0:T(8,128)(2,1)S(1)}, bf16[256,1536]{1,0:T(8,128)(2,1)}, u32[]{:S(2)}) copy-start(bf16[256,1536]{1,0:T(8,128)(2,1)} %k.3) | copy-start | bytes 2359300
  0.7 16.1 %copy-start.6 = (bf16[256,1536]{1,0:T(8,128)(2,1)S(1)}, bf16[256,1536]{1,0:T(8,128)(2,1)}, u32[]{:S(2)}) copy-start(bf16[256,1536]{1,0:T(8,128)(2,1)} %v.3) | copy-start | bytes 2359300
  0.7 16.1 %collective-permute-start.2 = (bf16[32,1536]{1,0:T(8,128)(2,1)}, bf16[32,1536]{1,0:T(8,128)(2,1)S(1)}, u32[]{:S(2)}, u32[]{:S(2)}) collective-permute-start(bf16[32,1536]{1,0:T(8,128)(2,1)} %q.1), channel_id=1, source_target_pairs={{0,2},{2,0},{4,6},{6,4},{8,10},{10,8},{12,14},{14,12},{16,18},{18,... | collective-permute-start | bytes 294920 | tf_op jit(solution)/shard_map/ppermute | solution.py:640
  2.9 13.9 %collective-permute-start.3 = (bf16[32,1536]{1,0:T(8,128)(2,1)}, bf16[32,1536]{1,0:T(8,128)(2,1)S(1)}, u32[]{:S(2)}, u32[]{:S(2)}) collective-permute-start(bf16[32,1536]{1,0:T(8,128)(2,1)} %q.1), channel_id=1, source_target_pairs={{0,254},{2,4},{4,2},{6,8},{8,6},{10,12},{12,10},{14,16},{16,14},{1... | collective-permute-start | bytes 294920 | tf_op jit(solution)/shard_map/ppermute | solution.py:643
  13.2 14.9 %collective-permute-start = (bf16[64,1536]{1,0:T(8,128)(2,1)S(1)}, bf16[64,1536]{1,0:T(8,128)(2,1)S(1)}, u32[]{:S(2)}, u32[]{:S(2)}) collective-permute-start(bf16[64,1536]{1,0:T(8,128)(2,1)S(1)} %shard_map.247), channel_id=1, source_target_pairs={{0,2},{2,0},{4,6},{6,4},{8,10},{10,8},{12,14},{14,12},{16,18},{18,... | collective-permute-start | bytes 589832 | tf_op jit(solution)/shard_map/ppermute | solution.py:640
  13.4 14.8 %collective-permute-start.1 = (bf16[64,1536]{1,0:T(8,128)(2,1)S(1)}, bf16[64,1536]{1,0:T(8,128)(2,1)S(1)}, u32[]{:S(2)}, u32[]{:S(2)}) collective-permute-start(bf16[64,1536]{1,0:T(8,128)(2,1)S(1)} %shard_map.247), channel_id=1, source_target_pairs={{0,254},{2,4},{4,2},{6,8},{8,6},{10,12},{12,10},{14,16},{16,14},{1... | collective-permute-start | bytes 589832 | tf_op jit(solution)/shard_map/ppermute | solution.py:643
  16.8 11.4 %copy-start.4 = (bf16[256,1536]{1,0:T(8,128)(2,1)S(1)}, bf16[256,1536]{1,0:T(8,128)(2,1)}, u32[]{:S(2)}) copy-start(bf16[256,1536]{1,0:T(8,128)(2,1)} %refs_1_.1) | copy-start | bytes 2359300
  16.8 11.3 %copy-start.8 = (bf16[32,1536]{1,0:T(8,128)(2,1)S(1)}, bf16[32,1536]{1,0:T(8,128)(2,1)}, u32[]{:S(2)}) copy-start(bf16[32,1536]{1,0:T(8,128)(2,1)} %refs_7_.5) | copy-start | bytes 294916
  18.4 11.3 %collective-permute-start.4 = (bf16[32,1664]{1,0:T(8,128)(2,1)S(1)}, bf16[32,1664]{1,0:T(8,128)(2,1)S(1)}, u32[]{:S(2)}, u32[]{:S(2)}) collective-permute-start(bf16[32,1664]{1,0:T(8,128)(2,1)S(1)} %get-tuple-element.55), channel_id=1, source_target_pairs={{0,2},{2,0},{4,6},{6,4},{8,10},{10,8},{12,14},{14,12},{16,18},{18,... | collective-permute-start | bytes 319496 | tf_op jit(solution)/shard_map/ppermute | solution.py:640
  18.6 11.1 %collective-permute-start.5 = (bf16[32,1664]{1,0:T(8,128)(2,1)S(1)}, bf16[32,1664]{1,0:T(8,128)(2,1)S(1)}, u32[]{:S(2)}, u32[]{:S(2)}) collective-permute-start(bf16[32,1664]{1,0:T(8,128)(2,1)S(1)} %get-tuple-element.56), channel_id=1, source_target_pairs={{0,254},{2,4},{4,2},{6,8},{8,6},{10,12},{12,10},{14,16},{16,14},{1... | collective-permute-start | bytes 319496 | tf_op jit(solution)/shard_map/ppermute | solution.py:643
  30.1 8.5 %collective-permute-start.6 = (bf16[32,1792]{1,0:T(8,128)(2,1)S(1)}, bf16[32,1792]{1,0:T(8,128)(2,1)S(1)}, u32[]{:S(2)}, u32[]{:S(2)}) collective-permute-start(bf16[32,1792]{1,0:T(8,128)(2,1)S(1)} %get-tuple-element.57), channel_id=1, source_target_pairs={{0,2},{2,0},{4,6},{6,4},{8,10},{10,8},{12,14},{14,12},{16,18},{18,... | collective-permute-start | bytes 344072 | tf_op jit(solution)/shard_map/ppermute | solution.py:640
  30.2 10.9 %collective-permute-start.7 = (bf16[32,1792]{1,0:T(8,128)(2,1)S(1)}, bf16[32,1792]{1,0:T(8,128)(2,1)S(1)}, u32[]{:S(2)}, u32[]{:S(2)}) collective-permute-start(bf16[32,1792]{1,0:T(8,128)(2,1)S(1)} %get-tuple-element.58), channel_id=1, source_target_pairs={{0,254},{2,4},{4,2},{6,8},{8,6},{10,12},{12,10},{14,16},{16,14},{1... | collective-permute-start | bytes 344072 | tf_op jit(solution)/shard_map/ppermute | solution.py:643
  41.6 4.0 %collective-permute-start.8 = (f32[80,128]{1,0:T(8,128)S(1)}, f32[80,128]{1,0:T(8,128)S(1)}, u32[]{:S(2)}, u32[]{:S(2)}) collective-permute-start(f32[80,128]{1,0:T(8,128)S(1)} %shard_map.252.refs_1_), channel_id=1, source_target_pairs={{0,1},{1,0},{2,3},{3,2},{4,5},{5,4},{6,7},{7,6},{8,9},{9,8},{10,11... | collective-permute-start | bytes 122888 | tf_op jit(solution)/shard_map/ppermute | solution.py:718
  47.7 3.4 %collective-permute-start.9 = (f32[8,1536]{1,0:T(8,128)S(1)}, f32[8,1536]{1,0:T(8,128)S(1)}, u32[]{:S(2)}, u32[]{:S(2)}) collective-permute-start(f32[8,1536]{1,0:T(8,128)S(1)} %get-tuple-element.61.refs_0_), channel_id=1, source_target_pairs={{0,32},{2,34},{4,36},{6,38},{8,40},{10,42},{12,44},{14,46},{16,48}... | collective-permute-start | bytes 147464 | tf_op jit(solution)/shard_map/ppermute | solution.py:739
  47.8 13.7 %collective-permute-start.10 = (bf16[64,1664]{1,0:T(8,128)(2,1)S(1)}, bf16[64,1664]{1,0:T(8,128)(2,1)S(1)}, u32[]{:S(2)}, u32[]{:S(2)}) collective-permute-start(bf16[64,1664]{1,0:T(8,128)(2,1)S(1)} %get-tuple-element.65), channel_id=1, source_target_pairs={{0,2},{2,0},{4,6},{6,4},{8,10},{10,8},{12,14},{14,12},{16,18},{18,... | collective-permute-start | bytes 638984 | tf_op jit(solution)/shard_map/ppermute | solution.py:640
  47.9 13.6 %collective-permute-start.11 = (bf16[64,1664]{1,0:T(8,128)(2,1)S(1)}, bf16[64,1664]{1,0:T(8,128)(2,1)S(1)}, u32[]{:S(2)}, u32[]{:S(2)}) collective-permute-start(bf16[64,1664]{1,0:T(8,128)(2,1)S(1)} %get-tuple-element.66), channel_id=1, source_target_pairs={{0,254},{2,4},{4,2},{6,8},{8,6},{10,12},{12,10},{14,16},{16,14},{1... | collective-permute-start | bytes 638984 | tf_op jit(solution)/shard_map/ppermute | solution.py:643
  51.1 4.4 %collective-permute-start.12 = (f32[8,1536]{1,0:T(8,128)S(1)}, f32[8,1536]{1,0:T(8,128)S(1)}, u32[]{:S(2)}, u32[]{:S(2)}) collective-permute-start(f32[8,1536]{1,0:T(8,128)S(1)} %shard_map.254.refs_13_.refs_0_), channel_id=1, source_target_pairs={{0,64},{2,66},{4,68},{6,70},{8,72},{10,74},{12,76},{14,78},{16,80}... | collective-permute-start | bytes 147464 | tf_op jit(solution)/shard_map/ppermute | solution.py:739
  55.4 4.2 %collective-permute-start.13 = (f32[8,1536]{1,0:T(8,128)S(1)}, f32[8,1536]{1,0:T(8,128)S(1)}, u32[]{:S(2)}, u32[]{:S(2)}) collective-permute-start(f32[8,1536]{1,0:T(8,128)S(1)} %shard_map.256.refs_0_), channel_id=1, source_target_pairs={{0,4},{2,6},{4,0},{6,2},{8,12},{10,14},{12,8},{14,10},{16,20},{18,... | collective-permute-start | bytes 147464 | tf_op jit(solution)/shard_map/ppermute | solution.py:739
  59.6 6.2 %collective-permute-start.14 = (f32[8,1536]{1,0:T(8,128)S(1)}, f32[8,1536]{1,0:T(8,128)S(1)}, u32[]{:S(2)}, u32[]{:S(2)}) collective-permute-start(f32[8,1536]{1,0:T(8,128)S(1)} %shard_map.257.refs_11_.refs_0_), channel_id=1, source_target_pairs={{0,2},{2,0},{4,6},{6,4},{8,10},{10,8},{12,14},{14,12},{16,18},{18,... | collective-permute-start | bytes 147464 | tf_op jit(solution)/shard_map/ppermute | solution.py:739
  65.8 5.4 %collective-permute-start.17 = (f32[8,1536]{1,0:T(8,128)S(1)}, f32[8,1536]{1,0:T(8,128)S(1)}, u32[]{:S(2)}, u32[]{:S(2)}) collective-permute-start(f32[8,1536]{1,0:T(8,128)S(1)} %shard_map.260._.refs_0_), channel_id=1, source_target_pairs={{0,192},{2,194},{4,196},{6,198},{8,200},{10,202},{12,204},{14,206}... | collective-permute-start | bytes 147464 | tf_op jit(solution)/shard_map/ppermute | solution.py:739
  66.7 16.2 %collective-permute-start.15 = (bf16[96,1536]{1,0:T(8,128)(2,1)S(1)}, bf16[96,1536]{1,0:T(8,128)(2,1)S(1)}, u32[]{:S(2)}, u32[]{:S(2)}) collective-permute-start(bf16[96,1536]{1,0:T(8,128)(2,1)S(1)} %get-tuple-element.82), channel_id=1, source_target_pairs={{0,2},{2,0},{4,6},{6,4},{8,10},{10,8},{12,14},{14,12},{16,18},{18,... | collective-permute-start | bytes 884744 | tf_op jit(solution)/shard_map/ppermute | solution.py:640
  68.5 14.8 %collective-permute-start.16 = (bf16[96,1536]{1,0:T(8,128)(2,1)S(1)}, bf16[96,1536]{1,0:T(8,128)(2,1)S(1)}, u32[]{:S(2)}, u32[]{:S(2)}) collective-permute-start(bf16[96,1536]{1,0:T(8,128)(2,1)S(1)} %get-tuple-element.83), channel_id=1, source_target_pairs={{0,254},{2,4},{4,2},{6,8},{8,6},{10,12},{12,10},{14,16},{16,14},{1... | collective-permute-start | bytes 884744 | tf_op jit(solution)/shard_map/ppermute | solution.py:643
  71.2 7.8 %collective-permute-start.18 = (f32[8,1536]{1,0:T(8,128)S(1)}, f32[8,1536]{1,0:T(8,128)S(1)}, u32[]{:S(2)}, u32[]{:S(2)}) collective-permute-start(f32[8,1536]{1,0:T(8,128)S(1)} %shard_map.263.refs_0_), channel_id=1, source_target_pairs={{0,28},{2,30},{4,24},{6,26},{8,20},{10,22},{12,16},{14,18},{16,12}... | collective-permute-start | bytes 147464 | tf_op jit(solution)/shard_map/ppermute | solution.py:739
  79.0 6.0 %collective-permute-start.19 = (f32[8,1536]{1,0:T(8,128)S(1)}, f32[8,1536]{1,0:T(8,128)S(1)}, u32[]{:S(2)}, u32[]{:S(2)}) collective-permute-start(f32[8,1536]{1,0:T(8,128)S(1)} %shard_map.264.mine), channel_id=1, source_target_pairs={{0,8},{2,10},{4,12},{6,14},{8,0},{10,2},{12,4},{14,6},{16,24},{18,... | collective-permute-start | bytes 147464 | tf_op jit(solution)/shard_map/ppermute | solution.py:739
  (14 other events, 75.1 us)

commit v7 on v6

--- a/solution.py
+++ b/solution.py
@@ -791,8 +791,8 @@
         (), (), (), (4,),
     )
     got_e, got_o = swap_e(give_e), swap_o(give_o)
+    total = summed(total, 14, micros=1.0)
     total = summed(total, 96, micros=1.0)
-    total = summed(total, 14, micros=1.0)
     one = ((rows_a, wide), BF)
     dk_a, dv_a, dq_a, token = call(
         settle,

time: 86.8 us -> 84.1 us (0.969); the launches traced: 85.6 us -> 84 us
  starting transfers between devices: 38.6 us -> 36.5 us
    ppermute x6, waiting for transfers between devices: 11.8 us -> 14.7 us  [swap_e(): return lax.ppermute(x, BLOCKS, even_route)]
    ppermute x7, waiting for transfers between devices: 11.9 us -> 9.86 us  [moved(): return lax.ppermute(x, BLOCKS, [(i, i ^ bits) for i in range(count)])]
    ppermute x7, starting transfers between devices: 8.63 us -> 7.51 us  [moved(): return lax.ppermute(x, BLOCKS, [(i, i ^ bits) for i in range(count)])]
  transfers between devices with their start and end apart: 20 -> 20, of which waited for: 12 -> 10; matrix products, arithmetic and copies ran while one was open for 0% -> 0% of each run, Pallas kernels for 12% -> 12%
where the time goes in v7:
time: 84.1 us; the launch traced here: 84 us
  starting transfers between devices  36.5 us (43%)
  waiting for transfers between devices  30.6 us (36%)
  Pallas kernels  14 us (17%)
  local copies, waits for them, and re-layouts  1.88 us (2%)
  between operations  1.01 us (1%)
    ppermute x6, starting transfers between devices, swap_o(): return lax.ppermute(x, BLOCKS, odd_route)  24.4 us
    ppermute x6, waiting for transfers between devices, swap_e(): return lax.ppermute(x, BLOCKS, even_route)  14.7 us
    pallas_call x19, Pallas kernels, call(): pl.pallas_call(kernel, out_shape=[jax.ShapeDtypeStruct(s, d) for s, d in...  14 us
    ppermute x7, waiting for transfers between devices, moved(): return lax.ppermute(x, BLOCKS, [(i, i ^ bits) for i in range(count)])  9.86 us
    ppermute x7, starting transfers between devices, moved(): return lax.ppermute(x, BLOCKS, [(i, i ^ bits) for i in range(count)])  7.51 us
    ppermute x6, starting transfers between devices, swap_e(): return lax.ppermute(x, BLOCKS, even_route)  4.08 us
    ppermute x1, waiting for transfers between devices, per_device(): lax.ppermute(stats, 'tp', [(i, i ^ 1) for i in range(tp_size)])  3.47 us
    ppermute x6, waiting for transfers between devices, swap_o(): return lax.ppermute(x, BLOCKS, odd_route)  2.51 us
  transfers between devices with their start and end apart: 20, of which 10 were waited for; matrix products, arithmetic and copies ran while one was open for 0% of the time, Pallas kernels for 12%

profile of v7, /device:TPU:2, one launch (start us, length us, event | category | flops | bytes accessed | tf_op | source)
XLA Modules:
  0.0 84.0 jit_solution(9392162850990584303)
XLA Ops:
  0.7 2.2 %collective-permute-start.2 = (bf16[32,1536]{1,0:T(8,128)(2,1)}, bf16[32,1536]{1,0:T(8,128)(2,1)S(1)}, u32[]{:S(2)}, u32[]{:S(2)}) collective-permute-start(bf16[32,1536]{1,0:T(8,128)(2,1)} %q.1), channel_id=1, source_target_pairs={{0,2},{2,0},{4,6},{6,4},{8,10},{10,8},{12,14},{14,12},{16,18},{18,... | collective-permute-start | bytes 294920 | tf_op jit(solution)/shard_map/ppermute | solution.py:640
  2.9 8.3 %collective-permute-start.3 = (bf16[32,1536]{1,0:T(8,128)(2,1)}, bf16[32,1536]{1,0:T(8,128)(2,1)S(1)}, u32[]{:S(2)}, u32[]{:S(2)}) collective-permute-start(bf16[32,1536]{1,0:T(8,128)(2,1)} %q.1), channel_id=1, source_target_pairs={{0,254},{2,4},{4,2},{6,8},{8,6},{10,12},{12,10},{14,16},{16,14},{1... | collective-permute-start | bytes 294920 | tf_op jit(solution)/shard_map/ppermute | solution.py:643
  13.4 3.4 %collective-permute-start.1 = (bf16[64,1536]{1,0:T(8,128)(2,1)S(1)}, bf16[64,1536]{1,0:T(8,128)(2,1)S(1)}, u32[]{:S(2)}, u32[]{:S(2)}) collective-permute-start(bf16[64,1536]{1,0:T(8,128)(2,1)S(1)} %shard_map.247), channel_id=1, source_target_pairs={{0,254},{2,4},{4,2},{6,8},{8,6},{10,12},{12,10},{14,16},{16,14},{1... | collective-permute-start | bytes 589832 | tf_op jit(solution)/shard_map/ppermute | solution.py:643
  16.9 1.5 %shard_map.248 = (bf16[32,1664]{1,0:T(8,128)(2,1)S(1)}, bf16[32,1664]{1,0:T(8,128)(2,1)S(1)}, f32[32,1536]{1,0:T(8,128)S(1)}, f32[32,128]{1,0:T(8,128)S(1)}, f32...) custom-call(s32[1]{0:T(128)} %bitcast.refs_0_.idx, s32[2,128]{1,0:T(2,128)S(1)} %bitcast.3, s32[128]{0:T(128)S(1)} %copy-done.14, ...), custom_call_target="tpu_custom_call" | custom-call | flops 1760000000 | bytes 1867776 | tf_op jit(solution)/shard_map/pallas_call | solution.py:31
  18.6 4.5 %collective-permute-start.5 = (bf16[32,1664]{1,0:T(8,128)(2,1)S(1)}, bf16[32,1664]{1,0:T(8,128)(2,1)S(1)}, u32[]{:S(2)}, u32[]{:S(2)}) collective-permute-start(bf16[32,1664]{1,0:T(8,128)(2,1)S(1)} %get-tuple-element.56), channel_id=1, source_target_pairs={{0,254},{2,4},{4,2},{6,8},{8,6},{10,12},{12,10},{14,16},{16,14},{1... | collective-permute-start | bytes 319496 | tf_op jit(solution)/shard_map/ppermute | solution.py:643
  23.1 5.1 %collective-permute-done.refs_6_.refs_9_ = bf16[64,1536]{1,0:T(8,128)(2,1)S(1)} collective-permute-done((bf16[64,1536]{1,0:T(8,128)(2,1)S(1)}, bf16[64,1536]{1,0:T(8,128)(2,1)S(1)}, u32[]{:S(2)}, u32[]{:S(2)}) %collective-permute-start) | collective-permute-done | bytes 196640 | tf_op jit(solution)/shard_map/ppermute | solution.py:640
  30.2 3.3 %collective-permute-start.7 = (bf16[32,1792]{1,0:T(8,128)(2,1)S(1)}, bf16[32,1792]{1,0:T(8,128)(2,1)S(1)}, u32[]{:S(2)}, u32[]{:S(2)}) collective-permute-start(bf16[32,1792]{1,0:T(8,128)(2,1)S(1)} %get-tuple-element.58), channel_id=1, source_target_pairs={{0,254},{2,4},{4,2},{6,8},{8,6},{10,12},{12,10},{14,16},{16,14},{1... | collective-permute-start | bytes 344072 | tf_op jit(solution)/shard_map/ppermute | solution.py:643
  34.2 4.5 %collective-permute-done.6.refs_3_.refs_4_ = bf16[32,1792]{1,0:T(8,128)(2,1)S(1)} collective-permute-done((bf16[32,1792]{1,0:T(8,128)(2,1)S(1)}, bf16[32,1792]{1,0:T(8,128)(2,1)S(1)}, u32[]{:S(2)}, u32[]{:S(2)}) %collective-permute-start.6) | collective-permute-done | bytes 114720 | tf_op jit(solution)/shard_map/ppermute | solution.py:640
  38.6 2.5 %collective-permute-done.7.refs_4_.refs_5_ = bf16[32,1792]{1,0:T(8,128)(2,1)S(1)} collective-permute-done((bf16[32,1792]{1,0:T(8,128)(2,1)S(1)}, bf16[32,1792]{1,0:T(8,128)(2,1)S(1)}, u32[]{:S(2)}, u32[]{:S(2)}) %collective-permute-start.7) | collective-permute-done | bytes 114720 | tf_op jit(solution)/shard_map/ppermute | solution.py:643
  42.2 3.5 %collective-permute-done.8.refs_2_ = f32[80,128]{1,0:T(8,128)S(1)} collective-permute-done((f32[80,128]{1,0:T(8,128)S(1)}, f32[80,128]{1,0:T(8,128)S(1)}, u32[]{:S(2)}, u32[]{:S(2)}) %collective-permute-start.8) | collective-permute-done | bytes 40992 | tf_op jit(solution)/shard_map/ppermute | solution.py:718
  45.7 2.0 %shard_map.253 = (f32[256,1536]{1,0:T(8,128)S(1)}, bf16[32,1536]{1,0:T(8,128)(2,1)S(1)}, bf16[64,1664]{1,0:T(8,128)(2,1)S(1)}, bf16[64,1664]{1,0:T(8,128)(2,1)S(...) custom-call(s32[1]{0:T(128)} %bitcast.refs_0_.idx, f32[80,128]{1,0:T(8,128)S(1)} %shard_map.252.refs_1_, ...), custom_call_target="tpu_custom_call" | custom-call | flops 2750000128 | bytes 2146304 | tf_op jit(solution)/shard_map/pallas_call | solution.py:31
  47.9 3.2 %collective-permute-start.11 = (bf16[64,1664]{1,0:T(8,128)(2,1)S(1)}, bf16[64,1664]{1,0:T(8,128)(2,1)S(1)}, u32[]{:S(2)}, u32[]{:S(2)}) collective-permute-start(bf16[64,1664]{1,0:T(8,128)(2,1)S(1)} %get-tuple-element.66), channel_id=1, source_target_pairs={{0,254},{2,4},{4,2},{6,8},{8,6},{10,12},{12,10},{14,16},{16,14},{1... | collective-permute-start | bytes 638984 | tf_op jit(solution)/shard_map/ppermute | solution.py:643
  51.4 1.5 %shard_map.255 = (bf16[256,1536]{1,0:T(8,128)(2,1)}, bf16[32,1536]{1,0:T(8,128)(2,1)}, f32[8,128]{1,0:T(8,128)S(1)}) custom-call(s32[1]{0:T(128)} %bitcast.refs_0_.idx, f32[80,128]{1,0:T(8,128)S(1)} %shard_map.252.refs_1_, f32[80,128]{1,0:T(8,128)S(1)} %collective-permute-done.8.refs_2_, bf16[256,1536]{1,0:T(8,128)(2,1)S(1)} %get-tuple-element.53.att_v.refs_2_.refs_3_, ...), custom_call_target="tpu_custom_call" | custom-call | flops 1650000000 | bytes 2179072 | tf_op jit(solution)/shard_map/pallas_call | solution.py:31
  52.9 2.5 %collective-permute-done.12.refs_1_ = f32[8,1536]{1,0:T(8,128)S(1)} collective-permute-done((f32[8,1536]{1,0:T(8,128)S(1)}, f32[8,1536]{1,0:T(8,128)S(1)}, u32[]{:S(2)}, u32[]{:S(2)}) %collective-permute-start.12) | collective-permute-done | bytes 49184 | tf_op jit(solution)/shard_map/ppermute | solution.py:739
  55.4 1.9 %collective-permute-start.13 = (f32[8,1536]{1,0:T(8,128)S(1)}, f32[8,1536]{1,0:T(8,128)S(1)}, u32[]{:S(2)}, u32[]{:S(2)}) collective-permute-start(f32[8,1536]{1,0:T(8,128)S(1)} %shard_map.256.refs_0_), channel_id=1, source_target_pairs={{0,4},{2,6},{4,0},{6,2},{8,12},{10,14},{12,8},{14,10},{16,20},{18,... | collective-permute-start | bytes 147464 | tf_op jit(solution)/shard_map/ppermute | solution.py:739
  57.3 2.3 %collective-permute-done.13.refs_1_ = f32[8,1536]{1,0:T(8,128)S(1)} collective-permute-done((f32[8,1536]{1,0:T(8,128)S(1)}, f32[8,1536]{1,0:T(8,128)S(1)}, u32[]{:S(2)}, u32[]{:S(2)}) %collective-permute-start.13) | collective-permute-done | bytes 49184 | tf_op jit(solution)/shard_map/ppermute | solution.py:739
  60.0 1.5 %collective-permute-done.10.refs_3_.re = bf16[64,1664]{1,0:T(8,128)(2,1)S(1)} collective-permute-done((bf16[64,1664]{1,0:T(8,128)(2,1)S(1)}, bf16[64,1664]{1,0:T(8,128)(2,1)S(1)}, u32[]{:S(2)}, u32[]{:S(2)}) %collective-permute-start.10) | collective-permute-done | bytes 213024 | tf_op jit(solution)/shard_map/ppermute | solution.py:640
  61.5 2.0 %shard_map.258 = (bf16[256,1536]{1,0:T(8,128)(2,1)}, f32[64,1536]{1,0:T(8,128)S(1)}, bf16[64,1536]{1,0:T(8,128)(2,1)S(1)}, bf16[64,1536]{1,0:T(8,128)(2,1)S(1)}) custom-call(s32[1]{0:T(128)} %bitcast.refs_0_.idx, bf16[256,1536]{1,0:T(8,128)(2,1)S(1)} %copy-done.4, f32[256,1536]{1,0:T(8,128)S(1)} %get-tuple-element.64.refs_2_, ...), custom_call_target="tpu_custom_call" | custom-call | flops 3300000000 | bytes 4032512 | tf_op jit(solution)/shard_map/pallas_call | solution.py:31
  63.5 2.3 %shard_map.259 = (bf16[256,1536]{1,0:T(8,128)(2,1)}, bf16[256,1536]{1,0:T(8,128)(2,1)}, f32[32,1536]{1,0:T(8,128)S(1)}, bf16[32,1536]{1,0:T(8,128)(2,1)S(1)}, bf16[32,1536]{1,0:T(8,128)(2,1)S(1)}) custom-call(bf16[32,1536]{1,0:T(8,128)(2,1)S(1)} %copy-done.11, bf16[32,1536]{1,0:T(8,128)(2,1)S(1)} %collective-permute-done.2.refs_4_.qe, ...), custom_call_target="tpu_custom_call" | custom-call | flops 3300000000 | bytes 3276800 | tf_op jit(solution)/shard_map/pallas_call | solution.py:31
  65.8 2.1 %collective-permute-start.17 = (f32[8,1536]{1,0:T(8,128)S(1)}, f32[8,1536]{1,0:T(8,128)S(1)}, u32[]{:S(2)}, u32[]{:S(2)}) collective-permute-start(f32[8,1536]{1,0:T(8,128)S(1)} %shard_map.260._.refs_0_), channel_id=1, source_target_pairs={{0,28},{2,30},{4,24},{6,26},{8,20},{10,22},{12,16},{14,18},{16,12}... | collective-permute-start | bytes 147464 | tf_op jit(solution)/shard_map/ppermute | solution.py:739
  69.3 1.7 %collective-permute-start.16 = (bf16[96,1536]{1,0:T(8,128)(2,1)S(1)}, bf16[96,1536]{1,0:T(8,128)(2,1)S(1)}, u32[]{:S(2)}, u32[]{:S(2)}) collective-permute-start(bf16[96,1536]{1,0:T(8,128)(2,1)S(1)} %get-tuple-element.83), channel_id=1, source_target_pairs={{0,254},{2,4},{4,2},{6,8},{8,6},{10,12},{12,10},{14,16},{16,14},{1... | collective-permute-start | bytes 884744 | tf_op jit(solution)/shard_map/ppermute | solution.py:643
  72.0 4.9 %collective-permute-done.18.refs_1_ = f32[8,1536]{1,0:T(8,128)S(1)} collective-permute-done((f32[8,1536]{1,0:T(8,128)S(1)}, f32[8,1536]{1,0:T(8,128)S(1)}, u32[]{:S(2)}, u32[]{:S(2)}) %collective-permute-start.18) | collective-permute-done | bytes 49184 | tf_op jit(solution)/shard_map/ppermute | solution.py:739
  76.9 1.9 %collective-permute-start.19 = (f32[8,1536]{1,0:T(8,128)S(1)}, f32[8,1536]{1,0:T(8,128)S(1)}, u32[]{:S(2)}, u32[]{:S(2)}) collective-permute-start(f32[8,1536]{1,0:T(8,128)S(1)} %shard_map.264.mine), channel_id=1, source_target_pairs={{0,8},{2,10},{4,12},{6,14},{8,0},{10,2},{12,4},{14,6},{16,24},{18,... | collective-permute-start | bytes 147464 | tf_op jit(solution)/shard_map/ppermute | solution.py:739
  78.9 3.7 %collective-permute-done.15.e = bf16[96,1536]{1,0:T(8,128)(2,1)S(1)} collective-permute-done((bf16[96,1536]{1,0:T(8,128)(2,1)S(1)}, bf16[96,1536]{1,0:T(8,128)(2,1)S(1)}, u32[]{:S(2)}, u32[]{:S(2)}) %collective-permute-start.15) | collective-permute-done | bytes 294944 | tf_op jit(solution)/shard_map/ppermute | solution.py:640
  (73 shorter events, 10.7 us)
Async XLA Ops:
  0.6 16.1 %copy-start.5 = (bf16[256,1536]{1,0:T(8,128)(2,1)S(1)}, bf16[256,1536]{1,0:T(8,128)(2,1)}, u32[]{:S(2)}) copy-start(bf16[256,1536]{1,0:T(8,128)(2,1)} %k.3) | copy-start | bytes 2359300
  0.7 16.1 %copy-start.6 = (bf16[256,1536]{1,0:T(8,128)(2,1)S(1)}, bf16[256,1536]{1,0:T(8,128)(2,1)}, u32[]{:S(2)}) copy-start(bf16[256,1536]{1,0:T(8,128)(2,1)} %v.3) | copy-start | bytes 2359300
  0.7 16.1 %collective-permute-start.2 = (bf16[32,1536]{1,0:T(8,128)(2,1)}, bf16[32,1536]{1,0:T(8,128)(2,1)S(1)}, u32[]{:S(2)}, u32[]{:S(2)}) collective-permute-start(bf16[32,1536]{1,0:T(8,128)(2,1)} %q.1), channel_id=1, source_target_pairs={{0,2},{2,0},{4,6},{6,4},{8,10},{10,8},{12,14},{14,12},{16,18},{18,... | collective-permute-start | bytes 294920 | tf_op jit(solution)/shard_map/ppermute | solution.py:640
  2.9 13.9 %collective-permute-start.3 = (bf16[32,1536]{1,0:T(8,128)(2,1)}, bf16[32,1536]{1,0:T(8,128)(2,1)S(1)}, u32[]{:S(2)}, u32[]{:S(2)}) collective-permute-start(bf16[32,1536]{1,0:T(8,128)(2,1)} %q.1), channel_id=1, source_target_pairs={{0,254},{2,4},{4,2},{6,8},{8,6},{10,12},{12,10},{14,16},{16,14},{1... | collective-permute-start | bytes 294920 | tf_op jit(solution)/shard_map/ppermute | solution.py:643
  13.2 14.9 %collective-permute-start = (bf16[64,1536]{1,0:T(8,128)(2,1)S(1)}, bf16[64,1536]{1,0:T(8,128)(2,1)S(1)}, u32[]{:S(2)}, u32[]{:S(2)}) collective-permute-start(bf16[64,1536]{1,0:T(8,128)(2,1)S(1)} %shard_map.247), channel_id=1, source_target_pairs={{0,2},{2,0},{4,6},{6,4},{8,10},{10,8},{12,14},{14,12},{16,18},{18,... | collective-permute-start | bytes 589832 | tf_op jit(solution)/shard_map/ppermute | solution.py:640
  13.4 14.8 %collective-permute-start.1 = (bf16[64,1536]{1,0:T(8,128)(2,1)S(1)}, bf16[64,1536]{1,0:T(8,128)(2,1)S(1)}, u32[]{:S(2)}, u32[]{:S(2)}) collective-permute-start(bf16[64,1536]{1,0:T(8,128)(2,1)S(1)} %shard_map.247), channel_id=1, source_target_pairs={{0,254},{2,4},{4,2},{6,8},{8,6},{10,12},{12,10},{14,16},{16,14},{1... | collective-permute-start | bytes 589832 | tf_op jit(solution)/shard_map/ppermute | solution.py:643
  16.8 11.4 %copy-start.4 = (bf16[256,1536]{1,0:T(8,128)(2,1)S(1)}, bf16[256,1536]{1,0:T(8,128)(2,1)}, u32[]{:S(2)}) copy-start(bf16[256,1536]{1,0:T(8,128)(2,1)} %refs_1_.1) | copy-start | bytes 2359300
  16.8 11.3 %copy-start.8 = (bf16[32,1536]{1,0:T(8,128)(2,1)S(1)}, bf16[32,1536]{1,0:T(8,128)(2,1)}, u32[]{:S(2)}) copy-start(bf16[32,1536]{1,0:T(8,128)(2,1)} %refs_7_.5) | copy-start | bytes 294916
  18.4 11.3 %collective-permute-start.4 = (bf16[32,1664]{1,0:T(8,128)(2,1)S(1)}, bf16[32,1664]{1,0:T(8,128)(2,1)S(1)}, u32[]{:S(2)}, u32[]{:S(2)}) collective-permute-start(bf16[32,1664]{1,0:T(8,128)(2,1)S(1)} %get-tuple-element.55), channel_id=1, source_target_pairs={{0,2},{2,0},{4,6},{6,4},{8,10},{10,8},{12,14},{14,12},{16,18},{18,... | collective-permute-start | bytes 319496 | tf_op jit(solution)/shard_map/ppermute | solution.py:640
  18.6 11.1 %collective-permute-start.5 = (bf16[32,1664]{1,0:T(8,128)(2,1)S(1)}, bf16[32,1664]{1,0:T(8,128)(2,1)S(1)}, u32[]{:S(2)}, u32[]{:S(2)}) collective-permute-start(bf16[32,1664]{1,0:T(8,128)(2,1)S(1)} %get-tuple-element.56), channel_id=1, source_target_pairs={{0,254},{2,4},{4,2},{6,8},{8,6},{10,12},{12,10},{14,16},{16,14},{1... | collective-permute-start | bytes 319496 | tf_op jit(solution)/shard_map/ppermute | solution.py:643
  30.1 8.5 %collective-permute-start.6 = (bf16[32,1792]{1,0:T(8,128)(2,1)S(1)}, bf16[32,1792]{1,0:T(8,128)(2,1)S(1)}, u32[]{:S(2)}, u32[]{:S(2)}) collective-permute-start(bf16[32,1792]{1,0:T(8,128)(2,1)S(1)} %get-tuple-element.57), channel_id=1, source_target_pairs={{0,2},{2,0},{4,6},{6,4},{8,10},{10,8},{12,14},{14,12},{16,18},{18,... | collective-permute-start | bytes 344072 | tf_op jit(solution)/shard_map/ppermute | solution.py:640
  30.2 10.9 %collective-permute-start.7 = (bf16[32,1792]{1,0:T(8,128)(2,1)S(1)}, bf16[32,1792]{1,0:T(8,128)(2,1)S(1)}, u32[]{:S(2)}, u32[]{:S(2)}) collective-permute-start(bf16[32,1792]{1,0:T(8,128)(2,1)S(1)} %get-tuple-element.58), channel_id=1, source_target_pairs={{0,254},{2,4},{4,2},{6,8},{8,6},{10,12},{12,10},{14,16},{16,14},{1... | collective-permute-start | bytes 344072 | tf_op jit(solution)/shard_map/ppermute | solution.py:643
  41.6 4.0 %collective-permute-start.8 = (f32[80,128]{1,0:T(8,128)S(1)}, f32[80,128]{1,0:T(8,128)S(1)}, u32[]{:S(2)}, u32[]{:S(2)}) collective-permute-start(f32[80,128]{1,0:T(8,128)S(1)} %shard_map.252.refs_1_), channel_id=1, source_target_pairs={{0,1},{1,0},{2,3},{3,2},{4,5},{5,4},{6,7},{7,6},{8,9},{9,8},{10,11... | collective-permute-start | bytes 122888 | tf_op jit(solution)/shard_map/ppermute | solution.py:718
  47.7 3.4 %collective-permute-start.9 = (f32[8,1536]{1,0:T(8,128)S(1)}, f32[8,1536]{1,0:T(8,128)S(1)}, u32[]{:S(2)}, u32[]{:S(2)}) collective-permute-start(f32[8,1536]{1,0:T(8,128)S(1)} %get-tuple-element.61.refs_0_), channel_id=1, source_target_pairs={{0,32},{2,34},{4,36},{6,38},{8,40},{10,42},{12,44},{14,46},{16,48}... | collective-permute-start | bytes 147464 | tf_op jit(solution)/shard_map/ppermute | solution.py:739
  47.8 13.7 %collective-permute-start.10 = (bf16[64,1664]{1,0:T(8,128)(2,1)S(1)}, bf16[64,1664]{1,0:T(8,128)(2,1)S(1)}, u32[]{:S(2)}, u32[]{:S(2)}) collective-permute-start(bf16[64,1664]{1,0:T(8,128)(2,1)S(1)} %get-tuple-element.65), channel_id=1, source_target_pairs={{0,2},{2,0},{4,6},{6,4},{8,10},{10,8},{12,14},{14,12},{16,18},{18,... | collective-permute-start | bytes 638984 | tf_op jit(solution)/shard_map/ppermute | solution.py:640
  47.9 13.6 %collective-permute-start.11 = (bf16[64,1664]{1,0:T(8,128)(2,1)S(1)}, bf16[64,1664]{1,0:T(8,128)(2,1)S(1)}, u32[]{:S(2)}, u32[]{:S(2)}) collective-permute-start(bf16[64,1664]{1,0:T(8,128)(2,1)S(1)} %get-tuple-element.66), channel_id=1, source_target_pairs={{0,254},{2,4},{4,2},{6,8},{8,6},{10,12},{12,10},{14,16},{16,14},{1... | collective-permute-start | bytes 638984 | tf_op jit(solution)/shard_map/ppermute | solution.py:643
  51.1 4.4 %collective-permute-start.12 = (f32[8,1536]{1,0:T(8,128)S(1)}, f32[8,1536]{1,0:T(8,128)S(1)}, u32[]{:S(2)}, u32[]{:S(2)}) collective-permute-start(f32[8,1536]{1,0:T(8,128)S(1)} %shard_map.254.refs_13_.refs_0_), channel_id=1, source_target_pairs={{0,64},{2,66},{4,68},{6,70},{8,72},{10,74},{12,76},{14,78},{16,80}... | collective-permute-start | bytes 147464 | tf_op jit(solution)/shard_map/ppermute | solution.py:739
  55.4 4.2 %collective-permute-start.13 = (f32[8,1536]{1,0:T(8,128)S(1)}, f32[8,1536]{1,0:T(8,128)S(1)}, u32[]{:S(2)}, u32[]{:S(2)}) collective-permute-start(f32[8,1536]{1,0:T(8,128)S(1)} %shard_map.256.refs_0_), channel_id=1, source_target_pairs={{0,4},{2,6},{4,0},{6,2},{8,12},{10,14},{12,8},{14,10},{16,20},{18,... | collective-permute-start | bytes 147464 | tf_op jit(solution)/shard_map/ppermute | solution.py:739
  59.6 6.2 %collective-permute-start.14 = (f32[8,1536]{1,0:T(8,128)S(1)}, f32[8,1536]{1,0:T(8,128)S(1)}, u32[]{:S(2)}, u32[]{:S(2)}) collective-permute-start(f32[8,1536]{1,0:T(8,128)S(1)} %shard_map.257.refs_11_.refs_0_), channel_id=1, source_target_pairs={{0,2},{2,0},{4,6},{6,4},{8,10},{10,8},{12,14},{14,12},{16,18},{18,... | collective-permute-start | bytes 147464 | tf_op jit(solution)/shard_map/ppermute | solution.py:739
  65.8 5.4 %collective-permute-start.17 = (f32[8,1536]{1,0:T(8,128)S(1)}, f32[8,1536]{1,0:T(8,128)S(1)}, u32[]{:S(2)}, u32[]{:S(2)}) collective-permute-start(f32[8,1536]{1,0:T(8,128)S(1)} %shard_map.260._.refs_0_), channel_id=1, source_target_pairs={{0,28},{2,30},{4,24},{6,26},{8,20},{10,22},{12,16},{14,18},{16,12}... | collective-permute-start | bytes 147464 | tf_op jit(solution)/shard_map/ppermute | solution.py:739
  68.0 14.6 %collective-permute-start.15 = (bf16[96,1536]{1,0:T(8,128)(2,1)S(1)}, bf16[96,1536]{1,0:T(8,128)(2,1)S(1)}, u32[]{:S(2)}, u32[]{:S(2)}) collective-permute-start(bf16[96,1536]{1,0:T(8,128)(2,1)S(1)} %get-tuple-element.82), channel_id=1, source_target_pairs={{0,2},{2,0},{4,6},{6,4},{8,10},{10,8},{12,14},{14,12},{16,18},{18,... | collective-permute-start | bytes 884744 | tf_op jit(solution)/shard_map/ppermute | solution.py:640
  69.3 13.3 %collective-permute-start.16 = (bf16[96,1536]{1,0:T(8,128)(2,1)S(1)}, bf16[96,1536]{1,0:T(8,128)(2,1)S(1)}, u32[]{:S(2)}, u32[]{:S(2)}) collective-permute-start(bf16[96,1536]{1,0:T(8,128)(2,1)S(1)} %get-tuple-element.83), channel_id=1, source_target_pairs={{0,254},{2,4},{4,2},{6,8},{8,6},{10,12},{12,10},{14,16},{16,14},{1... | collective-permute-start | bytes 884744 | tf_op jit(solution)/shard_map/ppermute | solution.py:643
  71.2 5.7 %collective-permute-start.18 = (f32[8,1536]{1,0:T(8,128)S(1)}, f32[8,1536]{1,0:T(8,128)S(1)}, u32[]{:S(2)}, u32[]{:S(2)}) collective-permute-start(f32[8,1536]{1,0:T(8,128)S(1)} %shard_map.263.refs_0_), channel_id=1, source_target_pairs={{0,192},{2,194},{4,196},{6,198},{8,200},{10,202},{12,204},{14,206}... | collective-permute-start | bytes 147464 | tf_op jit(solution)/shard_map/ppermute | solution.py:739
  76.9 6.4 %collective-permute-start.19 = (f32[8,1536]{1,0:T(8,128)S(1)}, f32[8,1536]{1,0:T(8,128)S(1)}, u32[]{:S(2)}, u32[]{:S(2)}) collective-permute-start(f32[8,1536]{1,0:T(8,128)S(1)} %shard_map.264.mine), channel_id=1, source_target_pairs={{0,8},{2,10},{4,12},{6,14},{8,0},{10,2},{12,4},{14,6},{16,24},{18,... | collective-permute-start | bytes 147464 | tf_op jit(solution)/shard_map/ppermute | solution.py:739
  (14 other events, 75.1 us)
